TPU v7x, 32 devices: a whole 2x2x4 slice. The times are simulated.
32 devices in a mesh: seq: 32 (over z, y, x, core).
Axes of the slice: x: 2, y: 2, z: 4, core: 2. Of those that a mesh axis runs over, the one named last changes fastest.
Arguments:
- inputs: bfloat16 [131072, 128], P('seq'), may hold values from -6 to 6
- segment_ids: int32 [512, 256], P('seq'), may hold values from 0 to 7, never falling along the last dimension, each value on 1 to 64 neighbouring positions
- cotangent: bfloat16 [131072, 128], P('seq'), may hold values from -6 to 6
- norm_gains: float32 [2, 2, 128], replicated, may hold values from 0.5 to 1.5
- norm_shifts: float32 [2, 2, 128], replicated, may hold values from -3 to 3
- w_qkv: bfloat16 [2, 128, 384], replicated, may hold values from -0.5 to 0.5
- qv_bias: float32 [2, 256], replicated, may hold values from -3 to 3
- w_out: bfloat16 [2, 128, 128], replicated, may hold values from -3 to 3
- out_bias: float32 [2, 128], replicated, may hold values from -3 to 3
- w_gate: bfloat16 [2, 128], replicated, may hold values from -0.5 to 0.5
- w_up: bfloat16 [2, 128, 256], replicated, may hold values from -0.5 to 0.5
- up_bias: float32 [2, 256], replicated, may hold values from -3 to 3
- w_down: bfloat16 [2, 256, 128], replicated, may hold values from -0.75 to 0.75
- down_bias: float32 [2, 128], replicated, may hold values from -3 to 3
Outputs:
- result: bfloat16 [131072, 128], P('seq')
- grad_inputs: float32 [131072, 128], P('seq')
- grad_gains: float32 [2, 2, 128], replicated
- grad_shifts: float32 [2, 2, 128], replicated
- grad_qkv: float32 [2, 128, 384], replicated
- grad_qv_bias: float32 [2, 256], replicated
- grad_out: float32 [2, 128, 128], replicated
- grad_out_bias: float32 [2, 128], replicated
- grad_gate: float32 [2, 128], replicated
- grad_up: float32 [2, 128, 256], replicated
- grad_up_bias: float32 [2, 256], replicated
- grad_down: float32 [2, 256, 128], replicated
- grad_down_bias: float32 [2, 128], replicated
Inputs may be any that keep to these rules, and one draw needn't show every extreme that they name: `segment_ids`: in each sequence the ids never fall; each of the 8 ids covers 1 to 64 tokens.
All inputs are finite; a program needn't handle non-finite values.
Results may differ from a plain program's by a relative error of at most 0.02.
Values sent between devices are 32-bit elements; how exact they have to be, the bound alone decides.
No kernel may reach another device: no remote copies, remote signals or barrier semaphores. Data moves between devices by JAX's collectives and lax.ppermute only.
A program may use at most 128 MiB of HBM per device.

v0:
```python
import jax
import jax.numpy as jnp
from jax import lax
from jax.experimental import pallas as pl
from jax.experimental.pallas import tpu as pltpu
from jax.sharding import PartitionSpec as P

HEADS = 8
LAYERS = 2
WIDTH = 128
FF = 256
LEN = 256
HALF = 128
WINDOW = 192
FAR = -1.0e9
GELU_A = 0.7978845608028654
GELU_B = 0.044715
F32 = jnp.float32
BF16 = jnp.bfloat16

GAIN_ONE, SHIFT_ONE, GAIN_TWO, SHIFT_TWO, OUT_BIAS, DOWN_BIAS, Q_BIAS, V_BIAS, GATE, UP_LOW, UP_HIGH = range(11)
COLUMNS = 11
S_GAIN_ONE, S_SHIFT_ONE, S_GAIN_TWO, S_SHIFT_TWO, S_OUT, S_DOWN, S_V, S_GATE, S_UP_LOW, S_UP_HIGH = range(10)
SUMS = 10
R_QKV, R_OUT, R_UP, R_DOWN, R_SMALL, ROWS = 0, 384, 512, 768, 1024, 1056


def dot(left, right):
    return lax.dot_general(left, right, (((1,), (0,)), ((), ())), preferred_element_type=F32)


def dot_t(left, right):
    return lax.dot_general(left, right, (((1,), (1,)), ((), ())), preferred_element_type=F32)


def both(column):
    return jnp.concatenate([column, column], axis=1)


def fold(value):
    return value[:, :HALF] + value[:, HALF:]


def zeros(rows, lanes=LEN):
    return jnp.zeros((rows, lanes), BF16)


def split_three(value):
    high = value.astype(BF16)
    rest = value - high.astype(F32)
    middle = rest.astype(BF16)
    low = (rest - middle.astype(F32)).astype(BF16)
    return high, middle, low


def norm_parts(value):
    average = jnp.sum(value, axis=0, keepdims=True) * (1.0 / WIDTH)
    centered = value - average
    variance = jnp.sum(centered * centered, axis=0, keepdims=True) * (1.0 / WIDTH)
    scale = lax.rsqrt(variance + 1e-05)
    return centered * scale, scale


def pair_block(rows, pair, block):
    lanes = slice(block * HALF, (block + 1) * HALF)
    first = rows[32 * pair : 32 * pair + 16, lanes]
    second = rows[32 * pair + 16 : 32 * pair + 32, lanes]
    gap = zeros(16, HALF)
    return jnp.concatenate(
        [jnp.concatenate([first, gap], axis=1), jnp.concatenate([gap, second], axis=1)], axis=0
    )


def place(pair, block, extra):
    lanes = block.shape[1]
    if pair % 2 == 0:
        features = [block, zeros(32, lanes)]
    else:
        features = [zeros(32, lanes), block]
    if extra is None:
        other = [zeros(64, lanes)]
    else:
        other = [extra, zeros(64 - extra.shape[0], lanes)]
    return jnp.concatenate(features + other if pair < 2 else other + features, axis=0)


def token_rows(rows, extra_low, extra_high):
    low = jnp.concatenate([rows[:64], extra_low, zeros(64 - extra_low.shape[0])], axis=0)
    high = jnp.concatenate([extra_high, zeros(64 - extra_high.shape[0]), rows[64:]], axis=0)
    return low.T, high.T


def skewed(units):
    running, waiting = [], list(units)
    while running or waiting:
        if waiting:
            running.insert(0, waiting.pop(0))
        running = [unit for unit in running if next(unit, "end") != "end"]
        yield


def together(parts):
    running = list(parts)
    while running:
        running = [part for part in running if next(part, "end") != "end"]


def window_of(block):
    return slice(0, WINDOW) if block == 0 else slice(LEN - WINDOW, LEN)


def segment_masks(segments):
    ids = lax.broadcasted_iota(jnp.int32, (16, LEN), 0)
    same = ids == segments
    one_hot = jnp.where(same, 1.0, 0.0).astype(BF16)
    other = jnp.where(same | (ids >= 8), 0.0, FAR).astype(BF16)
    return one_hot, other


def forward_unit(block, pair, keys_rows, query, values, marks, mixed_ref, total_ref):
    window = window_of(block)
    lanes = slice(block * HALF, (block + 1) * HALF)
    weights = place(pair, pair_block(query, pair, block), both(marks[:, lanes]))
    scores = dot(keys_rows[window], weights)
    yield
    peak = jnp.max(scores, axis=0, keepdims=True)
    powers = jnp.exp(scores - peak).astype(BF16)
    yield
    ones = jnp.ones((16, WINDOW), BF16)
    mixed = dot(jnp.concatenate([values[32 * pair : 32 * pair + 32, window], ones], axis=0), powers)
    yield
    total = mixed[32:33]
    scale = 1.0 / total
    mixed_ref[32 * pair : 32 * pair + 16, lanes] = mixed[:16, :HALF] * scale[:, :HALF]
    mixed_ref[32 * pair + 16 : 32 * pair + 32, lanes] = mixed[16:32, HALF:] * scale[:, HALF:]
    log_total = peak + jnp.log(total)
    total_ref[2 * pair : 2 * pair + 1, lanes] = log_total[:, :HALF]
    total_ref[2 * pair + 1 : 2 * pair + 2, lanes] = log_total[:, HALF:]


def attention_forward(query, keys, values, one_hot, other, mixed_ref, total_ref):
    low, high = token_rows(keys, other, other)
    yield
    yield from skewed(
        forward_unit(block, pair, low if pair < 2 else high, query, values, one_hot, mixed_ref, total_ref)
        for block in range(2)
        for pair in range(4)
    )


def forward_layer(layer, hidden, segments, weights, columns, mixed_ref, total_ref):
    qkv_t, out_t, up_t, down_t = weights
    column = lambda which: both(columns[layer, which])
    xhat, unused = norm_parts(hidden)
    normed = (xhat * column(GAIN_ONE) + column(SHIFT_ONE)).astype(BF16)
    yield
    projected = dot(qkv_t[layer], normed)
    yield
    query = (projected[:WIDTH] + column(Q_BIAS)).astype(BF16)
    keys = projected[WIDTH : 2 * WIDTH].astype(BF16)
    values = (projected[2 * WIDTH :] + column(V_BIAS)).astype(BF16)
    one_hot, other = segments
    yield from attention_forward(query, keys, values, one_hot, other, mixed_ref, total_ref)
    mixed = mixed_ref[...].astype(BF16)
    middle = hidden + (dot(out_t[layer], mixed) + column(OUT_BIAS))
    yield
    xhat_two, unused = norm_parts(middle)
    normed_two = (xhat_two * column(GAIN_TWO) + column(SHIFT_TWO)).astype(BF16)
    yield
    inner = dot(up_t[layer], normed_two)
    yield
    logit = inner[FF : FF + 1]
    inner = inner[:FF] + jnp.concatenate([column(UP_LOW), column(UP_HIGH)], axis=0)
    gated = inner * jax.nn.sigmoid(logit)
    power = jnp.tanh(GELU_A * gated * (1.0 + GELU_B * (gated * gated)))
    active = (0.5 * gated * (1.0 + power)).astype(BF16)
    yield
    output = middle + (dot(down_t[layer], active) + column(DOWN_BIAS))
    return output, (normed, query, keys, values, mixed, middle, normed_two, inner, logit)


def norm_backward(gradient, xhat, scale, gain):
    inner = gradient * gain
    first = jnp.sum(inner, axis=0, keepdims=True) * (1.0 / WIDTH)
    second = jnp.sum(inner * xhat, axis=0, keepdims=True) * (1.0 / WIDTH)
    return scale * (inner - first - xhat * second)


def backward_unit(
    block, pair, query_rows, grad_rows, query, keys, values, grad_mixed, other, pattern, dk_ref, dv_ref, results
):
    window = window_of(block)
    lanes = slice(block * HALF, (block + 1) * HALF)
    key_block = pair_block(keys, pair, block)
    value_block = pair_block(values, pair, block)
    ones = pattern[pair]
    key_weights = place(pair, key_block, jnp.concatenate([both(other[:, lanes]), ones], axis=0))
    value_weights = place(pair, value_block, jnp.concatenate([zeros(16), ones], axis=0))
    scores = dot(query_rows[window], key_weights)
    grad_probs = dot(grad_rows[window], value_weights)
    yield
    probs = jnp.exp(scores)
    grad_scores = (probs * grad_probs).astype(BF16)
    probs = probs.astype(BF16)
    yield
    rows = slice(32 * pair, 32 * pair + 32)
    grad_values = dot(grad_mixed[rows, window], probs)
    grad_keys = dot(query[rows, window], grad_scores)
    parts = [key_block]
    if pair > 0:
        parts = [zeros(32 * pair)] + parts
    if pair < 3:
        parts = parts + [zeros(96 - 32 * pair)]
    grad_query = dot_t(grad_scores, jnp.concatenate(parts, axis=0))
    results[block] = grad_query if pair == 0 else results[block] + grad_query
    yield
    first, second = slice(32 * pair, 32 * pair + 16), slice(32 * pair + 16, 32 * pair + 32)
    dv_ref[first, lanes] = grad_values[:16, :HALF]
    dv_ref[second, lanes] = grad_values[16:, HALF:]
    dk_ref[first, lanes] = grad_keys[:16, :HALF]
    dk_ref[second, lanes] = grad_keys[16:, HALF:]


def attention_backward(query, keys, values, mixed, log_total, grad_mixed, one_hot, other, pattern, dk_ref, dv_ref):
    product = grad_mixed.astype(F32) * mixed.astype(F32)
    deltas = [
        jnp.sum(product[16 * head : 16 * head + 16], axis=0, keepdims=True) for head in range(HEADS)
    ]
    delta = jnp.concatenate(deltas, axis=0)
    gap = jnp.zeros((4, LEN), F32)

    def extras(value):
        parts = [part.astype(F32) for part in split_three(-value)]
        low = jnp.concatenate([part[:4] for part in parts] + [gap], axis=0).astype(BF16)
        high = jnp.concatenate([part[4:] for part in parts] + [gap], axis=0).astype(BF16)
        return low, high

    total_low, total_high = extras(log_total)
    delta_low, delta_high = extras(delta)
    query_low, query_high = token_rows(
        query, jnp.concatenate([one_hot, total_low], axis=0), jnp.concatenate([one_hot, total_high], axis=0)
    )
    grad_low, grad_high = token_rows(
        grad_mixed, jnp.concatenate([zeros(16), delta_low], axis=0), jnp.concatenate([zeros(16), delta_high], axis=0)
    )
    yield
    results = {}
    yield from skewed(
        backward_unit(
            block, pair, query_low if pair < 2 else query_high, grad_low if pair < 2 else grad_high, query, keys,
            values, grad_mixed, other, pattern, dk_ref, dv_ref, results,
        )
        for block in range(2)
        for pair in range(4)
    )
    windows = [results[0], results[1]]
    edge = LEN - WINDOW
    grad_query = jnp.concatenate(
        [windows[0][:edge], windows[0][edge:] + windows[1][: WINDOW - edge], windows[1][WINDOW - edge :]], axis=0
    )
    return (grad_query * 0.25).astype(BF16)


def backward_layer(layer, gradient, hidden, segments, kept, log_total, raw, columns, pattern, totals, dk_ref, dv_ref):
    w_qkv, w_out, w_up, w_down = raw
    normed, query, keys, values, mixed, middle, normed_two, inner, logit = kept
    qkv_total, out_total, up_total, down_total, sums, query_sum = totals
    column = lambda which: both(columns[layer, which])
    branch = gradient.astype(BF16)
    sums[S_DOWN] += fold(branch.astype(F32))
    grad_active = dot(w_down[layer], branch).astype(BF16).astype(F32)
    yield
    gate = jax.nn.sigmoid(logit)
    gated = inner * gate
    square = gated * gated
    power = jnp.tanh(GELU_A * gated * (1.0 + GELU_B * square))
    half_up = 0.5 + 0.5 * power
    active = (gated * half_up).astype(BF16)
    slope = half_up + gated * (half_up * (1.0 - power)) * (GELU_A + (3.0 * GELU_A * GELU_B) * square)
    grad_gated = grad_active * slope
    grad_logit = jnp.sum(grad_gated * inner, axis=0, keepdims=True) * (gate * (1.0 - gate))
    grad_inner = (grad_gated * gate).astype(BF16)
    yield
    down_total[...] += dot_t(branch, active)
    up_total[...] += dot_t(normed_two, grad_inner)
    inner_sum = fold(grad_inner.astype(F32))
    sums[S_UP_LOW] += inner_sum[:HALF]
    sums[S_UP_HIGH] += inner_sum[HALF:]
    sums[S_GATE] += fold(normed_two.astype(F32) * grad_logit)
    grad_two = dot(w_up[layer], grad_inner) + column(GATE) * grad_logit
    yield
    xhat, scale = norm_parts(middle)
    sums[S_GAIN_TWO] += fold(grad_two * xhat)
    sums[S_SHIFT_TWO] += fold(grad_two)
    grad_middle = gradient + norm_backward(grad_two, xhat, scale, column(GAIN_TWO))
    attended = grad_middle.astype(BF16)
    sums[S_OUT] += fold(attended.astype(F32))
    yield
    out_total[...] += dot_t(mixed, attended)
    grad_mixed = dot(w_out[layer], attended).astype(BF16)
    one_hot, other = segments
    yield
    grad_query = yield from attention_backward(
        query, keys, values, mixed, log_total, grad_mixed, one_hot, other, pattern, dk_ref, dv_ref
    )
    yield
    grad_keys = dk_ref[...].astype(BF16)
    grad_values = dv_ref[...].astype(BF16)
    grad_kv = jnp.concatenate([grad_keys, grad_values], axis=0)
    qkv_total[:, :WIDTH] += dot(normed, grad_query)
    qkv_total[:, WIDTH:] += dot_t(normed, grad_kv)
    query_sum[...] += jnp.sum(grad_query.astype(F32).reshape(LEN // 8, 8, WIDTH), axis=0)
    sums[S_V] += fold(grad_values.astype(F32))
    grad_one = dot_t(w_qkv[layer][:, :WIDTH], grad_query) + dot(w_qkv[layer][:, WIDTH:], grad_kv)
    yield
    xhat, scale = norm_parts(hidden)
    sums[S_GAIN_ONE] += fold(grad_one * xhat)
    sums[S_SHIFT_ONE] += fold(grad_one)
    return grad_middle + norm_backward(grad_one, xhat, scale, column(GAIN_ONE))


def spread(row):
    return jnp.broadcast_to(row, (WIDTH, WIDTH)).T


def fill_columns(layer, columns, gains, shifts, qv_bias, out_bias, w_gate, up_bias, down_bias):
    columns[layer, GAIN_ONE] = spread(gains[layer, 0:1])
    columns[layer, GAIN_TWO] = spread(gains[layer, 1:2])
    columns[layer, SHIFT_ONE] = spread(shifts[layer, 0:1])
    columns[layer, SHIFT_TWO] = spread(shifts[layer, 1:2])
    columns[layer, OUT_BIAS] = spread(out_bias[layer : layer + 1])
    columns[layer, DOWN_BIAS] = spread(down_bias[layer : layer + 1])
    columns[layer, Q_BIAS] = spread(qv_bias[layer : layer + 1, :WIDTH]) * 0.25
    columns[layer, V_BIAS] = spread(qv_bias[layer : layer + 1, WIDTH:])
    columns[layer, GATE] = spread(w_gate[layer : layer + 1].astype(F32))
    columns[layer, UP_LOW] = spread(up_bias[layer : layer + 1, :WIDTH])
    columns[layer, UP_HIGH] = spread(up_bias[layer : layer + 1, WIDTH:])


def clear_totals(totals):
    for ref in totals:
        ref[...] = jnp.zeros_like(ref)


def write_totals(totals, grads_ref):
    qkv_total, out_total, up_total, down_total, sums, query_sum = totals
    for part in range(3):
        rows = slice(R_QKV + part * WIDTH, R_QKV + (part + 1) * WIDTH)
        grads_ref[rows] = qkv_total[:, part * WIDTH : (part + 1) * WIDTH]
    grads_ref[R_OUT : R_OUT + WIDTH] = out_total[...]
    for part in range(2):
        lanes = slice(part * WIDTH, (part + 1) * WIDTH)
        grads_ref[R_UP + part * WIDTH : R_UP + (part + 1) * WIDTH] = up_total[:, lanes]
        grads_ref[R_DOWN + part * WIDTH : R_DOWN + (part + 1) * WIDTH] = down_total[:, lanes].T
    rows = [jnp.sum(sums[which].T, axis=0, keepdims=True) for which in range(SUMS)]
    rows.append(jnp.sum(query_sum[...], axis=0, keepdims=True))
    rows.append(jnp.zeros((ROWS - R_SMALL - len(rows), WIDTH), F32))
    grads_ref[R_SMALL:ROWS] = jnp.concatenate(rows, axis=0)


def first_kernel(
    per_step,
    x_ref, seg_ref, cot_ref, gains, shifts, w_qkv, qv_bias, w_out, out_bias, w_gate, w_up, up_bias, w_down, down_bias,
    pattern,
    result_ref, grad_ref, normed_ref, qkv_ref, mixed_ref, total_ref, middle_ref, normed_two_ref, inner_ref, logit_ref,
    grads_ref,
    columns, qkv_t, out_t, up_t, down_t, mixed_scratch, total_scratch, dk_ref, dv_ref, *totals,
):
    @pl.when(pl.program_id(0) == 0)
    def start():
        clear_totals(totals)
        for layer in range(LAYERS):
            fill_columns(layer, columns, gains, shifts, qv_bias, out_bias, w_gate, up_bias, down_bias)
            qkv_t[layer, :WIDTH] = (w_qkv[layer][:, :WIDTH] * jnp.asarray(0.25, BF16)).T
            qkv_t[layer, WIDTH:] = w_qkv[layer][:, WIDTH:].T
            out_t[layer] = w_out[layer].T
            up_t[layer, :FF] = w_up[layer].T
            up_t[layer, FF:] = jnp.concatenate(
                [w_gate[layer : layer + 1].astype(F32), jnp.zeros((15, WIDTH), F32)], axis=0
            ).astype(BF16)
            down_t[layer] = w_down[layer].T

    weights = (qkv_t, out_t, up_t, down_t)
    raw = (w_qkv, w_out, w_up, w_down)
    def sequence(item):
        tokens = slice(item * LEN, (item + 1) * LEN)
        segments = segment_masks(seg_ref[0, item : item + 1])
        hidden = x_ref[tokens].astype(F32).T
        middle_hidden, kept = yield from forward_layer(
            0, hidden, segments, weights, columns, mixed_scratch.at[item], total_scratch.at[item]
        )
        normed, query, keys, values, mixed, middle, normed_two, inner, logit = kept
        normed_ref[item] = normed
        qkv_ref[item, :WIDTH] = query
        qkv_ref[item, WIDTH : 2 * WIDTH] = keys
        qkv_ref[item, 2 * WIDTH :] = values
        mixed_ref[item] = mixed
        total_ref[item] = total_scratch[item]
        middle_ref[item] = middle
        normed_two_ref[item] = normed_two
        inner_ref[item] = inner
        logit_ref[item] = jnp.broadcast_to(logit, (8, LEN))
        output, kept = yield from forward_layer(
            1, middle_hidden, segments, weights, columns, mixed_scratch.at[item], total_scratch.at[item]
        )
        result_ref[tokens] = output.T.astype(BF16)
        gradient = cot_ref[tokens].astype(F32).T
        grad_ref[item] = yield from backward_layer(
            1, gradient, middle_hidden, segments, kept, total_scratch[item], raw, columns, pattern, totals,
            dk_ref.at[item], dv_ref.at[item],
        )

    together([sequence(item) for item in range(per_step)])

    @pl.when(pl.program_id(0) == pl.num_programs(0) - 1)
    def finish():
        write_totals(totals, grads_ref)


def second_kernel(
    per_step,
    x_ref, seg_ref, grad_ref, gains, shifts, w_qkv, qv_bias, w_out, out_bias, w_gate, w_up, up_bias, w_down, down_bias,
    pattern, normed_ref, qkv_ref, mixed_ref, total_ref, middle_ref, normed_two_ref, inner_ref, logit_ref,
    grad_inputs_ref, grads_ref,
    columns, dk_ref, dv_ref, *totals,
):
    @pl.when(pl.program_id(0) == 0)
    def start():
        clear_totals(totals)
        fill_columns(0, columns, gains, shifts, qv_bias, out_bias, w_gate, up_bias, down_bias)

    raw = (w_qkv, w_out, w_up, w_down)
    def sequence(item):
        tokens = slice(item * LEN, (item + 1) * LEN)
        segments = segment_masks(seg_ref[0, item : item + 1])
        hidden = x_ref[tokens].astype(F32).T
        kept = (
            normed_ref[item], qkv_ref[item, :WIDTH], qkv_ref[item, WIDTH : 2 * WIDTH], qkv_ref[item, 2 * WIDTH :],
            mixed_ref[item], middle_ref[item], normed_two_ref[item], inner_ref[item], logit_ref[item, 0:1],
        )
        gradient = yield from backward_layer(
            0, grad_ref[item], hidden, segments, kept, total_ref[item], raw, columns, pattern, totals,
            dk_ref.at[item], dv_ref.at[item],
        )
        grad_inputs_ref[tokens] = gradient.T

    together([sequence(item) for item in range(per_step)])

    @pl.when(pl.program_id(0) == pl.num_programs(0) - 1)
    def finish():
        write_totals(totals, grads_ref)


def totals_scratch():
    return [
        pltpu.VMEM((WIDTH, 3 * WIDTH), F32),
        pltpu.VMEM((WIDTH, WIDTH), F32),
        pltpu.VMEM((WIDTH, FF), F32),
        pltpu.VMEM((WIDTH, FF), F32),
        pltpu.VMEM((SUMS, WIDTH, WIDTH), F32),
        pltpu.VMEM((8, WIDTH), F32),
    ]


def head_pattern():
    rows = lax.broadcasted_iota(jnp.int32, (4, 16, LEN), 1)
    pairs = lax.broadcasted_iota(jnp.int32, (4, 16, LEN), 0)
    lanes = lax.broadcasted_iota(jnp.int32, (4, 16, LEN), 2)
    head = (pairs % 2) * 2 + lanes // HALF
    return ((rows < 12) & (rows % 4 == head)).astype(BF16)


def local_part(inputs, segment_ids, cotangent, *parameters, per_step=4):
    seqs = segment_ids.shape[0]
    per_step = min(per_step, seqs)
    steps = seqs // per_step
    segments = segment_ids.reshape(steps, per_step, LEN)
    pattern = head_pattern()
    tokens = pl.BlockSpec((per_step * LEN, WIDTH), lambda i: (i, 0))
    segment_spec = pl.BlockSpec((1, per_step, LEN), lambda i: (i, 0, 0))

    def whole(array):
        zero = (0,) * array.ndim
        return pl.BlockSpec(array.shape, lambda i: zero)

    def kept(rows):
        return pl.BlockSpec((per_step, rows, LEN), lambda i: (i, 0, 0))

    kept_shapes = [
        (WIDTH, BF16), (3 * WIDTH, BF16), (WIDTH, BF16), (HEADS, F32), (WIDTH, F32), (WIDTH, BF16), (FF, F32), (8, F32),
    ]
    kept_specs = [kept(rows) for rows, unused in kept_shapes]
    grads_spec = pl.BlockSpec((ROWS, WIDTH), lambda i: (0, 0))
    grads_shape = jax.ShapeDtypeStruct((ROWS, WIDTH), F32)
    params = pltpu.CompilerParams(vmem_limit_bytes=56 * 1024 * 1024)
    first = pl.pallas_call(
        lambda *refs: first_kernel(per_step, *refs),
        grid=(steps,),
        in_specs=[tokens, segment_spec, tokens] + [whole(entry) for entry in parameters] + [whole(pattern)],
        out_specs=[tokens, kept(WIDTH)] + kept_specs + [grads_spec],
        out_shape=[
            jax.ShapeDtypeStruct(inputs.shape, BF16),
            jax.ShapeDtypeStruct((seqs, WIDTH, LEN), F32),
        ]
        + [jax.ShapeDtypeStruct((seqs, rows, LEN), dtype) for rows, dtype in kept_shapes]
        + [grads_shape],
        scratch_shapes=[
            pltpu.VMEM((LAYERS, COLUMNS, WIDTH, WIDTH), F32),
            pltpu.VMEM((LAYERS, 3 * WIDTH, WIDTH), BF16),
            pltpu.VMEM((LAYERS, WIDTH, WIDTH), BF16),
            pltpu.VMEM((LAYERS, FF + 16, WIDTH), BF16),
            pltpu.VMEM((LAYERS, WIDTH, FF), BF16),
            pltpu.VMEM((per_step, WIDTH, LEN), F32),
            pltpu.VMEM((per_step, HEADS, LEN), F32),
            pltpu.VMEM((per_step, WIDTH, LEN), F32),
            pltpu.VMEM((per_step, WIDTH, LEN), F32),
        ]
        + totals_scratch(),
        compiler_params=params,
        name="forward_and_last_backward",
    )(inputs, segments, cotangent, *parameters, pattern)
    result, gradient, saved, grads_one = first[0], first[1], first[2:-1], first[-1]
    grad_inputs, grads_zero = pl.pallas_call(
        lambda *refs: second_kernel(per_step, *refs),
        grid=(steps,),
        in_specs=[tokens, segment_spec, kept(WIDTH)]
        + [whole(entry) for entry in parameters]
        + [whole(pattern)]
        + kept_specs,
        out_specs=[tokens, grads_spec],
        out_shape=[jax.ShapeDtypeStruct(inputs.shape, F32), grads_shape],
        scratch_shapes=[
            pltpu.VMEM((1, COLUMNS, WIDTH, WIDTH), F32),
            pltpu.VMEM((per_step, WIDTH, LEN), F32),
            pltpu.VMEM((per_step, WIDTH, LEN), F32),
        ]
        + totals_scratch(),
        compiler_params=params,
        name="first_backward",
    )(inputs, segments, gradient, *parameters, pattern, *saved)
    return result, grad_inputs, grads_zero, grads_one


def unpack(grads):
    small = grads[:, R_SMALL:]
    gains = jnp.stack([small[:, S_GAIN_ONE], small[:, S_GAIN_TWO]], axis=1)
    shifts = jnp.stack([small[:, S_SHIFT_ONE], small[:, S_SHIFT_TWO]], axis=1)
    qkv = jnp.concatenate([grads[:, R_QKV + i * WIDTH : R_QKV + (i + 1) * WIDTH] for i in range(3)], axis=2)
    up = jnp.concatenate([grads[:, R_UP + i * WIDTH : R_UP + (i + 1) * WIDTH] for i in range(2)], axis=2)
    return (
        gains,
        shifts,
        qkv,
        jnp.concatenate([small[:, SUMS], small[:, S_V]], axis=1),
        grads[:, R_OUT : R_OUT + WIDTH],
        small[:, S_OUT],
        small[:, S_GATE],
        up,
        jnp.concatenate([small[:, S_UP_LOW], small[:, S_UP_HIGH]], axis=1),
        grads[:, R_DOWN : R_DOWN + FF],
        small[:, S_DOWN],
    )


def all_sum(zero, one, size):
    me = lax.axis_index("seq")
    bits = size.bit_length() - 1

    def swap(value, bit):
        return lax.ppermute(value, "seq", [(i, i ^ (1 << bit)) for i in range(size)])

    halves = (zero, one)
    sides = []
    for bit in range(bits):
        side = (me >> bit) & 1
        if bit >= 3:
            current = current + swap(current, bit)
            continue
        sides.append(side)
        mine = jnp.where(side == 0, halves[0], halves[1])
        others = jnp.where(side == 0, halves[1], halves[0])
        current = mine + swap(others, bit)
        middle = current.shape[0] // 2
        halves = (current[:middle], current[middle:])
    for bit in reversed(range(min(bits, 3))):
        others = swap(current, bit)
        first = jnp.where(sides[bit] == 0, current, others)
        second = jnp.where(sides[bit] == 0, others, current)
        current = jnp.concatenate([first, second], axis=0)
    return current.reshape(LAYERS, ROWS, WIDTH)


def body(size, *arguments):
    result, grad_inputs, grads_zero, grads_one = local_part(*arguments)
    if size & (size - 1) or size < 2:
        grads = lax.psum(jnp.stack([grads_zero, grads_one]), "seq")
    else:
        grads = all_sum(grads_zero, grads_one, size)
    return (result, grad_inputs) + unpack(grads)


def solution(mesh):
    rows = P("seq", None)
    return jax.shard_map(
        lambda *arguments: body(mesh.shape["seq"], *arguments),
        mesh=mesh,
        in_specs=(rows, rows, rows) + (P(),) * 11,
        out_specs=(rows, rows) + (P(),) * 11,
        check_vma=False,
    )
```

profile of v0, /device:TPU:0, one launch (start us, length us, event | category | flops | bytes accessed | tf_op | source)
XLA Modules:
  0.0 127.8 jit_solution(14002931284216694392)
XLA Ops:
  0.7 1.3 %reshape.32.refs_1_ = s32[4,4,256]{2,1,0:T(4,128)} reshape(s32[16,256]{1,0:T(8,128)} %param.15) | data formatting | bytes 32768 | tf_op jit(solution)/shard_map/reshape | solution.py:477
  2.1 0.7 fusion.1.refs_14_
  2.8 47.3 %forward_and_last_backward.1 = (bf16[4096,128]{1,0:T(8,128)(2,1)}, f32[16,128,256]{2,1,0:T(8,128)}, bf16[16,128,256]{2,1,0:T(8,128)(2,1)}, bf16[16,384,256]{2,1,...) custom-call(bf16[4096,128]{1,0:T(8,128)(2,1)} %refs_0_.3, ...), custom_call_target="tpu_custom_call" | custom-call | tf_op jit(solution)/shard_map/forward_and_last_backward/pallas_call | solution.py:496
  50.0 0.0 copy-start
  50.0 27.2 %first_backward.1 = (f32[4096,128]{1,0:T(8,128)}, f32[1056,128]{1,0:T(8,128)}) custom-call(bf16[4096,128]{1,0:T(8,128)(2,1)} %refs_0_.3, s32[4,4,256]{2,1,0:T(4,128)} %reshape.32.refs_1_, f32[16,128,256]{2,1,0:T(8,128)} %get-tuple-element.27.refs_2_, f32[2,2,128]{2,1,0:T(2,128)} %refs_3_.3, f32[2,2,128]{2,1,0:T(2,128)} %refs_4_.3, ...), custom_call_target="tpu_custom_call" | custom-call | tf_op jit(solution)/shard_map/first_backward/pallas_call | solution.py:523
  77.2 0.0 copy-start.1
  77.2 0.0 copy-done
  77.3 0.1 broadcast_select_fusion.2
  77.3 1.6 %collective-permute-start = (f32[1056,128]{1,0:T(8,128)S(1)}, f32[1056,128]{1,0:T(8,128)S(1)}, u32[]{:S(2)}, u32[]{:S(2)}) collective-permute-start(f32[1056,128]{1,0:T(8,128)S(1)} %broadcast_select_fusion.2), channel_id=1, source_target_pairs={{0,1},{1,0},{2,3},{3,2},{4,5},{5,4},{6,7},{7,6},{8,9},{9,8},{10,11... | collective-permute-start | bytes 1622024 | tf_op jit(solution)/shard_map/ppermute | solution.py:570
  78.9 1.6 %collective-permute-done = f32[1056,128]{1,0:T(8,128)S(1)} collective-permute-done((f32[1056,128]{1,0:T(8,128)S(1)}, f32[1056,128]{1,0:T(8,128)S(1)}, u32[]{:S(2)}, u32[]{:S(2)}) %collective-permute-start) | collective-permute-done | bytes 540704 | tf_op jit(solution)/shard_map/ppermute | solution.py:570
  80.5 0.0 copy-done.1
  80.5 0.1 select_add_fusion
  80.6 2.4 %collective-permute-start.1 = (f32[528,128]{1,0:T(8,128)S(1)}, f32[528,128]{1,0:T(8,128)S(1)}, u32[]{:S(2)}, u32[]{:S(2)}) collective-permute-start(f32[528,128]{1,0:T(8,128)S(1)} %slice_select_fusion), channel_id=1, source_target_pairs={{0,2},{1,3},{2,0},{3,1},{4,6},{5,7},{6,4},{7,5},{8,10},{9,11},{10,... | collective-permute-start | bytes 811016 | tf_op jit(solution)/shard_map/ppermute | solution.py:570
  83.0 7.0 %collective-permute-done.1 = f32[528,128]{1,0:T(8,128)S(1)} collective-permute-done((f32[528,128]{1,0:T(8,128)S(1)}, f32[528,128]{1,0:T(8,128)S(1)}, u32[]{:S(2)}, u32[]{:S(2)}) %collective-permute-start.1) | collective-permute-done | bytes 270368 | tf_op jit(solution)/shard_map/ppermute | solution.py:570
  90.1 1.8 %collective-permute-start.2 = (f32[264,128]{1,0:T(8,128)S(1)}, f32[264,128]{1,0:T(8,128)S(1)}, u32[]{:S(2)}, u32[]{:S(2)}) collective-permute-start(f32[264,128]{1,0:T(8,128)S(1)} %slice_select_fusion.1), channel_id=1, source_target_pairs={{0,4},{1,5},{2,6},{3,7},{4,0},{5,1},{6,2},{7,3},{8,12},{9,13},{10,... | collective-permute-start | bytes 405512 | tf_op jit(solution)/shard_map/ppermute | solution.py:570
  91.9 3.5 %collective-permute-done.2 = f32[264,128]{1,0:T(8,128)S(1)} collective-permute-done((f32[264,128]{1,0:T(8,128)S(1)}, f32[264,128]{1,0:T(8,128)S(1)}, u32[]{:S(2)}, u32[]{:S(2)}) %collective-permute-start.2) | collective-permute-done | bytes 135200 | tf_op jit(solution)/shard_map/ppermute | solution.py:570
  95.5 1.6 %collective-permute-start.3 = (f32[264,128]{1,0:T(8,128)S(1)}, f32[264,128]{1,0:T(8,128)S(1)}, u32[]{:S(2)}, u32[]{:S(2)}) collective-permute-start(f32[264,128]{1,0:T(8,128)S(1)} %select_add_fusion.2), channel_id=1, source_target_pairs={{0,8},{1,9},{2,10},{3,11},{4,12},{5,13},{6,14},{7,15},{8,0},{9,1},... | collective-permute-start | bytes 405512 | tf_op jit(solution)/shard_map/ppermute | solution.py:570
  97.1 3.4 %collective-permute-done.3 = f32[264,128]{1,0:T(8,128)S(1)} collective-permute-done((f32[264,128]{1,0:T(8,128)S(1)}, f32[264,128]{1,0:T(8,128)S(1)}, u32[]{:S(2)}, u32[]{:S(2)}) %collective-permute-start.3) | collective-permute-done | bytes 135200 | tf_op jit(solution)/shard_map/ppermute | solution.py:570
  100.6 2.8 %collective-permute-start.4 = (f32[264,128]{1,0:T(8,128)S(1)}, f32[264,128]{1,0:T(8,128)S(1)}, u32[]{:S(2)}, u32[]{:S(2)}) collective-permute-start(f32[264,128]{1,0:T(8,128)S(1)} %add.44), channel_id=1, source_target_pairs={{0,16},{1,17},{2,18},{3,19},{4,20},{5,21},{6,22},{7,23},{8,24},{9,... | collective-permute-start | bytes 405512 | tf_op jit(solution)/shard_map/ppermute | solution.py:570
  103.4 4.6 %collective-permute-done.4 = f32[264,128]{1,0:T(8,128)S(1)} collective-permute-done((f32[264,128]{1,0:T(8,128)S(1)}, f32[264,128]{1,0:T(8,128)S(1)}, u32[]{:S(2)}, u32[]{:S(2)}) %collective-permute-start.4) | collective-permute-done | bytes 135200 | tf_op jit(solution)/shard_map/ppermute | solution.py:570
  108.0 1.6 %collective-permute-start.5 = (f32[264,128]{1,0:T(8,128)S(1)}, f32[264,128]{1,0:T(8,128)S(1)}, u32[]{:S(2)}, u32[]{:S(2)}) collective-permute-start(f32[264,128]{1,0:T(8,128)S(1)} %add.45), channel_id=1, source_target_pairs={{0,4},{1,5},{2,6},{3,7},{4,0},{5,1},{6,2},{7,3},{8,12},{9,13},{10,... | collective-permute-start | bytes 405512 | tf_op jit(solution)/shard_map/ppermute | solution.py:570
  109.6 3.5 %collective-permute-done.5 = f32[264,128]{1,0:T(8,128)S(1)} collective-permute-done((f32[264,128]{1,0:T(8,128)S(1)}, f32[264,128]{1,0:T(8,128)S(1)}, u32[]{:S(2)}, u32[]{:S(2)}) %collective-permute-start.5) | collective-permute-done | bytes 135200 | tf_op jit(solution)/shard_map/ppermute | solution.py:570
  113.2 1.6 %collective-permute-start.6 = (f32[528,128]{1,0:T(8,128)S(1)}, f32[528,128]{1,0:T(8,128)S(1)}, u32[]{:S(2)}, u32[]{:S(2)}) collective-permute-start(f32[528,128]{1,0:T(8,128)S(1)} %pad_maximum_fusion.3), channel_id=1, source_target_pairs={{0,2},{1,3},{2,0},{3,1},{4,6},{5,7},{6,4},{7,5},{8,10},{9,11},{10,... | collective-permute-start | bytes 811016 | tf_op jit(solution)/shard_map/ppermute | solution.py:570
  114.7 5.0 %collective-permute-done.6 = f32[528,128]{1,0:T(8,128)S(1)} collective-permute-done((f32[528,128]{1,0:T(8,128)S(1)}, f32[528,128]{1,0:T(8,128)S(1)}, u32[]{:S(2)}, u32[]{:S(2)}) %collective-permute-start.6) | collective-permute-done | bytes 270368 | tf_op jit(solution)/shard_map/ppermute | solution.py:570
  119.8 0.1 collective-permute-start.7
  119.9 1.9 %collective-permute-done.7 = f32[1056,128]{1,0:T(8,128)S(1)} collective-permute-done((f32[1056,128]{1,0:T(8,128)S(1)}, f32[1056,128]{1,0:T(8,128)S(1)}, u32[]{:S(2)}, u32[]{:S(2)}) %collective-permute-start.7) | collective-permute-done | bytes 540704 | tf_op jit(solution)/shard_map/ppermute | solution.py:570
  121.8 0.1 broadcast_select_fusion.1
  121.8 0.1 pad_maximum_fusion
  121.9 0.6 fusion.2
  122.5 0.7 fusion.3
  123.2 0.7 slice.120
  123.9 0.6 pad_maximum_fusion.8
  124.5 0.7 pad_maximum_fusion.4
  125.2 0.6 pad_maximum_fusion.7
  125.8 0.6 pad_maximum_fusion.6
  126.4 0.6 pad_maximum_fusion.5
  127.0 0.8 pad_maximum_fusion.2
  (16 shorter events, 0.3 us)
Async XLA Ops:
  50.0 27.2 %copy-start = (f32[1056,128]{1,0:T(8,128)S(1)}, f32[1056,128]{1,0:T(8,128)}, u32[]{:S(2)}) copy-start(f32[1056,128]{1,0:T(8,128)} %get-tuple-element.38) | copy-start | bytes 1622020
  77.2 3.3 %copy-start.1 = (f32[1056,128]{1,0:T(8,128)S(1)}, f32[1056,128]{1,0:T(8,128)}, u32[]{:S(2)}) copy-start(f32[1056,128]{1,0:T(8,128)} %get-tuple-element.37) | copy-start | bytes 1622020
  77.3 3.2 %collective-permute-start = (f32[1056,128]{1,0:T(8,128)S(1)}, f32[1056,128]{1,0:T(8,128)S(1)}, u32[]{:S(2)}, u32[]{:S(2)}) collective-permute-start(f32[1056,128]{1,0:T(8,128)S(1)} %broadcast_select_fusion.2), channel_id=1, source_target_pairs={{0,1},{1,0},{2,3},{3,2},{4,5},{5,4},{6,7},{7,6},{8,9},{9,8},{10,11... | collective-permute-start | bytes 1622024 | tf_op jit(solution)/shard_map/ppermute | solution.py:570
  80.6 9.4 %collective-permute-start.1 = (f32[528,128]{1,0:T(8,128)S(1)}, f32[528,128]{1,0:T(8,128)S(1)}, u32[]{:S(2)}, u32[]{:S(2)}) collective-permute-start(f32[528,128]{1,0:T(8,128)S(1)} %slice_select_fusion), channel_id=1, source_target_pairs={{0,2},{1,3},{2,0},{3,1},{4,6},{5,7},{6,4},{7,5},{8,10},{9,11},{10,... | collective-permute-start | bytes 811016 | tf_op jit(solution)/shard_map/ppermute | solution.py:570
  90.1 5.4 %collective-permute-start.2 = (f32[264,128]{1,0:T(8,128)S(1)}, f32[264,128]{1,0:T(8,128)S(1)}, u32[]{:S(2)}, u32[]{:S(2)}) collective-permute-start(f32[264,128]{1,0:T(8,128)S(1)} %slice_select_fusion.1), channel_id=1, source_target_pairs={{0,4},{1,5},{2,6},{3,7},{4,0},{5,1},{6,2},{7,3},{8,12},{9,13},{10,... | collective-permute-start | bytes 405512 | tf_op jit(solution)/shard_map/ppermute | solution.py:570
  95.5 5.1 %collective-permute-start.3 = (f32[264,128]{1,0:T(8,128)S(1)}, f32[264,128]{1,0:T(8,128)S(1)}, u32[]{:S(2)}, u32[]{:S(2)}) collective-permute-start(f32[264,128]{1,0:T(8,128)S(1)} %select_add_fusion.2), channel_id=1, source_target_pairs={{0,8},{1,9},{2,10},{3,11},{4,12},{5,13},{6,14},{7,15},{8,0},{9,1},... | collective-permute-start | bytes 405512 | tf_op jit(solution)/shard_map/ppermute | solution.py:570
  100.6 7.4 %collective-permute-start.4 = (f32[264,128]{1,0:T(8,128)S(1)}, f32[264,128]{1,0:T(8,128)S(1)}, u32[]{:S(2)}, u32[]{:S(2)}) collective-permute-start(f32[264,128]{1,0:T(8,128)S(1)} %add.44), channel_id=1, source_target_pairs={{0,16},{1,17},{2,18},{3,19},{4,20},{5,21},{6,22},{7,23},{8,24},{9,... | collective-permute-start | bytes 405512 | tf_op jit(solution)/shard_map/ppermute | solution.py:570
  108.0 5.1 %collective-permute-start.5 = (f32[264,128]{1,0:T(8,128)S(1)}, f32[264,128]{1,0:T(8,128)S(1)}, u32[]{:S(2)}, u32[]{:S(2)}) collective-permute-start(f32[264,128]{1,0:T(8,128)S(1)} %add.45), channel_id=1, source_target_pairs={{0,4},{1,5},{2,6},{3,7},{4,0},{5,1},{6,2},{7,3},{8,12},{9,13},{10,... | collective-permute-start | bytes 405512 | tf_op jit(solution)/shard_map/ppermute | solution.py:570
  113.2 6.5 %collective-permute-start.6 = (f32[528,128]{1,0:T(8,128)S(1)}, f32[528,128]{1,0:T(8,128)S(1)}, u32[]{:S(2)}, u32[]{:S(2)}) collective-permute-start(f32[528,128]{1,0:T(8,128)S(1)} %pad_maximum_fusion.3), channel_id=1, source_target_pairs={{0,2},{1,3},{2,0},{3,1},{4,6},{5,7},{6,4},{7,5},{8,10},{9,11},{10,... | collective-permute-start | bytes 811016 | tf_op jit(solution)/shard_map/ppermute | solution.py:570
  119.8 2.0 %collective-permute-start.7 = (f32[1056,128]{1,0:T(8,128)S(1)}, f32[1056,128]{1,0:T(8,128)S(1)}, u32[]{:S(2)}, u32[]{:S(2)}) collective-permute-start(f32[1056,128]{1,0:T(8,128)S(1)} %pad_maximum_fusion.1), channel_id=1, source_target_pairs={{0,1},{1,0},{2,3},{3,2},{4,5},{5,4},{6,7},{7,6},{8,9},{9,8},{10,11... | collective-permute-start | bytes 1622024 | tf_op jit(solution)/shard_map/ppermute | solution.py:570
where the time goes:
time: 128 us
  Pallas kernels  74.5 us (58%)
  waiting for transfers between devices  30.5 us (24%)
  starting transfers between devices  13.5 us (11%)
  other arithmetic  5.14 us (4%)
  local copies, waits for them, and re-layouts  3.35 us (3%)
    pallas_call x1, Pallas kernels, local_part(): pl.pallas_call(lambda *refs: first_kernel(per_step, *refs), grid=(steps,)...  47.3 us
    ppermute x8, waiting for transfers between devices, swap(): return lax.ppermute(value, 'seq', [(i, i ^ 1 << bit) for i in range(size)])  30.5 us
    pallas_call x1, Pallas kernels, local_part(): pl.pallas_call(lambda *refs: second_kernel(per_step, *refs), grid=(steps,...  27.2 us
    ppermute x8, starting transfers between devices, swap(): return lax.ppermute(value, 'seq', [(i, i ^ 1 << bit) for i in range(size)])  13.5 us
  transfers between devices with their start and end apart: 8, of which 8 were waited for; matrix products, arithmetic and copies ran while one was open for 0% of the time, Pallas kernels for 0%

commit v1 on v0

v1 whole, which is shorter than its diff:
```python
import jax
import jax.numpy as jnp
from jax import lax
from jax.experimental import pallas as pl
from jax.experimental.pallas import tpu as pltpu
from jax.sharding import PartitionSpec as P

HEADS = 8
LAYERS = 2
WIDTH = 128
FF = 256
LEN = 256
HALF = 128
CHUNK = 64
QUARTER = 64
WINDOWS = ((0, 128), (0, 192), (64, 256), (128, 256))
PLACES = ((0, 128), (256, 448), (640, 832), (1024, 1152))
POWER_ROWS = 1280
FAR = -1.0e9
GELU_A = 0.7978845608028654
GELU_B = 0.044715
F32 = jnp.float32
BF16 = jnp.bfloat16

GAIN_ONE, SHIFT_ONE, GAIN_TWO, SHIFT_TWO, OUT_BIAS, DOWN_BIAS, Q_BIAS, V_BIAS, GATE, UP_LOW, UP_HIGH = range(11)
COLUMNS = 11
S_GAIN_ONE, S_SHIFT_ONE, S_GAIN_TWO, S_SHIFT_TWO, S_DOWN, S_GATE = range(6)
SUMS = 6
S_OUT, S_Q, S_K, S_V, S_UP_LOW, S_UP_HIGH, SMALL = range(6, 13)
R_QKV, R_OUT, R_UP, R_DOWN, R_SMALL, ROWS = 0, 384, 512, 768, 1024, 1056


def dot(left, right):
    return lax.dot_general(left, right, (((1,), (0,)), ((), ())), preferred_element_type=F32)


def both(column):
    return jnp.concatenate([column, column], axis=1)


def fold(value):
    return value[:, :HALF] + value[:, HALF:]


def zeros(rows, lanes=LEN):
    return jnp.zeros((rows, lanes), BF16)


def ones(rows, lanes=LEN):
    return jnp.ones((rows, lanes), BF16)


def split_three(value):
    high = value.astype(BF16)
    rest = value - high.astype(F32)
    middle = rest.astype(BF16)
    low = (rest - middle.astype(F32)).astype(BF16)
    return high, middle, low


def norm_parts(value):
    average = jnp.sum(value, axis=0, keepdims=True) * (1.0 / WIDTH)
    centered = value - average
    variance = jnp.sum(centered * centered, axis=0, keepdims=True) * (1.0 / WIDTH)
    scale = lax.rsqrt(variance + 1e-05)
    return centered * scale, scale


def lane_mask(rows, which):
    row = lax.broadcasted_iota(jnp.int32, (rows, HALF), 0)
    lane = lax.broadcasted_iota(jnp.int32, (rows, HALF), 1)
    return jnp.where(which(row, lane < QUARTER), 1.0, 0.0).astype(BF16)


def turned(rows):
    return jnp.concatenate(
        [rows[:, 64:128], rows[:, :64], rows[:, 192:256], rows[:, 128:192]], axis=1
    )


def make_masks():
    low = lane_mask(16, lambda row, left: left)
    high = lane_mask(16, lambda row, left: ~left)
    heads = [
        lane_mask(16, lambda row, left, head=head: (row % 4 == head) & (left if head % 2 == 0 else ~left))
        for head in range(4)
    ]
    return low, high, heads


def halves_of(rows, masks):
    low, high, unused = masks
    count = rows.shape[0] // 16
    low_all = jnp.concatenate([both(low)] * count, axis=0)
    high_all = jnp.concatenate([both(high)] * count, axis=0)
    other = turned(rows)
    return ((rows * low_all, other * high_all), (other * low_all, rows * high_all))


def head_block(variants, block, group):
    lanes = slice((block // 2) * HALF, (block // 2 + 1) * HALF)
    gap = zeros(16, HALF)
    pieces = []
    for head in range(4):
        first = QUARTER * group + 16 * head
        piece = variants[block % 2][head % 2][first : first + 16, lanes]
        pieces.append(jnp.concatenate([piece, gap] if head < 2 else [gap, piece], axis=1))
    return jnp.concatenate(pieces, axis=0)


def with_extra(features, extra):
    return jnp.concatenate([features, extra], axis=0)


def spread_marks(rows, masks, block):
    low, high, unused = masks
    lanes = slice((block // 2) * HALF, (block // 2 + 1) * HALF)
    here, there = rows[:, lanes], turned(rows)[:, lanes]
    once = here * low + there * high if block % 2 == 0 else there * low + here * high
    return both(once)


def spread_rows(rows, masks, block):
    unused, unused, heads = masks
    lanes = slice((block // 2) * HALF, (block // 2 + 1) * HALF)
    here, there = rows[:, lanes], turned(rows)[:, lanes]
    if block % 2 == 1:
        here, there = there, here
    return jnp.concatenate([here * heads[0] + there * heads[1], here * heads[2] + there * heads[3]], axis=1)


def join_blocks(even, odd, head):
    left = lax.broadcasted_iota(jnp.int32, even.shape, 1) < QUARTER
    if head % 2 == 0:
        return jnp.where(left, even, pltpu.roll(odd, QUARTER, 1))
    return jnp.where(left, pltpu.roll(even, QUARTER, 1), odd)


def token_rows(rows, extra):
    return [
        jnp.concatenate([rows[QUARTER * group : QUARTER * group + QUARTER], extra], axis=0).T for group in range(2)
    ]


def skewed(units):
    running, waiting = [], list(units)
    while running or waiting:
        if waiting:
            running.insert(0, waiting.pop(0))
        running = [unit for unit in running if next(unit, "end") != "end"]
        yield


def together(parts):
    running = list(parts)
    while running:
        running = [part for part in running if next(part, "end") != "end"]


def segment_masks(segments):
    ids = lax.broadcasted_iota(jnp.int32, (16, LEN), 0)
    same = ids == segments
    one_hot = jnp.where(same, 1.0, 0.0).astype(BF16)
    other = jnp.where(same | (ids >= 8), 0.0, FAR).astype(BF16)
    return one_hot, other


def forward_unit(block, group, keys_rows, variants, values, marks, power_ref, mixed_ref, scale_ref, results):
    first, last = WINDOWS[block]
    weights = with_extra(head_block(variants, block, group), marks[block])
    scores = dot(keys_rows[first:last], weights)
    yield
    peak = jnp.max(scores, axis=0, keepdims=True)
    powers = jnp.exp(scores - peak).astype(BF16)
    start = PLACES[block][group]
    power_ref[start : start + last - first] = powers
    yield
    rows = values[QUARTER * group : QUARTER * group + QUARTER, first:last]
    mixed = dot(jnp.concatenate([rows, ones(16, last - first)], axis=0), powers)
    yield
    scale = 1.0 / mixed[QUARTER : QUARTER + 8]
    results[block, group] = (mixed, scale)
    if block % 2 == 0:
        return
    even, even_scale = results[block - 1, group]
    lanes = slice((block // 2) * HALF, (block // 2 + 1) * HALF)
    for head in range(4):
        tile = slice((head // 2) * HALF, (head // 2 + 1) * HALF)
        rows = slice(16 * head, 16 * head + 16)
        factor = join_blocks(even_scale[:, tile], scale[:, tile], head)
        joined = join_blocks(even[rows, tile], mixed[rows, tile], head)
        place = QUARTER * group + 16 * head
        mixed_ref[place : place + 16, lanes] = joined * jnp.concatenate([factor, factor], axis=0)
        place = 8 * (4 * group + head)
        scale_ref[place : place + 8, lanes] = factor


def attention_forward(query, keys, values, segments, masks, power_ref, mixed_ref, scale_ref):
    one_hot, other = segments
    rows = token_rows(keys, other)
    variants = halves_of(query, masks)
    marks = [spread_marks(one_hot, masks, block) for block in range(4)]
    yield
    results = {}
    yield from skewed(
        forward_unit(block, group, rows[group], variants, values, marks, power_ref, mixed_ref, scale_ref, results)
        for block in (0, 1, 2, 3)
        for group in range(2)
    )


def forward_layer(layer, hidden, segments, masks, weights, columns, power_ref, mixed_ref, scale_ref):
    qkv_t, out_t, up_t, down_t = weights
    column = lambda which: both(columns[layer, which])
    xhat, unused = norm_parts(hidden)
    normed = (xhat * column(GAIN_ONE) + column(SHIFT_ONE)).astype(BF16)
    yield
    projected = dot(qkv_t[layer], normed)
    yield
    query = (projected[:WIDTH] + column(Q_BIAS)).astype(BF16)
    keys = projected[WIDTH : 2 * WIDTH].astype(BF16)
    values = (projected[2 * WIDTH :] + column(V_BIAS)).astype(BF16)
    yield from attention_forward(query, keys, values, segments, masks, power_ref, mixed_ref, scale_ref)
    mixed = mixed_ref[...].astype(BF16)
    middle = hidden + (dot(out_t[layer], mixed) + column(OUT_BIAS))
    yield
    xhat_two, unused = norm_parts(middle)
    normed_two = (xhat_two * column(GAIN_TWO) + column(SHIFT_TWO)).astype(BF16)
    yield
    inner = dot(up_t[layer], normed_two)
    yield
    logit = inner[FF : FF + 1]
    inner = inner[:FF] + jnp.concatenate([column(UP_LOW), column(UP_HIGH)], axis=0)
    gate = jax.nn.sigmoid(logit)
    parts = []
    for start in range(0, FF, CHUNK):
        gated = inner[start : start + CHUNK] * gate
        power = jnp.tanh(gated * (GELU_A + (GELU_A * GELU_B) * (gated * gated)))
        parts.append((gated * (0.5 + 0.5 * power)).astype(BF16))
        yield
    active = jnp.concatenate(parts, axis=0)
    output = middle + (dot(down_t[layer], active) + column(DOWN_BIAS))
    return output, (normed, query, keys, values, mixed, middle, normed_two, inner, logit)


def norm_backward(gradient, xhat, scale, gain):
    inner = gradient * gain
    first = jnp.sum(inner, axis=0, keepdims=True) * (1.0 / WIDTH)
    second = jnp.sum(inner * xhat, axis=0, keepdims=True) * (1.0 / WIDTH)
    return scale * (inner - first - xhat * second)


def backward_unit(block, values_rows, query_variants, grad_variants, keys, deltas, power_ref, results, dq_ref):
    first, last = WINDOWS[block]
    query_blocks = [head_block(query_variants, block, group) for group in range(2)]
    grad_blocks = [head_block(grad_variants, block, group) for group in range(2)]
    products = [
        dot(values_rows[group][first:last], with_extra(grad_blocks[group], deltas[block][group]))
        for group in range(2)
    ]
    yield
    powers, grad_scores = [], []
    for group in range(2):
        start = PLACES[block][group]
        powers.append(power_ref[start : start + last - first])
        grad_scores.append((powers[group].astype(F32) * products[group]).astype(BF16))
        yield
    mixed = [
        dot(keys[QUARTER * group : QUARTER * group + QUARTER, first:last], grad_scores[group]) for group in range(2)
    ]

    def together_rows(blocks):
        gap = zeros(QUARTER)
        low = jnp.concatenate([blocks[0], gap], axis=0)
        high = jnp.concatenate([gap, blocks[1]], axis=0)
        return jnp.concatenate([low, high], axis=1)

    grad_keys = dot(jnp.concatenate(grad_scores, axis=1), together_rows(query_blocks).T)
    grad_values = dot(jnp.concatenate(powers, axis=1), together_rows(grad_blocks).T)
    results[block] = (grad_keys, grad_values, mixed)
    yield
    if block % 2 == 0:
        return
    lanes = slice((block // 2) * HALF, (block // 2 + 1) * HALF)
    for group in range(2):
        even, odd = results[block - 1][2][group], mixed[group]
        for head in range(4):
            tile = slice((head // 2) * HALF, (head // 2 + 1) * HALF)
            rows = slice(16 * head, 16 * head + 16)
            place = QUARTER * group + 16 * head
            dq_ref[place : place + 16, lanes] = join_blocks(even[rows, tile], odd[rows, tile], head)


def attention_backward(query, keys, values, mixed, scale, grad_mixed, masks, power_ref, dq_ref):
    factors = [scale[8 * head : 8 * head + 8] for head in range(HEADS)]
    grad = (grad_mixed * jnp.concatenate([row for factor in factors for row in (factor, factor)], axis=0)).astype(BF16)
    product = grad.astype(F32) * mixed.astype(F32)
    delta = jnp.concatenate(
        [jnp.sum(product[16 * head : 16 * head + 16], axis=0, keepdims=True) for head in range(HEADS)], axis=0
    )
    yield
    parts = [part.astype(F32) for part in split_three(-delta)]
    gap = jnp.zeros((4, LEN), F32)
    extras = [
        jnp.concatenate([part[4 * group : 4 * group + 4] for part in parts] + [gap], axis=0).astype(BF16)
        for group in range(2)
    ]
    deltas = [[spread_rows(extras[group], masks, block) for group in range(2)] for block in range(4)]
    query_variants = halves_of(query, masks)
    grad_variants = halves_of(grad, masks)
    rows = token_rows(values, ones(16))
    yield
    results = {}
    yield from skewed(
        backward_unit(block, rows, query_variants, grad_variants, keys, deltas, power_ref, results, dq_ref)
        for block in range(4)
    )

    def collect(which):
        parts = [results[block][which] for block in range(4)]
        return jnp.concatenate(
            [
                parts[0][:64] + parts[1][:64],
                parts[0][64:] + parts[1][64:128] + parts[2][:64],
                parts[1][128:] + parts[2][64:128] + parts[3][:64],
                parts[2][128:] + parts[3][64:],
            ],
            axis=0,
        ).astype(BF16)

    return (dq_ref[...] * 0.25).astype(BF16), collect(0), collect(1)


def backward_layer(
    layer, gradient, hidden, masks, kept, power_ref, scale_ref, raw, columns, totals, dq_ref
):
    w_qkv, w_out, w_up, w_down = raw
    normed, query, keys, values, mixed, middle, normed_two, inner, logit = kept
    qkv_total, out_total, up_total, down_total, sums = totals
    column = lambda which: both(columns[layer, which])
    branch = gradient.astype(BF16)
    sums[S_DOWN] += fold(branch.astype(F32))
    grad_active = dot(w_down[layer], branch)
    yield
    gate = jax.nn.sigmoid(logit)
    actives, inners = [], []
    logit_sum = jnp.zeros((1, LEN), F32)
    for start in range(0, FF, CHUNK):
        rows = slice(start, start + CHUNK)
        gated = inner[rows] * gate
        square = gated * gated
        power = jnp.tanh(gated * (GELU_A + (GELU_A * GELU_B) * square))
        half_up = 0.5 + 0.5 * power
        active = gated * half_up
        slope = half_up + (active * (1.0 - power)) * (GELU_A + (3.0 * GELU_A * GELU_B) * square)
        grad_gated = grad_active[rows].astype(BF16).astype(F32) * slope
        logit_sum = logit_sum + jnp.sum(grad_gated * inner[rows], axis=0, keepdims=True)
        actives.append(active.astype(BF16))
        inners.append((grad_gated * gate).astype(BF16))
        yield
    grad_logit = logit_sum * (gate * (1.0 - gate))
    active = jnp.concatenate(actives, axis=0)
    grad_inner = jnp.concatenate(inners, axis=0)
    grad_two = dot(w_up[layer], grad_inner) + column(GATE) * grad_logit
    down_total[...] += dot(branch, active.T)
    up_total[...] += dot(jnp.concatenate([normed_two, ones(16)], axis=0), grad_inner.T)
    sums[S_GATE] += fold(normed_two.astype(F32) * grad_logit)
    yield
    xhat, scale = norm_parts(middle)
    sums[S_GAIN_TWO] += fold(grad_two * xhat)
    sums[S_SHIFT_TWO] += fold(grad_two)
    grad_middle = gradient + norm_backward(grad_two, xhat, scale, column(GAIN_TWO))
    attended = grad_middle.astype(BF16)
    yield
    grad_mixed = dot(w_out[layer], attended)
    out_total[...] += dot(jnp.concatenate([mixed, ones(16)], axis=0), attended.T)
    yield
    grad_query, grad_keys, grad_values = yield from attention_backward(
        query, keys, values, mixed, scale_ref[...], grad_mixed, masks, power_ref, dq_ref
    )
    yield
    grad_rows = jnp.concatenate([grad_query.T, grad_keys, grad_values], axis=1)
    qkv_total[...] += dot(jnp.concatenate([normed, ones(16)], axis=0), grad_rows)
    grad_one = dot(w_qkv[layer], jnp.concatenate([grad_query, grad_keys.T, grad_values.T], axis=0))
    yield
    xhat, scale = norm_parts(hidden)
    sums[S_GAIN_ONE] += fold(grad_one * xhat)
    sums[S_SHIFT_ONE] += fold(grad_one)
    return grad_middle + norm_backward(grad_one, xhat, scale, column(GAIN_ONE))


def spread(row):
    return jnp.broadcast_to(row, (WIDTH, WIDTH)).T


def fill_columns(layer, columns, gains, shifts, qv_bias, out_bias, w_gate, up_bias, down_bias):
    columns[layer, GAIN_ONE] = spread(gains[layer, 0:1])
    columns[layer, GAIN_TWO] = spread(gains[layer, 1:2])
    columns[layer, SHIFT_ONE] = spread(shifts[layer, 0:1])
    columns[layer, SHIFT_TWO] = spread(shifts[layer, 1:2])
    columns[layer, OUT_BIAS] = spread(out_bias[layer : layer + 1])
    columns[layer, DOWN_BIAS] = spread(down_bias[layer : layer + 1])
    columns[layer, Q_BIAS] = spread(qv_bias[layer : layer + 1, :WIDTH]) * 0.25
    columns[layer, V_BIAS] = spread(qv_bias[layer : layer + 1, WIDTH:])
    columns[layer, GATE] = spread(w_gate[layer : layer + 1].astype(F32))
    columns[layer, UP_LOW] = spread(up_bias[layer : layer + 1, :WIDTH])
    columns[layer, UP_HIGH] = spread(up_bias[layer : layer + 1, WIDTH:])


def clear_totals(totals):
    for ref in totals:
        ref[...] = jnp.zeros_like(ref)


def write_totals(totals, grads_ref):
    qkv_total, out_total, up_total, down_total, sums = totals
    for part in range(3):
        rows = slice(R_QKV + part * WIDTH, R_QKV + (part + 1) * WIDTH)
        grads_ref[rows] = qkv_total[:WIDTH, part * WIDTH : (part + 1) * WIDTH]
    grads_ref[R_OUT : R_OUT + WIDTH] = out_total[:WIDTH]
    for part in range(2):
        lanes = slice(part * WIDTH, (part + 1) * WIDTH)
        grads_ref[R_UP + part * WIDTH : R_UP + (part + 1) * WIDTH] = up_total[:WIDTH, lanes]
        grads_ref[R_DOWN + part * WIDTH : R_DOWN + (part + 1) * WIDTH] = down_total[:, lanes].T
    rows = [jnp.sum(sums[which].T, axis=0, keepdims=True) for which in range(SUMS)]
    rows.append(out_total[WIDTH : WIDTH + 1])
    rows.extend(qkv_total[WIDTH : WIDTH + 1, part * WIDTH : (part + 1) * WIDTH] for part in range(3))
    rows.extend(up_total[WIDTH : WIDTH + 1, part * WIDTH : (part + 1) * WIDTH] for part in range(2))
    rows.append(jnp.zeros((ROWS - R_SMALL - len(rows), WIDTH), F32))
    grads_ref[R_SMALL:ROWS] = jnp.concatenate(rows, axis=0)


def kernel(
    per_step, steps,
    x_ref, seg_ref, cot_ref, gains, shifts, w_qkv, qv_bias, w_out, out_bias, w_gate, w_up, up_bias, w_down, down_bias,
    result_ref, grad_inputs_ref, grads_ref,
    columns, qkv_t, out_t, up_t, down_t, mixed_scratch, dq_ref, power_last, scale_last,
    grad_kept, normed_kept, qkv_kept, mixed_kept, scale_kept, middle_kept, normed_two_kept, inner_kept, logit_kept,
    power_kept, *totals,
):
    step = pl.program_id(0)
    totals_zero, totals_one = totals[: len(totals) // 2], totals[len(totals) // 2 :]

    @pl.when(step == 0)
    def start():
        clear_totals(totals)
        for layer in range(LAYERS):
            fill_columns(layer, columns, gains, shifts, qv_bias, out_bias, w_gate, up_bias, down_bias)
            qkv_t[layer, :WIDTH] = (w_qkv[layer][:, :WIDTH] * jnp.asarray(0.25, BF16)).T
            qkv_t[layer, WIDTH:] = w_qkv[layer][:, WIDTH:].T
            out_t[layer] = w_out[layer].T
            up_t[layer, :FF] = w_up[layer].T
            up_t[layer, FF:] = jnp.concatenate(
                [w_gate[layer : layer + 1].astype(F32), jnp.zeros((15, WIDTH), F32)], axis=0
            ).astype(BF16)
            down_t[layer] = w_down[layer].T

    masks = make_masks()
    weights = (qkv_t, out_t, up_t, down_t)
    raw = (w_qkv, w_out, w_up, w_down)

    def upward(item):
        tokens = slice(item * LEN, (item + 1) * LEN)
        place = step * per_step + item
        segments = segment_masks(seg_ref[0, item : item + 1])
        hidden = x_ref[tokens].astype(F32).T
        middle_hidden, kept = yield from forward_layer(
            0, hidden, segments, masks, weights, columns, power_kept.at[place], mixed_scratch.at[item],
            scale_kept.at[place],
        )
        normed, query, keys, values, mixed, middle, normed_two, inner, logit = kept
        normed_kept[place] = normed
        qkv_kept[place, :WIDTH] = query
        qkv_kept[place, WIDTH : 2 * WIDTH] = keys
        qkv_kept[place, 2 * WIDTH :] = values
        mixed_kept[place] = mixed
        middle_kept[place] = middle
        normed_two_kept[place] = normed_two
        inner_kept[place] = inner
        logit_kept[place] = jnp.broadcast_to(logit, (8, LEN))
        output, kept = yield from forward_layer(
            1, middle_hidden, segments, masks, weights, columns, power_last.at[item], mixed_scratch.at[item],
            scale_last.at[item],
        )
        result_ref[tokens] = output.T.astype(BF16)
        gradient = cot_ref[tokens].astype(F32).T
        grad_kept[place] = yield from backward_layer(
            1, gradient, middle_hidden, masks, kept, power_last.at[item], scale_last.at[item], raw, columns,
            totals_one, dq_ref.at[item],
        )

    def downward(item):
        tokens = slice(item * LEN, (item + 1) * LEN)
        place = (step - steps) * per_step + item
        hidden = x_ref[tokens].astype(F32).T
        kept = (
            normed_kept[place], qkv_kept[place, :WIDTH], qkv_kept[place, WIDTH : 2 * WIDTH],
            qkv_kept[place, 2 * WIDTH :], mixed_kept[place], middle_kept[place], normed_two_kept[place],
            inner_kept[place], logit_kept[place, 0:1],
        )
        gradient = yield from backward_layer(
            0, grad_kept[place], hidden, masks, kept, power_kept.at[place], scale_kept.at[place], raw, columns,
            totals_zero, dq_ref.at[item],
        )
        grad_inputs_ref[tokens] = gradient.T

    @pl.when(step < steps)
    def first_half():
        together([upward(item) for item in range(per_step)])

    @pl.when(step >= steps)
    def second_half():
        together([downward(item) for item in range(per_step)])

    @pl.when(step == 2 * steps - 1)
    def finish():
        write_totals(totals_zero, grads_ref.at[0])
        write_totals(totals_one, grads_ref.at[1])


def totals_scratch():
    return [
        pltpu.VMEM((WIDTH + 16, 3 * WIDTH), F32),
        pltpu.VMEM((WIDTH + 16, WIDTH), F32),
        pltpu.VMEM((WIDTH + 16, FF), F32),
        pltpu.VMEM((WIDTH, FF), F32),
        pltpu.VMEM((SUMS, WIDTH, WIDTH), F32),
    ]


def local_part(inputs, segment_ids, cotangent, *parameters, per_step=4):
    seqs = segment_ids.shape[0]
    per_step = min(per_step, seqs)
    steps = seqs // per_step
    segments = segment_ids.reshape(steps, per_step, LEN)
    rows = (per_step * LEN, WIDTH)

    def whole(array):
        zero = (0,) * array.ndim
        return pl.BlockSpec(array.shape, lambda i: zero)

    def kept(rows, dtype, count=seqs):
        return pltpu.VMEM((count, rows, LEN), dtype)

    return pl.pallas_call(
        lambda *refs: kernel(per_step, steps, *refs),
        grid=(2 * steps,),
        in_specs=[
            pl.BlockSpec(rows, lambda i: (i % steps, 0)),
            pl.BlockSpec((1, per_step, LEN), lambda i: (i % steps, 0, 0)),
            pl.BlockSpec(rows, lambda i: (jnp.minimum(i, steps - 1), 0)),
        ]
        + [whole(entry) for entry in parameters],
        out_specs=[
            pl.BlockSpec(rows, lambda i: (jnp.minimum(i, steps - 1), 0)),
            pl.BlockSpec(rows, lambda i: (jnp.maximum(i - steps, 0), 0)),
            pl.BlockSpec((LAYERS, ROWS, WIDTH), lambda i: (0, 0, 0)),
        ],
        out_shape=[
            jax.ShapeDtypeStruct(inputs.shape, BF16),
            jax.ShapeDtypeStruct(inputs.shape, F32),
            jax.ShapeDtypeStruct((LAYERS, ROWS, WIDTH), F32),
        ],
        scratch_shapes=[
            pltpu.VMEM((LAYERS, COLUMNS, WIDTH, WIDTH), F32),
            pltpu.VMEM((LAYERS, 3 * WIDTH, WIDTH), BF16),
            pltpu.VMEM((LAYERS, WIDTH, WIDTH), BF16),
            pltpu.VMEM((LAYERS, FF + 16, WIDTH), BF16),
            pltpu.VMEM((LAYERS, WIDTH, FF), BF16),
            kept(WIDTH, F32, per_step),
            kept(WIDTH, F32, per_step),
            kept(POWER_ROWS, BF16, per_step),
            kept(8 * HEADS, F32, per_step),
            kept(WIDTH, F32),
            kept(WIDTH, BF16),
            kept(3 * WIDTH, BF16),
            kept(WIDTH, BF16),
            kept(8 * HEADS, F32),
            kept(WIDTH, F32),
            kept(WIDTH, BF16),
            kept(FF, F32),
            kept(8, F32),
            kept(POWER_ROWS, BF16),
        ]
        + totals_scratch()
        + totals_scratch(),
        compiler_params=pltpu.CompilerParams(vmem_limit_bytes=60 * 1024 * 1024),
        name="layers",
    )(inputs, segments, cotangent, *parameters)


def unpack(grads):
    small = grads[:, R_SMALL:]
    gains = jnp.stack([small[:, S_GAIN_ONE], small[:, S_GAIN_TWO]], axis=1)
    shifts = jnp.stack([small[:, S_SHIFT_ONE], small[:, S_SHIFT_TWO]], axis=1)
    qkv = jnp.concatenate([grads[:, R_QKV + i * WIDTH : R_QKV + (i + 1) * WIDTH] for i in range(3)], axis=2)
    up = jnp.concatenate([grads[:, R_UP + i * WIDTH : R_UP + (i + 1) * WIDTH] for i in range(2)], axis=2)
    return (
        gains,
        shifts,
        qkv,
        jnp.concatenate([small[:, S_Q], small[:, S_V]], axis=1),
        grads[:, R_OUT : R_OUT + WIDTH],
        small[:, S_OUT],
        small[:, S_GATE],
        up,
        jnp.concatenate([small[:, S_UP_LOW], small[:, S_UP_HIGH]], axis=1),
        grads[:, R_DOWN : R_DOWN + FF],
        small[:, S_DOWN],
    )


def all_sum(grads, size):
    me = lax.axis_index("seq")
    bits = size.bit_length() - 1

    def swap(value, bit):
        return lax.ppermute(value, "seq", [(i, i ^ (1 << bit)) for i in range(size)])

    halves = (grads[0], grads[1])
    sides = []
    for bit in range(bits):
        side = (me >> bit) & 1
        if bit >= 3:
            current = current + swap(current, bit)
            continue
        sides.append(side)
        mine = jnp.where(side == 0, halves[0], halves[1])
        others = jnp.where(side == 0, halves[1], halves[0])
        current = mine + swap(others, bit)
        middle = current.shape[0] // 2
        halves = (current[:middle], current[middle:])
    for bit in reversed(range(min(bits, 3))):
        others = swap(current, bit)
        first = jnp.where(sides[bit] == 0, current, others)
        second = jnp.where(sides[bit] == 0, others, current)
        current = jnp.concatenate([first, second], axis=0)
    return current.reshape(LAYERS, ROWS, WIDTH)


def body(size, *arguments):
    result, grad_inputs, grads = local_part(*arguments)
    if size & (size - 1) or size < 2:
        grads = lax.psum(grads, "seq")
    else:
        grads = all_sum(grads, size)
    return (result, grad_inputs) + unpack(grads)


def solution(mesh):
    rows = P("seq", None)
    return jax.shard_map(
        lambda *arguments: body(mesh.shape["seq"], *arguments),
        mesh=mesh,
        in_specs=(rows, rows, rows) + (P(),) * 11,
        out_specs=(rows, rows) + (P(),) * 11,
        check_vma=False,
    )
```

time: 128 us -> 116 us (0.906)
  Pallas kernels: 74.5 us -> 63.7 us
    pallas_call x2 -> x1, Pallas kernels: 74.5 us -> 63.7 us  [local_part(): pl.pallas_call(lambda *refs: kernel(per_step, steps, *refs), grid=(2 * st...]
    select_n x3, other arithmetic: 0.12 us -> 1.41 us  [all_sum(): others = jnp.where(side == 0, halves[1], halves[0])]
where the time goes in v1:
time: 116 us
  Pallas kernels  63.7 us (55%)
  waiting for transfers between devices  29.8 us (26%)
  starting transfers between devices  13.5 us (12%)
  other arithmetic  4.53 us (4%)
  local copies, waits for them, and re-layouts  3.35 us (3%)
    pallas_call x1, Pallas kernels, local_part(): pl.pallas_call(lambda *refs: kernel(per_step, steps, *refs), grid=(2 * st...  63.7 us
    ppermute x8, waiting for transfers between devices, swap(): return lax.ppermute(value, 'seq', [(i, i ^ 1 << bit) for i in range(size)])  29.8 us
    ppermute x8, starting transfers between devices, swap(): return lax.ppermute(value, 'seq', [(i, i ^ 1 << bit) for i in range(size)])  13.5 us
  transfers between devices with their start and end apart: 8, of which 8 were waited for; matrix products, arithmetic and copies ran while one was open for 0% of the time, Pallas kernels for 0%

profile of v1, /device:TPU:0, one launch (start us, length us, event | category | flops | bytes accessed | tf_op | source)
XLA Modules:
  0.0 115.6 jit_solution(15609244456948589061)
XLA Ops:
  0.7 1.3 %reshape.36.refs_1_ = s32[4,4,256]{2,1,0:T(4,128)} reshape(s32[16,256]{1,0:T(8,128)} %param.15) | data formatting | bytes 32768 | tf_op jit(solution)/shard_map/reshape | solution.py:535
  2.0 63.7 %layers.1 = (bf16[4096,128]{1,0:T(8,128)(2,1)}, f32[4096,128]{1,0:T(8,128)}, f32[2,1056,128]{2,1,0:T(8,128)}) custom-call(bf16[4096,128]{1,0:T(8,128)(2,1)} %refs_0_.1, s32[4,4,256]{2,1,0:T(4,128)} %reshape.36.refs_1_, bf16[4096,128]{1,0:T(8,128)(2,1)} %refs_2_.1, f32[2,2,128]{2,1,0:T(2,128)} %refs_3_.1, f32[2,2,128]{2,1,0:T(2,128)} %refs_4_.1, ...), custom_call_target="tpu_custom_call" | custom-call | tf_op jit(solution)/shard_map/layers/pallas_call | solution.py:545
  65.7 0.0 copy-start
  65.7 1.4 %select_bitcast_fusion = f32[1056,128]{1,0:T(8,128)S(1)} fusion(f32[2,1056,128]{2,1,0:T(8,128)} %get-tuple-element.18, pred[]{:T(512)S(6)} %eq.6), kind=kLoop, calls=%fused_computation.3 | loop fusion | flops 135168 | bytes 1622017 | tf_op jit(solution)/shard_map/jit(_where)/select_n | solution.py:629
  67.1 0.5 collective-permute-start
  67.6 1.6 %collective-permute-done = f32[1056,128]{1,0:T(8,128)S(1)} collective-permute-done((f32[1056,128]{1,0:T(8,128)S(1)}, f32[1056,128]{1,0:T(8,128)S(1)}, u32[]{:S(2)}, u32[]{:S(2)}) %collective-permute-start) | collective-permute-done | bytes 540704 | tf_op jit(solution)/shard_map/ppermute | solution.py:618
  69.2 0.0 copy-done
  69.2 0.1 bitcast_add_fusion
  69.3 2.9 %collective-permute-start.1 = (f32[528,128]{1,0:T(8,128)S(1)}, f32[528,128]{1,0:T(8,128)S(1)}, u32[]{:S(2)}, u32[]{:S(2)}) collective-permute-start(f32[528,128]{1,0:T(8,128)S(1)} %slice_select_fusion), channel_id=1, source_target_pairs={{0,2},{1,3},{2,0},{3,1},{4,6},{5,7},{6,4},{7,5},{8,10},{9,11},{10,... | collective-permute-start | bytes 811016 | tf_op jit(solution)/shard_map/ppermute | solution.py:618
  72.2 6.8 %collective-permute-done.1 = f32[528,128]{1,0:T(8,128)S(1)} collective-permute-done((f32[528,128]{1,0:T(8,128)S(1)}, f32[528,128]{1,0:T(8,128)S(1)}, u32[]{:S(2)}, u32[]{:S(2)}) %collective-permute-start.1) | collective-permute-done | bytes 270368 | tf_op jit(solution)/shard_map/ppermute | solution.py:618
  79.1 1.8 %collective-permute-start.2 = (f32[264,128]{1,0:T(8,128)S(1)}, f32[264,128]{1,0:T(8,128)S(1)}, u32[]{:S(2)}, u32[]{:S(2)}) collective-permute-start(f32[264,128]{1,0:T(8,128)S(1)} %slice_select_fusion.1), channel_id=1, source_target_pairs={{0,4},{1,5},{2,6},{3,7},{4,0},{5,1},{6,2},{7,3},{8,12},{9,13},{10,... | collective-permute-start | bytes 405512 | tf_op jit(solution)/shard_map/ppermute | solution.py:618
  80.9 3.4 %collective-permute-done.2 = f32[264,128]{1,0:T(8,128)S(1)} collective-permute-done((f32[264,128]{1,0:T(8,128)S(1)}, f32[264,128]{1,0:T(8,128)S(1)}, u32[]{:S(2)}, u32[]{:S(2)}) %collective-permute-start.2) | collective-permute-done | bytes 135200 | tf_op jit(solution)/shard_map/ppermute | solution.py:618
  84.3 1.8 %collective-permute-start.3 = (f32[264,128]{1,0:T(8,128)S(1)}, f32[264,128]{1,0:T(8,128)S(1)}, u32[]{:S(2)}, u32[]{:S(2)}) collective-permute-start(f32[264,128]{1,0:T(8,128)S(1)} %select_add_fusion.1), channel_id=1, source_target_pairs={{0,8},{1,9},{2,10},{3,11},{4,12},{5,13},{6,14},{7,15},{8,0},{9,1},... | collective-permute-start | bytes 405512 | tf_op jit(solution)/shard_map/ppermute | solution.py:618
  86.1 3.3 %collective-permute-done.3 = f32[264,128]{1,0:T(8,128)S(1)} collective-permute-done((f32[264,128]{1,0:T(8,128)S(1)}, f32[264,128]{1,0:T(8,128)S(1)}, u32[]{:S(2)}, u32[]{:S(2)}) %collective-permute-start.3) | collective-permute-done | bytes 135200 | tf_op jit(solution)/shard_map/ppermute | solution.py:618
  89.4 3.2 %collective-permute-start.4 = (f32[264,128]{1,0:T(8,128)S(1)}, f32[264,128]{1,0:T(8,128)S(1)}, u32[]{:S(2)}, u32[]{:S(2)}) collective-permute-start(f32[264,128]{1,0:T(8,128)S(1)} %add.18), channel_id=1, source_target_pairs={{0,16},{1,17},{2,18},{3,19},{4,20},{5,21},{6,22},{7,23},{8,24},{9,... | collective-permute-start | bytes 405512 | tf_op jit(solution)/shard_map/ppermute | solution.py:618
  92.6 4.4 %collective-permute-done.4 = f32[264,128]{1,0:T(8,128)S(1)} collective-permute-done((f32[264,128]{1,0:T(8,128)S(1)}, f32[264,128]{1,0:T(8,128)S(1)}, u32[]{:S(2)}, u32[]{:S(2)}) %collective-permute-start.4) | collective-permute-done | bytes 135200 | tf_op jit(solution)/shard_map/ppermute | solution.py:618
  97.1 1.6 %collective-permute-start.5 = (f32[264,128]{1,0:T(8,128)S(1)}, f32[264,128]{1,0:T(8,128)S(1)}, u32[]{:S(2)}, u32[]{:S(2)}) collective-permute-start(f32[264,128]{1,0:T(8,128)S(1)} %add.19), channel_id=1, source_target_pairs={{0,4},{1,5},{2,6},{3,7},{4,0},{5,1},{6,2},{7,3},{8,12},{9,13},{10,... | collective-permute-start | bytes 405512 | tf_op jit(solution)/shard_map/ppermute | solution.py:618
  98.6 3.5 %collective-permute-done.5 = f32[264,128]{1,0:T(8,128)S(1)} collective-permute-done((f32[264,128]{1,0:T(8,128)S(1)}, f32[264,128]{1,0:T(8,128)S(1)}, u32[]{:S(2)}, u32[]{:S(2)}) %collective-permute-start.5) | collective-permute-done | bytes 135200 | tf_op jit(solution)/shard_map/ppermute | solution.py:618
  102.2 1.6 %collective-permute-start.6 = (f32[528,128]{1,0:T(8,128)S(1)}, f32[528,128]{1,0:T(8,128)S(1)}, u32[]{:S(2)}, u32[]{:S(2)}) collective-permute-start(f32[528,128]{1,0:T(8,128)S(1)} %pad_maximum_fusion.3), channel_id=1, source_target_pairs={{0,2},{1,3},{2,0},{3,1},{4,6},{5,7},{6,4},{7,5},{8,10},{9,11},{10,... | collective-permute-start | bytes 811016 | tf_op jit(solution)/shard_map/ppermute | solution.py:618
  103.7 5.0 %collective-permute-done.6 = f32[528,128]{1,0:T(8,128)S(1)} collective-permute-done((f32[528,128]{1,0:T(8,128)S(1)}, f32[528,128]{1,0:T(8,128)S(1)}, u32[]{:S(2)}, u32[]{:S(2)}) %collective-permute-start.6) | collective-permute-done | bytes 270368 | tf_op jit(solution)/shard_map/ppermute | solution.py:618
  108.8 0.1 collective-permute-start.7
  108.9 1.9 %collective-permute-done.7 = f32[1056,128]{1,0:T(8,128)S(1)} collective-permute-done((f32[1056,128]{1,0:T(8,128)S(1)}, f32[1056,128]{1,0:T(8,128)S(1)}, u32[]{:S(2)}, u32[]{:S(2)}) %collective-permute-start.7) | collective-permute-done | bytes 540704 | tf_op jit(solution)/shard_map/ppermute | solution.py:618
  110.8 0.1 broadcast_select_fusion.1
  110.9 0.1 pad_maximum_fusion
  111.0 0.6 fusion
  111.5 0.7 slice.128
  112.3 0.7 fusion.1
  113.0 0.7 pad_maximum_fusion.4
  113.7 0.8 pad_maximum_fusion.2
  114.5 0.6 pad_maximum_fusion.7
  115.0 0.6 pad_maximum_fusion.5
  (10 shorter events, 0.3 us)
Async XLA Ops:
  65.7 3.5 %copy-start = (f32[2,1056,128]{2,1,0:T(8,128)S(1)}, f32[2,1056,128]{2,1,0:T(8,128)}, u32[]{:S(2)}) copy-start(f32[2,1056,128]{2,1,0:T(8,128)} %get-tuple-element.18) | copy-start | bytes 3244036
  67.1 2.1 %collective-permute-start = (f32[1056,128]{1,0:T(8,128)S(1)}, f32[1056,128]{1,0:T(8,128)S(1)}, u32[]{:S(2)}, u32[]{:S(2)}) collective-permute-start(f32[1056,128]{1,0:T(8,128)S(1)} %select_bitcast_fusion), channel_id=1, source_target_pairs={{0,1},{1,0},{2,3},{3,2},{4,5},{5,4},{6,7},{7,6},{8,9},{9,8},{10,11... | collective-permute-start | bytes 1622024 | tf_op jit(solution)/shard_map/ppermute | solution.py:618
  69.3 9.7 %collective-permute-start.1 = (f32[528,128]{1,0:T(8,128)S(1)}, f32[528,128]{1,0:T(8,128)S(1)}, u32[]{:S(2)}, u32[]{:S(2)}) collective-permute-start(f32[528,128]{1,0:T(8,128)S(1)} %slice_select_fusion), channel_id=1, source_target_pairs={{0,2},{1,3},{2,0},{3,1},{4,6},{5,7},{6,4},{7,5},{8,10},{9,11},{10,... | collective-permute-start | bytes 811016 | tf_op jit(solution)/shard_map/ppermute | solution.py:618
  79.1 5.2 %collective-permute-start.2 = (f32[264,128]{1,0:T(8,128)S(1)}, f32[264,128]{1,0:T(8,128)S(1)}, u32[]{:S(2)}, u32[]{:S(2)}) collective-permute-start(f32[264,128]{1,0:T(8,128)S(1)} %slice_select_fusion.1), channel_id=1, source_target_pairs={{0,4},{1,5},{2,6},{3,7},{4,0},{5,1},{6,2},{7,3},{8,12},{9,13},{10,... | collective-permute-start | bytes 405512 | tf_op jit(solution)/shard_map/ppermute | solution.py:618
  84.3 5.1 %collective-permute-start.3 = (f32[264,128]{1,0:T(8,128)S(1)}, f32[264,128]{1,0:T(8,128)S(1)}, u32[]{:S(2)}, u32[]{:S(2)}) collective-permute-start(f32[264,128]{1,0:T(8,128)S(1)} %select_add_fusion.1), channel_id=1, source_target_pairs={{0,8},{1,9},{2,10},{3,11},{4,12},{5,13},{6,14},{7,15},{8,0},{9,1},... | collective-permute-start | bytes 405512 | tf_op jit(solution)/shard_map/ppermute | solution.py:618
  89.4 7.7 %collective-permute-start.4 = (f32[264,128]{1,0:T(8,128)S(1)}, f32[264,128]{1,0:T(8,128)S(1)}, u32[]{:S(2)}, u32[]{:S(2)}) collective-permute-start(f32[264,128]{1,0:T(8,128)S(1)} %add.18), channel_id=1, source_target_pairs={{0,16},{1,17},{2,18},{3,19},{4,20},{5,21},{6,22},{7,23},{8,24},{9,... | collective-permute-start | bytes 405512 | tf_op jit(solution)/shard_map/ppermute | solution.py:618
  97.1 5.1 %collective-permute-start.5 = (f32[264,128]{1,0:T(8,128)S(1)}, f32[264,128]{1,0:T(8,128)S(1)}, u32[]{:S(2)}, u32[]{:S(2)}) collective-permute-start(f32[264,128]{1,0:T(8,128)S(1)} %add.19), channel_id=1, source_target_pairs={{0,4},{1,5},{2,6},{3,7},{4,0},{5,1},{6,2},{7,3},{8,12},{9,13},{10,... | collective-permute-start | bytes 405512 | tf_op jit(solution)/shard_map/ppermute | solution.py:618
  102.2 6.5 %collective-permute-start.6 = (f32[528,128]{1,0:T(8,128)S(1)}, f32[528,128]{1,0:T(8,128)S(1)}, u32[]{:S(2)}, u32[]{:S(2)}) collective-permute-start(f32[528,128]{1,0:T(8,128)S(1)} %pad_maximum_fusion.3), channel_id=1, source_target_pairs={{0,2},{1,3},{2,0},{3,1},{4,6},{5,7},{6,4},{7,5},{8,10},{9,11},{10,... | collective-permute-start | bytes 811016 | tf_op jit(solution)/shard_map/ppermute | solution.py:618
  108.8 2.0 %collective-permute-start.7 = (f32[1056,128]{1,0:T(8,128)S(1)}, f32[1056,128]{1,0:T(8,128)S(1)}, u32[]{:S(2)}, u32[]{:S(2)}) collective-permute-start(f32[1056,128]{1,0:T(8,128)S(1)} %pad_maximum_fusion.1), channel_id=1, source_target_pairs={{0,1},{1,0},{2,3},{3,2},{4,5},{5,4},{6,7},{7,6},{8,9},{9,8},{10,11... | collective-permute-start | bytes 1622024 | tf_op jit(solution)/shard_map/ppermute | solution.py:618

commit v2 on v1

--- a/solution.py
+++ b/solution.py
@@ -221,8 +221,8 @@
     keys = projected[WIDTH : 2 * WIDTH].astype(BF16)
     values = (projected[2 * WIDTH :] + column(V_BIAS)).astype(BF16)
     yield from attention_forward(query, keys, values, segments, masks, power_ref, mixed_ref, scale_ref)
-    mixed = mixed_ref[...].astype(BF16)
-    middle = hidden + (dot(out_t[layer], mixed) + column(OUT_BIAS))
+    mixed = mixed_ref[...]
+    middle = hidden + (dot(out_t[layer], mixed.astype(BF16)) + column(OUT_BIAS))
     yield
     xhat_two, unused = norm_parts(middle)
     normed_two = (xhat_two * column(GAIN_TWO) + column(SHIFT_TWO)).astype(BF16)
@@ -294,7 +294,7 @@
 def attention_backward(query, keys, values, mixed, scale, grad_mixed, masks, power_ref, dq_ref):
     factors = [scale[8 * head : 8 * head + 8] for head in range(HEADS)]
     grad = (grad_mixed * jnp.concatenate([row for factor in factors for row in (factor, factor)], axis=0)).astype(BF16)
-    product = grad.astype(F32) * mixed.astype(F32)
+    product = grad.astype(F32) * mixed
     delta = jnp.concatenate(
         [jnp.sum(product[16 * head : 16 * head + 16], axis=0, keepdims=True) for head in range(HEADS)], axis=0
     )
@@ -373,7 +373,7 @@
     attended = grad_middle.astype(BF16)
     yield
     grad_mixed = dot(w_out[layer], attended)
-    out_total[...] += dot(jnp.concatenate([mixed, ones(16)], axis=0), attended.T)
+    out_total[...] += dot(jnp.concatenate([mixed.astype(BF16), ones(16)], axis=0), attended.T)
     yield
     grad_query, grad_keys, grad_values = yield from attention_backward(
         query, keys, values, mixed, scale_ref[...], grad_mixed, masks, power_ref, dq_ref
@@ -462,7 +462,7 @@
     def upward(item):
         tokens = slice(item * LEN, (item + 1) * LEN)
         place = step * per_step + item
-        segments = segment_masks(seg_ref[0, item : item + 1])
+        segments = segment_masks(seg_ref[pl.ds(place, 1)])
         hidden = x_ref[tokens].astype(F32).T
         middle_hidden, kept = yield from forward_layer(
             0, hidden, segments, masks, weights, columns, power_kept.at[place], mixed_scratch.at[item],
@@ -532,7 +532,6 @@
     seqs = segment_ids.shape[0]
     per_step = min(per_step, seqs)
     steps = seqs // per_step
-    segments = segment_ids.reshape(steps, per_step, LEN)
     rows = (per_step * LEN, WIDTH)
 
     def whole(array):
@@ -547,7 +546,7 @@
         grid=(2 * steps,),
         in_specs=[
             pl.BlockSpec(rows, lambda i: (i % steps, 0)),
-            pl.BlockSpec((1, per_step, LEN), lambda i: (i % steps, 0, 0)),
+            whole(segment_ids),
             pl.BlockSpec(rows, lambda i: (jnp.minimum(i, steps - 1), 0)),
         ]
         + [whole(entry) for entry in parameters],
@@ -574,7 +573,7 @@
             kept(WIDTH, F32),
             kept(WIDTH, BF16),
             kept(3 * WIDTH, BF16),
-            kept(WIDTH, BF16),
+            kept(WIDTH, F32),
             kept(8 * HEADS, F32),
             kept(WIDTH, F32),
             kept(WIDTH, BF16),
@@ -586,65 +585,87 @@
         + totals_scratch(),
         compiler_params=pltpu.CompilerParams(vmem_limit_bytes=60 * 1024 * 1024),
         name="layers",
-    )(inputs, segments, cotangent, *parameters)
-
-
-def unpack(grads):
-    small = grads[:, R_SMALL:]
-    gains = jnp.stack([small[:, S_GAIN_ONE], small[:, S_GAIN_TWO]], axis=1)
-    shifts = jnp.stack([small[:, S_SHIFT_ONE], small[:, S_SHIFT_TWO]], axis=1)
-    qkv = jnp.concatenate([grads[:, R_QKV + i * WIDTH : R_QKV + (i + 1) * WIDTH] for i in range(3)], axis=2)
-    up = jnp.concatenate([grads[:, R_UP + i * WIDTH : R_UP + (i + 1) * WIDTH] for i in range(2)], axis=2)
-    return (
-        gains,
-        shifts,
-        qkv,
-        jnp.concatenate([small[:, S_Q], small[:, S_V]], axis=1),
-        grads[:, R_OUT : R_OUT + WIDTH],
-        small[:, S_OUT],
-        small[:, S_GATE],
-        up,
-        jnp.concatenate([small[:, S_UP_LOW], small[:, S_UP_HIGH]], axis=1),
-        grads[:, R_DOWN : R_DOWN + FF],
-        small[:, S_DOWN],
-    )
+    )(inputs, segment_ids, cotangent, *parameters)
+
+
+def unpack_kernel(
+    where_ref, near_ref, far_ref,
+    gains_ref, shifts_ref, qkv_ref, qv_bias_ref, out_ref, out_bias_ref, gate_ref, up_ref, up_bias_ref, down_ref,
+    down_bias_ref,
+    grads,
+):
+    core, part = where_ref[0], where_ref[1]
+    quarter = ROWS // 4
+    for mask in range(4):
+        place = pl.ds(pl.multiple_of((part ^ mask) * quarter, 8), quarter)
+        rows = slice(mask * quarter, (mask + 1) * quarter)
+        grads[core, place] = near_ref[rows]
+        grads[1 - core, place] = far_ref[rows]
+    for layer in range(LAYERS):
+        for part in range(3):
+            lanes = slice(part * WIDTH, (part + 1) * WIDTH)
+            qkv_ref[layer, :, lanes] = grads[layer, R_QKV + part * WIDTH : R_QKV + (part + 1) * WIDTH]
+        out_ref[layer] = grads[layer, R_OUT : R_OUT + WIDTH]
+        for part in range(2):
+            lanes = slice(part * WIDTH, (part + 1) * WIDTH)
+            up_ref[layer, :, lanes] = grads[layer, R_UP + part * WIDTH : R_UP + (part + 1) * WIDTH]
+        down_ref[layer] = grads[layer, R_DOWN : R_DOWN + FF]
+        one = slice(layer, layer + 1)
+
+        def row(which):
+            return grads[layer, R_SMALL + which : R_SMALL + which + 1]
+
+        gains_ref[layer, 0:1], gains_ref[layer, 1:2] = row(S_GAIN_ONE), row(S_GAIN_TWO)
+        shifts_ref[layer, 0:1], shifts_ref[layer, 1:2] = row(S_SHIFT_ONE), row(S_SHIFT_TWO)
+        qv_bias_ref[one, :WIDTH], qv_bias_ref[one, WIDTH:] = row(S_Q), row(S_V)
+        out_bias_ref[one], gate_ref[one], down_bias_ref[one] = row(S_OUT), row(S_GATE), row(S_DOWN)
+        up_bias_ref[one, :WIDTH], up_bias_ref[one, WIDTH:] = row(S_UP_LOW), row(S_UP_HIGH)
+
+
+def unpack(where, near, far):
+    shapes = [
+        (LAYERS, 2, WIDTH), (LAYERS, 2, WIDTH), (LAYERS, WIDTH, 3 * WIDTH), (LAYERS, 2 * WIDTH), (LAYERS, WIDTH, WIDTH),
+        (LAYERS, WIDTH), (LAYERS, WIDTH), (LAYERS, WIDTH, FF), (LAYERS, FF), (LAYERS, FF, WIDTH), (LAYERS, WIDTH),
+    ]
+    return pl.pallas_call(
+        unpack_kernel,
+        in_specs=[pl.BlockSpec(memory_space=pltpu.SMEM), pl.BlockSpec(), pl.BlockSpec()],
+        out_shape=[jax.ShapeDtypeStruct(shape, F32) for shape in shapes],
+        scratch_shapes=[pltpu.VMEM((LAYERS, ROWS, WIDTH), F32)],
+        compiler_params=pltpu.CompilerParams(vmem_limit_bytes=16 * 1024 * 1024),
+        name="unpack",
+    )(where, near, far)
 
 
 def all_sum(grads, size):
     me = lax.axis_index("seq")
     bits = size.bit_length() - 1
-
-    def swap(value, bit):
-        return lax.ppermute(value, "seq", [(i, i ^ (1 << bit)) for i in range(size)])
-
-    halves = (grads[0], grads[1])
-    sides = []
-    for bit in range(bits):
-        side = (me >> bit) & 1
-        if bit >= 3:
-            current = current + swap(current, bit)
-            continue
-        sides.append(side)
-        mine = jnp.where(side == 0, halves[0], halves[1])
-        others = jnp.where(side == 0, halves[1], halves[0])
-        current = mine + swap(others, bit)
-        middle = current.shape[0] // 2
-        halves = (current[:middle], current[middle:])
-    for bit in reversed(range(min(bits, 3))):
-        others = swap(current, bit)
-        first = jnp.where(sides[bit] == 0, current, others)
-        second = jnp.where(sides[bit] == 0, others, current)
-        current = jnp.concatenate([first, second], axis=0)
-    return current.reshape(LAYERS, ROWS, WIDTH)
+    core, part = me & 1, (me >> 1) & 3
+
+    def swap(value, mask):
+        return lax.ppermute(value, "seq", [(i, i ^ mask) for i in range(size)])
+
+    def pick(value, index):
+        return lax.dynamic_index_in_dim(value, index, 0, keepdims=False)
+
+    layer = pick(grads, core) + swap(pick(grads, 1 - core), 1)
+    quarters = layer.reshape(4, ROWS // 4, WIDTH)
+    others = [swap(pick(quarters, part ^ mask), 2 * mask) for mask in (1, 2, 3)]
+    mine = pick(quarters, part) + others[0] + others[1] + others[2]
+    for bit in range(3, bits):
+        mine = mine + swap(mine, 1 << bit)
+    near = jnp.concatenate([mine] + [swap(mine, 2 * mask) for mask in (1, 2, 3)], axis=0)
+    return jnp.stack([core, part]).astype(jnp.int32), near, swap(near, 1)
 
 
 def body(size, *arguments):
     result, grad_inputs, grads = local_part(*arguments)
-    if size & (size - 1) or size < 2:
+    if size & (size - 1) or size < 8:
         grads = lax.psum(grads, "seq")
+        summed = (jnp.zeros((2,), jnp.int32), grads[0], grads[1])
     else:
-        grads = all_sum(grads, size)
-    return (result, grad_inputs) + unpack(grads)
+        summed = all_sum(grads, size)
+    return (result, grad_inputs) + tuple(unpack(*summed))
 
 
 def solution(mesh):

time: 116 us -> 103 us (0.89)
  waiting for transfers between devices: 29.8 us -> 22.8 us
  other arithmetic: 4.53 us -> 0.25 us
  local copies, waits for them, and re-layouts: 3.35 us -> 1.23 us
  Pallas kernels: 63.7 us -> 65.2 us
    ppermute x8 -> x10, waiting for transfers between devices: 29.8 us -> 22.8 us  [swap(): return lax.ppermute(value, 'seq', [(i, i ^ mask) for i in range(size)])]
    concatenate x6 -> x1, other arithmetic: 2.2 us -> 0.04 us  [all_sum(): jnp.concatenate([mine] + [swap(mine, 2 * mask) for mask in (1, 2, 3)], ax...]
    slice x3 -> x0, local copies, waits for them, and re-layouts: 2.01 us -> none  [the longest x1 0.72 us: unpack(): grads[:, R_DOWN:R_DOWN + FF]]
    pallas_call x0 -> x1, Pallas kernels: none -> 1.61 us  [unpack(): pl.pallas_call(unpack_kernel, in_specs=[pl.BlockSpec(memory_space=pltpu.S...]
    select_n x6 -> x0, other arithmetic: 1.55 us -> none  [the longest x3 1.41 us: all_sum(): others = jnp.where(side == 0, halves[1], halves[0])]
    reshape x1 -> x0, local copies, waits for them, and re-layouts: 1.33 us -> none  [local_part(): segments = segment_ids.reshape(steps, per_step, LEN)]
    squeeze x0 -> x2, local copies, waits for them, and re-layouts: none -> 1.22 us  [pick(): return lax.dynamic_index_in_dim(value, index, 0, keepdims=False)]
    ppermute x8 -> x10, starting transfers between devices: 13.5 us -> 12.9 us  [swap(): return lax.ppermute(value, 'seq', [(i, i ^ mask) for i in range(size)])]
  transfers between devices with their start and end apart: 8 -> 10, of which waited for: 8 -> 9; matrix products, arithmetic and copies ran while one was open for 0% -> 0% of each run, Pallas kernels for 0% -> 0%
where the time goes in v2:
time: 103 us
  Pallas kernels  65.2 us (63%)
  waiting for transfers between devices  22.8 us (22%)
  starting transfers between devices  12.9 us (13%)
  local copies, waits for them, and re-layouts  1.23 us (1%)
    pallas_call x1, Pallas kernels, local_part(): pl.pallas_call(lambda *refs: kernel(per_step, steps, *refs), grid=(2 * st...  63.6 us
    ppermute x10, waiting for transfers between devices, swap(): return lax.ppermute(value, 'seq', [(i, i ^ mask) for i in range(size)])  22.8 us
    ppermute x10, starting transfers between devices, swap(): return lax.ppermute(value, 'seq', [(i, i ^ mask) for i in range(size)])  12.9 us
  transfers between devices with their start and end apart: 10, of which 9 were waited for; matrix products, arithmetic and copies ran while one was open for 0% of the time, Pallas kernels for 0%

profile of v2, /device:TPU:0, one launch (start us, length us, event | category | flops | bytes accessed | tf_op | source)
XLA Modules:
  0.0 103.1 jit_solution(7708176131946666506)
XLA Ops:
  0.7 63.6 %layers.1 = (bf16[4096,128]{1,0:T(8,128)(2,1)}, f32[4096,128]{1,0:T(8,128)}, f32[2,1056,128]{2,1,0:T(8,128)}) custom-call(bf16[4096,128]{1,0:T(8,128)(2,1)} %refs_0_.1, s32[16,256]{1,0:T(8,128)} %refs_1_.1, bf16[4096,128]{1,0:T(8,128)(2,1)} %refs_2_.1, f32[2,2,128]{2,1,0:T(2,128)} %refs_3_.1, f32[2,2,128]{2,1,0:T(2,128)} %refs_4_.1, ...), custom_call_target="tpu_custom_call" | custom-call | tf_op jit(solution)/shard_map/layers/pallas_call | solution.py:544
  64.3 0.0 copy-start
  64.3 1.2 %dynamic-slice_bitcast_fusion = f32[1056,128]{1,0:T(8,128)S(1)} fusion(f32[2,1056,128]{2,1,0:T(8,128)} %get-tuple-element.29, s32[]{:T(128)S(6)} %select_n.21), kind=kLoop, calls=%fused_computation.2 | loop fusion | bytes 1081348 | tf_op jit(solution)/shard_map/jit(dynamic_index_in_dim)/squeeze | solution.py:649
  65.5 0.5 collective-permute-start
  66.0 1.6 %collective-permute-done = f32[1056,128]{1,0:T(8,128)S(1)} collective-permute-done((f32[1056,128]{1,0:T(8,128)S(1)}, f32[1056,128]{1,0:T(8,128)S(1)}, u32[]{:S(2)}, u32[]{:S(2)}) %collective-permute-start) | collective-permute-done | bytes 540704 | tf_op jit(solution)/shard_map/ppermute | solution.py:646
  67.6 0.0 copy-done
  67.6 0.1 bitcast_add_fusion
  67.7 2.9 %collective-permute-start.1 = (f32[264,128]{1,0:T(8,128)S(1)}, f32[264,128]{1,0:T(8,128)S(1)}, u32[]{:S(2)}, u32[]{:S(2)}) collective-permute-start(f32[264,128]{1,0:T(8,128)S(1)} %get-tuple-element.41), channel_id=1, source_target_pairs={{0,2},{1,3},{2,0},{3,1},{4,6},{5,7},{6,4},{7,5},{8,10},{9,11},{10,... | collective-permute-start | bytes 405512 | tf_op jit(solution)/shard_map/ppermute | solution.py:646
  70.6 1.5 %collective-permute-start.2 = (f32[264,128]{1,0:T(8,128)S(1)}, f32[264,128]{1,0:T(8,128)S(1)}, u32[]{:S(2)}, u32[]{:S(2)}) collective-permute-start(f32[264,128]{1,0:T(8,128)S(1)} %get-tuple-element.43), channel_id=1, source_target_pairs={{0,4},{1,5},{2,6},{3,7},{4,0},{5,1},{6,2},{7,3},{8,12},{9,13},{10,... | collective-permute-start | bytes 405512 | tf_op jit(solution)/shard_map/ppermute | solution.py:646
  72.1 0.0 collective-permute-start.3
  72.1 2.5 %collective-permute-done.1 = f32[264,128]{1,0:T(8,128)S(1)} collective-permute-done((f32[264,128]{1,0:T(8,128)S(1)}, f32[264,128]{1,0:T(8,128)S(1)}, u32[]{:S(2)}, u32[]{:S(2)}) %collective-permute-start.1) | collective-permute-done | bytes 135200 | tf_op jit(solution)/shard_map/ppermute | solution.py:646
  74.7 4.2 %collective-permute-done.2 = f32[264,128]{1,0:T(8,128)S(1)} collective-permute-done((f32[264,128]{1,0:T(8,128)S(1)}, f32[264,128]{1,0:T(8,128)S(1)}, u32[]{:S(2)}, u32[]{:S(2)}) %collective-permute-start.2) | collective-permute-done | bytes 135200 | tf_op jit(solution)/shard_map/ppermute | solution.py:646
  78.8 0.0 collective-permute-done.3
  78.9 1.6 %collective-permute-start.4 = (f32[264,128]{1,0:T(8,128)S(1)}, f32[264,128]{1,0:T(8,128)S(1)}, u32[]{:S(2)}, u32[]{:S(2)}) collective-permute-start(f32[264,128]{1,0:T(8,128)S(1)} %fusion.1), channel_id=1, source_target_pairs={{0,8},{1,9},{2,10},{3,11},{4,12},{5,13},{6,14},{7,15},{8,0},{9,1},... | collective-permute-start | bytes 405512 | tf_op jit(solution)/shard_map/ppermute | solution.py:646
  80.5 3.4 %collective-permute-done.4 = f32[264,128]{1,0:T(8,128)S(1)} collective-permute-done((f32[264,128]{1,0:T(8,128)S(1)}, f32[264,128]{1,0:T(8,128)S(1)}, u32[]{:S(2)}, u32[]{:S(2)}) %collective-permute-start.4) | collective-permute-done | bytes 135200 | tf_op jit(solution)/shard_map/ppermute | solution.py:646
  84.0 2.6 %collective-permute-start.5 = (f32[264,128]{1,0:T(8,128)S(1)}, f32[264,128]{1,0:T(8,128)S(1)}, u32[]{:S(2)}, u32[]{:S(2)}) collective-permute-start(f32[264,128]{1,0:T(8,128)S(1)} %add.49), channel_id=1, source_target_pairs={{0,16},{1,17},{2,18},{3,19},{4,20},{5,21},{6,22},{7,23},{8,24},{9,... | collective-permute-start | bytes 405512 | tf_op jit(solution)/shard_map/ppermute | solution.py:646
  86.6 4.8 %collective-permute-done.5 = f32[264,128]{1,0:T(8,128)S(1)} collective-permute-done((f32[264,128]{1,0:T(8,128)S(1)}, f32[264,128]{1,0:T(8,128)S(1)}, u32[]{:S(2)}, u32[]{:S(2)}) %collective-permute-start.5) | collective-permute-done | bytes 135200 | tf_op jit(solution)/shard_map/ppermute | solution.py:646
  91.4 1.4 %collective-permute-start.6 = (f32[264,128]{1,0:T(8,128)S(1)}, f32[264,128]{1,0:T(8,128)S(1)}, u32[]{:S(2)}, u32[]{:S(2)}) collective-permute-start(f32[264,128]{1,0:T(8,128)S(1)} %add.50), channel_id=1, source_target_pairs={{0,2},{1,3},{2,0},{3,1},{4,6},{5,7},{6,4},{7,5},{8,10},{9,11},{10,... | collective-permute-start | bytes 405512 | tf_op jit(solution)/shard_map/ppermute | solution.py:646
  92.8 0.7 collective-permute-start.7
  93.5 1.4 %collective-permute-start.8 = (f32[264,128]{1,0:T(8,128)S(1)}, f32[264,128]{1,0:T(8,128)S(1)}, u32[]{:S(2)}, u32[]{:S(2)}) collective-permute-start(f32[264,128]{1,0:T(8,128)S(1)} %add.50), channel_id=1, source_target_pairs={{0,6},{1,7},{2,4},{3,5},{4,2},{5,3},{6,0},{7,1},{8,14},{9,15},{10,... | collective-permute-start | bytes 405512 | tf_op jit(solution)/shard_map/ppermute | solution.py:646
  95.0 1.5 %collective-permute-done.6 = f32[264,128]{1,0:T(8,128)S(1)} collective-permute-done((f32[264,128]{1,0:T(8,128)S(1)}, f32[264,128]{1,0:T(8,128)S(1)}, u32[]{:S(2)}, u32[]{:S(2)}) %collective-permute-start.6) | collective-permute-done | bytes 135200 | tf_op jit(solution)/shard_map/ppermute | solution.py:646
  96.5 1.3 %collective-permute-done.7 = f32[264,128]{1,0:T(8,128)S(1)} collective-permute-done((f32[264,128]{1,0:T(8,128)S(1)}, f32[264,128]{1,0:T(8,128)S(1)}, u32[]{:S(2)}, u32[]{:S(2)}) %collective-permute-start.7) | collective-permute-done | bytes 135200 | tf_op jit(solution)/shard_map/ppermute | solution.py:646
  97.8 1.6 %collective-permute-done.8 = f32[264,128]{1,0:T(8,128)S(1)} collective-permute-done((f32[264,128]{1,0:T(8,128)S(1)}, f32[264,128]{1,0:T(8,128)S(1)}, u32[]{:S(2)}, u32[]{:S(2)}) %collective-permute-start.8) | collective-permute-done | bytes 135200 | tf_op jit(solution)/shard_map/ppermute | solution.py:646
  99.5 0.1 collective-permute-start.9
  99.6 0.1 pad_add_fusion.where_ref
  99.6 1.8 %collective-permute-done.9.far_ref = f32[1056,128]{1,0:T(8,128)S(1)} collective-permute-done((f32[1056,128]{1,0:T(8,128)S(1)}, f32[1056,128]{1,0:T(8,128)S(1)}, u32[]{:S(2)}, u32[]{:S(2)}) %collective-permute-start.9) | collective-permute-done | bytes 540704 | tf_op jit(solution)/shard_map/ppermute | solution.py:646
  101.5 1.6 %unpack.1 = (f32[2,2,128]{2,1,0:T(2,128)}, f32[2,2,128]{2,1,0:T(2,128)}, f32[2,128,384]{2,1,0:T(8,128)}, f32[2,256]{1,0:T(2,128)}, f32[2,128,128]{2,1,0:T(8,128)...) custom-call(s32[2]{0:T(128)S(1)} %pad_add_fusion.where_ref, ...), custom_call_target="tpu_custom_call" | custom-call | tf_op jit(solution)/shard_map/unpack/pallas_call | solution.py:630
  (5 shorter events, 0.2 us)
Async XLA Ops:
  64.3 3.3 %copy-start = (f32[2,1056,128]{2,1,0:T(8,128)S(1)}, f32[2,1056,128]{2,1,0:T(8,128)}, u32[]{:S(2)}) copy-start(f32[2,1056,128]{2,1,0:T(8,128)} %get-tuple-element.29) | copy-start | bytes 3244036
  65.5 2.1 %collective-permute-start = (f32[1056,128]{1,0:T(8,128)S(1)}, f32[1056,128]{1,0:T(8,128)S(1)}, u32[]{:S(2)}, u32[]{:S(2)}) collective-permute-start(f32[1056,128]{1,0:T(8,128)S(1)} %dynamic-slice_bitcast_fusion), channel_id=1, source_target_pairs={{0,1},{1,0},{2,3},{3,2},{4,5},{5,4},{6,7},{7,6},{8,9},{9,8},{10,11... | collective-permute-start | bytes 1622024 | tf_op jit(solution)/shard_map/ppermute | solution.py:646
  67.7 7.0 %collective-permute-start.1 = (f32[264,128]{1,0:T(8,128)S(1)}, f32[264,128]{1,0:T(8,128)S(1)}, u32[]{:S(2)}, u32[]{:S(2)}) collective-permute-start(f32[264,128]{1,0:T(8,128)S(1)} %get-tuple-element.41), channel_id=1, source_target_pairs={{0,2},{1,3},{2,0},{3,1},{4,6},{5,7},{6,4},{7,5},{8,10},{9,11},{10,... | collective-permute-start | bytes 405512 | tf_op jit(solution)/shard_map/ppermute | solution.py:646
  70.6 8.2 %collective-permute-start.2 = (f32[264,128]{1,0:T(8,128)S(1)}, f32[264,128]{1,0:T(8,128)S(1)}, u32[]{:S(2)}, u32[]{:S(2)}) collective-permute-start(f32[264,128]{1,0:T(8,128)S(1)} %get-tuple-element.43), channel_id=1, source_target_pairs={{0,4},{1,5},{2,6},{3,7},{4,0},{5,1},{6,2},{7,3},{8,12},{9,13},{10,... | collective-permute-start | bytes 405512 | tf_op jit(solution)/shard_map/ppermute | solution.py:646
  72.1 6.7 %collective-permute-start.3 = (f32[264,128]{1,0:T(8,128)S(1)}, f32[264,128]{1,0:T(8,128)S(1)}, u32[]{:S(2)}, u32[]{:S(2)}) collective-permute-start(f32[264,128]{1,0:T(8,128)S(1)} %get-tuple-element.42), channel_id=1, source_target_pairs={{0,6},{1,7},{2,4},{3,5},{4,2},{5,3},{6,0},{7,1},{8,14},{9,15},{10,... | collective-permute-start | bytes 405512 | tf_op jit(solution)/shard_map/ppermute | solution.py:646
  78.9 5.1 %collective-permute-start.4 = (f32[264,128]{1,0:T(8,128)S(1)}, f32[264,128]{1,0:T(8,128)S(1)}, u32[]{:S(2)}, u32[]{:S(2)}) collective-permute-start(f32[264,128]{1,0:T(8,128)S(1)} %fusion.1), channel_id=1, source_target_pairs={{0,8},{1,9},{2,10},{3,11},{4,12},{5,13},{6,14},{7,15},{8,0},{9,1},... | collective-permute-start | bytes 405512 | tf_op jit(solution)/shard_map/ppermute | solution.py:646
  84.0 7.4 %collective-permute-start.5 = (f32[264,128]{1,0:T(8,128)S(1)}, f32[264,128]{1,0:T(8,128)S(1)}, u32[]{:S(2)}, u32[]{:S(2)}) collective-permute-start(f32[264,128]{1,0:T(8,128)S(1)} %add.49), channel_id=1, source_target_pairs={{0,16},{1,17},{2,18},{3,19},{4,20},{5,21},{6,22},{7,23},{8,24},{9,... | collective-permute-start | bytes 405512 | tf_op jit(solution)/shard_map/ppermute | solution.py:646
  91.4 5.1 %collective-permute-start.6 = (f32[264,128]{1,0:T(8,128)S(1)}, f32[264,128]{1,0:T(8,128)S(1)}, u32[]{:S(2)}, u32[]{:S(2)}) collective-permute-start(f32[264,128]{1,0:T(8,128)S(1)} %add.50), channel_id=1, source_target_pairs={{0,2},{1,3},{2,0},{3,1},{4,6},{5,7},{6,4},{7,5},{8,10},{9,11},{10,... | collective-permute-start | bytes 405512 | tf_op jit(solution)/shard_map/ppermute | solution.py:646
  92.8 5.0 %collective-permute-start.7 = (f32[264,128]{1,0:T(8,128)S(1)}, f32[264,128]{1,0:T(8,128)S(1)}, u32[]{:S(2)}, u32[]{:S(2)}) collective-permute-start(f32[264,128]{1,0:T(8,128)S(1)} %add.50), channel_id=1, source_target_pairs={{0,4},{1,5},{2,6},{3,7},{4,0},{5,1},{6,2},{7,3},{8,12},{9,13},{10,... | collective-permute-start | bytes 405512 | tf_op jit(solution)/shard_map/ppermute | solution.py:646
  93.5 5.9 %collective-permute-start.8 = (f32[264,128]{1,0:T(8,128)S(1)}, f32[264,128]{1,0:T(8,128)S(1)}, u32[]{:S(2)}, u32[]{:S(2)}) collective-permute-start(f32[264,128]{1,0:T(8,128)S(1)} %add.50), channel_id=1, source_target_pairs={{0,6},{1,7},{2,4},{3,5},{4,2},{5,3},{6,0},{7,1},{8,14},{9,15},{10,... | collective-permute-start | bytes 405512 | tf_op jit(solution)/shard_map/ppermute | solution.py:646
  99.5 2.0 %collective-permute-start.9 = (f32[1056,128]{1,0:T(8,128)S(1)}, f32[1056,128]{1,0:T(8,128)S(1)}, u32[]{:S(2)}, u32[]{:S(2)}) collective-permute-start(f32[1056,128]{1,0:T(8,128)S(1)} %pad_maximum_fusion.near_ref), channel_id=1, source_target_pairs={{0,1},{1,0},{2,3},{3,2},{4,5},{5,4},{6,7},{7,6},{8,9},{9,8},{10,11... | collective-permute-start | bytes 1622024 | tf_op jit(solution)/shard_map/ppermute | solution.py:646

commit v3 on v2

--- a/solution.py
+++ b/solution.py
@@ -11,7 +11,7 @@
 FF = 256
 LEN = 256
 HALF = 128
-CHUNK = 64
+CHUNK = 128
 QUARTER = 64
 WINDOWS = ((0, 128), (0, 192), (64, 256), (128, 256))
 PLACES = ((0, 128), (256, 448), (640, 832), (1024, 1152))
@@ -22,11 +22,13 @@
 F32 = jnp.float32
 BF16 = jnp.bfloat16
 
-GAIN_ONE, SHIFT_ONE, GAIN_TWO, SHIFT_TWO, OUT_BIAS, DOWN_BIAS, Q_BIAS, V_BIAS, GATE, UP_LOW, UP_HIGH = range(11)
-COLUMNS = 11
-S_GAIN_ONE, S_SHIFT_ONE, S_GAIN_TWO, S_SHIFT_TWO, S_DOWN, S_GATE = range(6)
-SUMS = 6
-S_OUT, S_Q, S_K, S_V, S_UP_LOW, S_UP_HIGH, SMALL = range(6, 13)
+GAIN_ONE, SHIFT_ONE, GAIN_TWO, SHIFT_TWO, DOWN_BIAS, GATE = range(6)
+COLUMNS = 6
+EXTENDED = WIDTH + 16
+S_DOWN, S_GATE = range(2)
+SUMS = 2
+S_LOGIT = 2
+S_OUT, S_Q, S_K, S_V, S_UP_LOW, S_UP_HIGH, S_SHIFT_ONE, S_SHIFT_TWO, S_GAIN_ONE, S_GAIN_TWO = range(2, 12)
 R_QKV, R_OUT, R_UP, R_DOWN, R_SMALL, ROWS = 0, 384, 512, 768, 1024, 1056
 
 
@@ -146,14 +148,16 @@
     running, waiting = [], list(units)
     while running or waiting:
         if waiting:
-            running.insert(0, waiting.pop(0))
+            running.append(waiting.pop(0))
         running = [unit for unit in running if next(unit, "end") != "end"]
         yield
 
 
 def together(parts):
-    running = list(parts)
-    while running:
+    running, waiting = [], list(parts)
+    while running or waiting:
+        if waiting:
+            running.append(waiting.pop(0))
         running = [part for part in running if next(part, "end") != "end"]
 
 
@@ -209,38 +213,42 @@
     )
 
 
-def forward_layer(layer, hidden, segments, masks, weights, columns, power_ref, mixed_ref, scale_ref):
+def forward_layer(
+    layer, hidden, segments, masks, weights, columns, power_ref, mixed_ref, scale_ref, gated_ref, twice_ref
+):
     qkv_t, out_t, up_t, down_t = weights
     column = lambda which: both(columns[layer, which])
-    xhat, unused = norm_parts(hidden)
+    xhat, spread_one = norm_parts(hidden)
     normed = (xhat * column(GAIN_ONE) + column(SHIFT_ONE)).astype(BF16)
     yield
-    projected = dot(qkv_t[layer], normed)
-    yield
-    query = (projected[:WIDTH] + column(Q_BIAS)).astype(BF16)
+    projected = dot(qkv_t[layer][:, :EXTENDED], jnp.concatenate([normed, ones(16)], axis=0))
+    yield
+    query = projected[:WIDTH].astype(BF16)
     keys = projected[WIDTH : 2 * WIDTH].astype(BF16)
-    values = (projected[2 * WIDTH :] + column(V_BIAS)).astype(BF16)
+    values = projected[2 * WIDTH :].astype(BF16)
     yield from attention_forward(query, keys, values, segments, masks, power_ref, mixed_ref, scale_ref)
     mixed = mixed_ref[...]
-    middle = hidden + (dot(out_t[layer], mixed.astype(BF16)) + column(OUT_BIAS))
-    yield
-    xhat_two, unused = norm_parts(middle)
+    middle = hidden + dot(out_t[layer][:, :EXTENDED], jnp.concatenate([mixed.astype(BF16), ones(16)], axis=0))
+    yield
+    xhat_two, spread_two = norm_parts(middle)
     normed_two = (xhat_two * column(GAIN_TWO) + column(SHIFT_TWO)).astype(BF16)
     yield
-    inner = dot(up_t[layer], normed_two)
+    inner = dot(up_t[layer][:, :EXTENDED], jnp.concatenate([normed_two, ones(16)], axis=0))
     yield
     logit = inner[FF : FF + 1]
-    inner = inner[:FF] + jnp.concatenate([column(UP_LOW), column(UP_HIGH)], axis=0)
     gate = jax.nn.sigmoid(logit)
     parts = []
     for start in range(0, FF, CHUNK):
         gated = inner[start : start + CHUNK] * gate
-        power = jnp.tanh(gated * (GELU_A + (GELU_A * GELU_B) * (gated * gated)))
-        parts.append((gated * (0.5 + 0.5 * power)).astype(BF16))
+        twice_up = 1.0 + jnp.tanh(gated * (GELU_A + (GELU_A * GELU_B) * (gated * gated)))
+        gated_ref[start : start + CHUNK] = gated
+        twice_ref[start : start + CHUNK] = twice_up
+        parts.append((gated * twice_up).astype(BF16))
         yield
     active = jnp.concatenate(parts, axis=0)
     output = middle + (dot(down_t[layer], active) + column(DOWN_BIAS))
-    return output, (normed, query, keys, values, mixed, middle, normed_two, inner, logit)
+    rows = jnp.concatenate([spread_one, spread_two, gate, jnp.zeros((5, LEN), F32)], axis=0)
+    return output, (normed, query, keys, values, mixed, xhat, xhat_two, normed_two, rows)
 
 
 def norm_backward(gradient, xhat, scale, gain):
@@ -332,44 +340,41 @@
 
 
 def backward_layer(
-    layer, gradient, hidden, masks, kept, power_ref, scale_ref, raw, columns, totals, dq_ref
+    layer, gradient, masks, kept, power_ref, scale_ref, gated_ref, twice_ref, raw, columns, totals, dq_ref
 ):
     w_qkv, w_out, w_up, w_down = raw
-    normed, query, keys, values, mixed, middle, normed_two, inner, logit = kept
+    normed, query, keys, values, mixed, xhat, xhat_two, normed_two, rows = kept
+    spread_one, spread_two, gate = rows[0:1], rows[1:2], rows[2:3]
     qkv_total, out_total, up_total, down_total, sums = totals
     column = lambda which: both(columns[layer, which])
     branch = gradient.astype(BF16)
-    sums[S_DOWN] += fold(branch.astype(F32))
+    sums[S_DOWN] += fold(gradient)
     grad_active = dot(w_down[layer], branch)
     yield
-    gate = jax.nn.sigmoid(logit)
     actives, inners = [], []
     logit_sum = jnp.zeros((1, LEN), F32)
     for start in range(0, FF, CHUNK):
         rows = slice(start, start + CHUNK)
-        gated = inner[rows] * gate
-        square = gated * gated
-        power = jnp.tanh(gated * (GELU_A + (GELU_A * GELU_B) * square))
-        half_up = 0.5 + 0.5 * power
-        active = gated * half_up
-        slope = half_up + (active * (1.0 - power)) * (GELU_A + (3.0 * GELU_A * GELU_B) * square)
-        grad_gated = grad_active[rows].astype(BF16).astype(F32) * slope
-        logit_sum = logit_sum + jnp.sum(grad_gated * inner[rows], axis=0, keepdims=True)
+        gated = gated_ref[rows]
+        twice_up = twice_ref[rows]
+        active = gated * twice_up
+        curve = GELU_A + (3.0 * GELU_A * GELU_B) * (gated * gated)
+        slope = twice_up + (active * (2.0 - twice_up)) * curve
+        grad_gated = grad_active[rows] * slope
+        logit_sum = logit_sum + jnp.sum(grad_gated * gated, axis=0, keepdims=True)
         actives.append(active.astype(BF16))
         inners.append((grad_gated * gate).astype(BF16))
         yield
-    grad_logit = logit_sum * (gate * (1.0 - gate))
+    grad_logit = logit_sum * (1.0 - gate)
     active = jnp.concatenate(actives, axis=0)
     grad_inner = jnp.concatenate(inners, axis=0)
     grad_two = dot(w_up[layer], grad_inner) + column(GATE) * grad_logit
     down_total[...] += dot(branch, active.T)
     up_total[...] += dot(jnp.concatenate([normed_two, ones(16)], axis=0), grad_inner.T)
     sums[S_GATE] += fold(normed_two.astype(F32) * grad_logit)
-    yield
-    xhat, scale = norm_parts(middle)
-    sums[S_GAIN_TWO] += fold(grad_two * xhat)
-    sums[S_SHIFT_TWO] += fold(grad_two)
-    grad_middle = gradient + norm_backward(grad_two, xhat, scale, column(GAIN_TWO))
+    sums[S_LOGIT, 0:1] += fold(grad_logit)
+    yield
+    grad_middle = gradient + norm_backward(grad_two, xhat_two, spread_two, column(GAIN_TWO))
     attended = grad_middle.astype(BF16)
     yield
     grad_mixed = dot(w_out[layer], attended)
@@ -383,28 +388,25 @@
     qkv_total[...] += dot(jnp.concatenate([normed, ones(16)], axis=0), grad_rows)
     grad_one = dot(w_qkv[layer], jnp.concatenate([grad_query, grad_keys.T, grad_values.T], axis=0))
     yield
-    xhat, scale = norm_parts(hidden)
-    sums[S_GAIN_ONE] += fold(grad_one * xhat)
-    sums[S_SHIFT_ONE] += fold(grad_one)
-    return grad_middle + norm_backward(grad_one, xhat, scale, column(GAIN_ONE))
+    return grad_middle + norm_backward(grad_one, xhat, spread_one, column(GAIN_ONE))
 
 
 def spread(row):
     return jnp.broadcast_to(row, (WIDTH, WIDTH)).T
 
 
-def fill_columns(layer, columns, gains, shifts, qv_bias, out_bias, w_gate, up_bias, down_bias):
+def bias_lanes(row):
+    parts = [part.astype(F32) for part in split_three(row)]
+    return jnp.concatenate(parts + [jnp.zeros((13, WIDTH), F32)], axis=0).T.astype(BF16)
+
+
+def fill_columns(layer, columns, gains, shifts, w_gate, down_bias):
     columns[layer, GAIN_ONE] = spread(gains[layer, 0:1])
     columns[layer, GAIN_TWO] = spread(gains[layer, 1:2])
     columns[layer, SHIFT_ONE] = spread(shifts[layer, 0:1])
     columns[layer, SHIFT_TWO] = spread(shifts[layer, 1:2])
-    columns[layer, OUT_BIAS] = spread(out_bias[layer : layer + 1])
     columns[layer, DOWN_BIAS] = spread(down_bias[layer : layer + 1])
-    columns[layer, Q_BIAS] = spread(qv_bias[layer : layer + 1, :WIDTH]) * 0.25
-    columns[layer, V_BIAS] = spread(qv_bias[layer : layer + 1, WIDTH:])
     columns[layer, GATE] = spread(w_gate[layer : layer + 1].astype(F32))
-    columns[layer, UP_LOW] = spread(up_bias[layer : layer + 1, :WIDTH])
-    columns[layer, UP_HIGH] = spread(up_bias[layer : layer + 1, WIDTH:])
 
 
 def clear_totals(totals):
@@ -412,7 +414,20 @@
         ref[...] = jnp.zeros_like(ref)
 
 
-def write_totals(totals, grads_ref):
+def through(weights, row):
+    parts = jnp.concatenate(split_three(row), axis=0)
+    return jnp.sum(lax.dot_general(parts, weights, (((1,), (1,)), ((), ())), preferred_element_type=F32), axis=0, keepdims=True)
+
+
+def across(value):
+    parts = [value[:, start : start + WIDTH] for start in range(0, value.shape[1], WIDTH)]
+    total = parts[0]
+    for part in parts[1:]:
+        total = total + part
+    return jnp.sum(total.T, axis=0, keepdims=True)
+
+
+def write_totals(totals, grads_ref, w_qkv, w_gate, w_up, gains, shifts):
     qkv_total, out_total, up_total, down_total, sums = totals
     for part in range(3):
         rows = slice(R_QKV + part * WIDTH, R_QKV + (part + 1) * WIDTH)
@@ -421,11 +436,21 @@
     for part in range(2):
         lanes = slice(part * WIDTH, (part + 1) * WIDTH)
         grads_ref[R_UP + part * WIDTH : R_UP + (part + 1) * WIDTH] = up_total[:WIDTH, lanes]
-        grads_ref[R_DOWN + part * WIDTH : R_DOWN + (part + 1) * WIDTH] = down_total[:, lanes].T
+        grads_ref[R_DOWN + part * WIDTH : R_DOWN + (part + 1) * WIDTH] = down_total[:, lanes].T * 0.5
     rows = [jnp.sum(sums[which].T, axis=0, keepdims=True) for which in range(SUMS)]
     rows.append(out_total[WIDTH : WIDTH + 1])
     rows.extend(qkv_total[WIDTH : WIDTH + 1, part * WIDTH : (part + 1) * WIDTH] for part in range(3))
     rows.extend(up_total[WIDTH : WIDTH + 1, part * WIDTH : (part + 1) * WIDTH] for part in range(2))
+    rows.append(through(w_qkv, qkv_total[WIDTH : WIDTH + 1]))
+    logit = jnp.sum(sums[S_LOGIT, 0:1], axis=1, keepdims=True)
+    rows.append(through(w_up, up_total[WIDTH : WIDTH + 1]) + logit * w_gate.astype(F32))
+    moments = (
+        across(qkv_total[:WIDTH] * w_qkv.astype(F32)),
+        across(up_total[:WIDTH] * w_up.astype(F32)) + rows[S_GATE] * w_gate.astype(F32),
+    )
+    for which, moment in enumerate(moments):
+        norm = slice(which, which + 1)
+        rows.append((moment - shifts[norm] * rows[S_SHIFT_ONE + which]) / gains[norm])
     rows.append(jnp.zeros((ROWS - R_SMALL - len(rows), WIDTH), F32))
     grads_ref[R_SMALL:ROWS] = jnp.concatenate(rows, axis=0)
 
@@ -434,9 +459,9 @@
     per_step, steps,
     x_ref, seg_ref, cot_ref, gains, shifts, w_qkv, qv_bias, w_out, out_bias, w_gate, w_up, up_bias, w_down, down_bias,
     result_ref, grad_inputs_ref, grads_ref,
-    columns, qkv_t, out_t, up_t, down_t, mixed_scratch, dq_ref, power_last, scale_last,
-    grad_kept, normed_kept, qkv_kept, mixed_kept, scale_kept, middle_kept, normed_two_kept, inner_kept, logit_kept,
-    power_kept, *totals,
+    columns, qkv_t, out_t, up_t, down_t, half_down, mixed_scratch, dq_ref, power_last, scale_last, gated_last, twice_last,
+    grad_kept, normed_kept, qkv_kept, mixed_kept, scale_kept, xhat_kept, xhat_two_kept, normed_two_kept, rows_kept,
+    power_kept, gated_kept, twice_kept, *totals,
 ):
     step = pl.program_id(0)
     totals_zero, totals_one = totals[: len(totals) // 2], totals[len(totals) // 2 :]
@@ -445,19 +470,29 @@
     def start():
         clear_totals(totals)
         for layer in range(LAYERS):
-            fill_columns(layer, columns, gains, shifts, qv_bias, out_bias, w_gate, up_bias, down_bias)
-            qkv_t[layer, :WIDTH] = (w_qkv[layer][:, :WIDTH] * jnp.asarray(0.25, BF16)).T
-            qkv_t[layer, WIDTH:] = w_qkv[layer][:, WIDTH:].T
-            out_t[layer] = w_out[layer].T
-            up_t[layer, :FF] = w_up[layer].T
-            up_t[layer, FF:] = jnp.concatenate(
+            fill_columns(layer, columns, gains, shifts, w_gate, down_bias)
+            for ref in (qkv_t, out_t, up_t):
+                ref[layer, :, WIDTH:] = zeros(ref.shape[1], WIDTH)
+            qkv_t[layer, :WIDTH, :WIDTH] = (w_qkv[layer][:, :WIDTH] * jnp.asarray(0.25, BF16)).T
+            qkv_t[layer, WIDTH:, :WIDTH] = w_qkv[layer][:, WIDTH:].T
+            biases = qv_bias[layer : layer + 1]
+            qkv_t[layer, :WIDTH, WIDTH:EXTENDED] = bias_lanes(biases[:, :WIDTH] * 0.25)
+            qkv_t[layer, 2 * WIDTH :, WIDTH:EXTENDED] = bias_lanes(biases[:, WIDTH:])
+            out_t[layer, :, :WIDTH] = w_out[layer].T
+            out_t[layer, :, WIDTH:EXTENDED] = bias_lanes(out_bias[layer : layer + 1])
+            up_t[layer, :FF, :WIDTH] = w_up[layer].T
+            up_t[layer, FF:, :WIDTH] = jnp.concatenate(
                 [w_gate[layer : layer + 1].astype(F32), jnp.zeros((15, WIDTH), F32)], axis=0
             ).astype(BF16)
-            down_t[layer] = w_down[layer].T
+            biases = up_bias[layer : layer + 1]
+            up_t[layer, :WIDTH, WIDTH:EXTENDED] = bias_lanes(biases[:, :WIDTH])
+            up_t[layer, WIDTH:FF, WIDTH:EXTENDED] = bias_lanes(biases[:, WIDTH:])
+            half_down[layer] = w_down[layer] * jnp.asarray(0.5, BF16)
+            down_t[layer] = half_down[layer].T
 
     masks = make_masks()
     weights = (qkv_t, out_t, up_t, down_t)
-    raw = (w_qkv, w_out, w_up, w_down)
+    raw = (w_qkv, w_out, w_up, half_down)
 
     def upward(item):
         tokens = slice(item * LEN, (item + 1) * LEN)
@@ -466,41 +501,40 @@
         hidden = x_ref[tokens].astype(F32).T
         middle_hidden, kept = yield from forward_layer(
             0, hidden, segments, masks, weights, columns, power_kept.at[place], mixed_scratch.at[item],
-            scale_kept.at[place],
+            scale_kept.at[place], gated_kept.at[place], twice_kept.at[place],
         )
-        normed, query, keys, values, mixed, middle, normed_two, inner, logit = kept
+        normed, query, keys, values, mixed, xhat, xhat_two, normed_two, rows = kept
         normed_kept[place] = normed
         qkv_kept[place, :WIDTH] = query
         qkv_kept[place, WIDTH : 2 * WIDTH] = keys
         qkv_kept[place, 2 * WIDTH :] = values
         mixed_kept[place] = mixed
-        middle_kept[place] = middle
+        xhat_kept[place] = xhat
+        xhat_two_kept[place] = xhat_two
         normed_two_kept[place] = normed_two
-        inner_kept[place] = inner
-        logit_kept[place] = jnp.broadcast_to(logit, (8, LEN))
+        rows_kept[place] = rows
         output, kept = yield from forward_layer(
             1, middle_hidden, segments, masks, weights, columns, power_last.at[item], mixed_scratch.at[item],
-            scale_last.at[item],
+            scale_last.at[item], gated_last.at[item], twice_last.at[item],
         )
         result_ref[tokens] = output.T.astype(BF16)
         gradient = cot_ref[tokens].astype(F32).T
         grad_kept[place] = yield from backward_layer(
-            1, gradient, middle_hidden, masks, kept, power_last.at[item], scale_last.at[item], raw, columns,
-            totals_one, dq_ref.at[item],
+            1, gradient, masks, kept, power_last.at[item], scale_last.at[item], gated_last.at[item],
+            twice_last.at[item], raw, columns, totals_one, dq_ref.at[item],
         )
 
     def downward(item):
         tokens = slice(item * LEN, (item + 1) * LEN)
         place = (step - steps) * per_step + item
-        hidden = x_ref[tokens].astype(F32).T
         kept = (
             normed_kept[place], qkv_kept[place, :WIDTH], qkv_kept[place, WIDTH : 2 * WIDTH],
-            qkv_kept[place, 2 * WIDTH :], mixed_kept[place], middle_kept[place], normed_two_kept[place],
-            inner_kept[place], logit_kept[place, 0:1],
+            qkv_kept[place, 2 * WIDTH :], mixed_kept[place], xhat_kept[place], xhat_two_kept[place],
+            normed_two_kept[place], rows_kept[place],
         )
         gradient = yield from backward_layer(
-            0, grad_kept[place], hidden, masks, kept, power_kept.at[place], scale_kept.at[place], raw, columns,
-            totals_zero, dq_ref.at[item],
+            0, grad_kept[place], masks, kept, power_kept.at[place], scale_kept.at[place], gated_kept.at[place],
+            twice_kept.at[place], raw, columns, totals_zero, dq_ref.at[item],
         )
         grad_inputs_ref[tokens] = gradient.T
 
@@ -514,8 +548,11 @@
 
     @pl.when(step == 2 * steps - 1)
     def finish():
-        write_totals(totals_zero, grads_ref.at[0])
-        write_totals(totals_one, grads_ref.at[1])
+        for layer, part in enumerate((totals_zero, totals_one)):
+            write_totals(
+                part, grads_ref.at[layer], w_qkv[layer], w_gate[layer : layer + 1], w_up[layer], gains[layer],
+                shifts[layer],
+            )
 
 
 def totals_scratch():
@@ -524,7 +561,7 @@
         pltpu.VMEM((WIDTH + 16, WIDTH), F32),
         pltpu.VMEM((WIDTH + 16, FF), F32),
         pltpu.VMEM((WIDTH, FF), F32),
-        pltpu.VMEM((SUMS, WIDTH, WIDTH), F32),
+        pltpu.VMEM((SUMS + 1, WIDTH, WIDTH), F32),
     ]
 
 
@@ -545,7 +582,7 @@
         lambda *refs: kernel(per_step, steps, *refs),
         grid=(2 * steps,),
         in_specs=[
-            pl.BlockSpec(rows, lambda i: (i % steps, 0)),
+            pl.BlockSpec(rows, lambda i: (jnp.minimum(i, steps - 1), 0)),
             whole(segment_ids),
             pl.BlockSpec(rows, lambda i: (jnp.minimum(i, steps - 1), 0)),
         ]
@@ -562,24 +599,29 @@
         ],
         scratch_shapes=[
             pltpu.VMEM((LAYERS, COLUMNS, WIDTH, WIDTH), F32),
-            pltpu.VMEM((LAYERS, 3 * WIDTH, WIDTH), BF16),
-            pltpu.VMEM((LAYERS, WIDTH, WIDTH), BF16),
-            pltpu.VMEM((LAYERS, FF + 16, WIDTH), BF16),
+            pltpu.VMEM((LAYERS, 3 * WIDTH, 2 * WIDTH), BF16),
+            pltpu.VMEM((LAYERS, WIDTH, 2 * WIDTH), BF16),
+            pltpu.VMEM((LAYERS, FF + 16, 2 * WIDTH), BF16),
             pltpu.VMEM((LAYERS, WIDTH, FF), BF16),
+            pltpu.VMEM((LAYERS, FF, WIDTH), BF16),
             kept(WIDTH, F32, per_step),
             kept(WIDTH, F32, per_step),
             kept(POWER_ROWS, BF16, per_step),
             kept(8 * HEADS, F32, per_step),
+            kept(FF, F32, per_step),
+            kept(FF, F32, per_step),
             kept(WIDTH, F32),
             kept(WIDTH, BF16),
             kept(3 * WIDTH, BF16),
             kept(WIDTH, F32),
             kept(8 * HEADS, F32),
             kept(WIDTH, F32),
+            kept(WIDTH, F32),
             kept(WIDTH, BF16),
-            kept(FF, F32),
             kept(8, F32),
             kept(POWER_ROWS, BF16),
+            kept(FF, F32),
+            kept(FF, F32),
         ]
         + totals_scratch()
         + totals_scratch(),

time: 103 us -> 97.4 us (0.946)
  Pallas kernels: 65.2 us -> 59.3 us
    pallas_call x1, Pallas kernels: 63.6 us -> 57.7 us  [local_part(): pl.pallas_call(lambda *refs: kernel(per_step, steps, *refs), grid=(2 * st...]
where the time goes in v3:
time: 97.4 us; the launch traced here: 97.2 us
  Pallas kernels  59.3 us (61%)
  waiting for transfers between devices  22.8 us (23%)
  starting transfers between devices  12.9 us (13%)
  local copies, waits for them, and re-layouts  1.23 us (1%)
    pallas_call x1, Pallas kernels, local_part(): pl.pallas_call(lambda *refs: kernel(per_step, steps, *refs), grid=(2 * st...  57.7 us
    ppermute x10, waiting for transfers between devices, swap(): return lax.ppermute(value, 'seq', [(i, i ^ mask) for i in range(size)])  22.8 us
    ppermute x10, starting transfers between devices, swap(): return lax.ppermute(value, 'seq', [(i, i ^ mask) for i in range(size)])  12.9 us
  transfers between devices with their start and end apart: 10, of which 9 were waited for; matrix products, arithmetic and copies ran while one was open for 0% of the time, Pallas kernels for 0%

profile of v3, /device:TPU:0, one launch (start us, length us, event | category | flops | bytes accessed | tf_op | source)
XLA Modules:
  0.0 97.2 jit_solution(15676905441005366994)
XLA Ops:
  0.7 57.7 %layers.1 = (bf16[4096,128]{1,0:T(8,128)(2,1)}, f32[4096,128]{1,0:T(8,128)}, f32[2,1056,128]{2,1,0:T(8,128)}) custom-call(bf16[4096,128]{1,0:T(8,128)(2,1)} %refs_0_.1, s32[16,256]{1,0:T(8,128)} %refs_1_.1, bf16[4096,128]{1,0:T(8,128)(2,1)} %refs_2_.1, f32[2,2,128]{2,1,0:T(2,128)} %refs_3_.1, f32[2,2,128]{2,1,0:T(2,128)} %refs_4_.1, ...), custom_call_target="tpu_custom_call" | custom-call | tf_op jit(solution)/shard_map/layers/pallas_call | solution.py:581
  58.4 0.0 copy-start
  58.4 1.2 %dynamic-slice_bitcast_fusion = f32[1056,128]{1,0:T(8,128)S(1)} fusion(f32[2,1056,128]{2,1,0:T(8,128)} %get-tuple-element.29, s32[]{:T(128)S(6)} %select_n.21), kind=kLoop, calls=%fused_computation.2 | loop fusion | bytes 1081348 | tf_op jit(solution)/shard_map/jit(dynamic_index_in_dim)/squeeze | solution.py:691
  59.6 0.5 collective-permute-start
  60.1 1.6 %collective-permute-done = f32[1056,128]{1,0:T(8,128)S(1)} collective-permute-done((f32[1056,128]{1,0:T(8,128)S(1)}, f32[1056,128]{1,0:T(8,128)S(1)}, u32[]{:S(2)}, u32[]{:S(2)}) %collective-permute-start) | collective-permute-done | bytes 540704 | tf_op jit(solution)/shard_map/ppermute | solution.py:688
  61.7 0.0 copy-done
  61.7 0.1 bitcast_add_fusion
  61.8 2.9 %collective-permute-start.1 = (f32[264,128]{1,0:T(8,128)S(1)}, f32[264,128]{1,0:T(8,128)S(1)}, u32[]{:S(2)}, u32[]{:S(2)}) collective-permute-start(f32[264,128]{1,0:T(8,128)S(1)} %get-tuple-element.41), channel_id=1, source_target_pairs={{0,2},{1,3},{2,0},{3,1},{4,6},{5,7},{6,4},{7,5},{8,10},{9,11},{10,... | collective-permute-start | bytes 405512 | tf_op jit(solution)/shard_map/ppermute | solution.py:688
  64.7 1.5 %collective-permute-start.2 = (f32[264,128]{1,0:T(8,128)S(1)}, f32[264,128]{1,0:T(8,128)S(1)}, u32[]{:S(2)}, u32[]{:S(2)}) collective-permute-start(f32[264,128]{1,0:T(8,128)S(1)} %get-tuple-element.43), channel_id=1, source_target_pairs={{0,4},{1,5},{2,6},{3,7},{4,0},{5,1},{6,2},{7,3},{8,12},{9,13},{10,... | collective-permute-start | bytes 405512 | tf_op jit(solution)/shard_map/ppermute | solution.py:688
  66.2 0.0 collective-permute-start.3
  66.2 2.5 %collective-permute-done.1 = f32[264,128]{1,0:T(8,128)S(1)} collective-permute-done((f32[264,128]{1,0:T(8,128)S(1)}, f32[264,128]{1,0:T(8,128)S(1)}, u32[]{:S(2)}, u32[]{:S(2)}) %collective-permute-start.1) | collective-permute-done | bytes 135200 | tf_op jit(solution)/shard_map/ppermute | solution.py:688
  68.8 4.2 %collective-permute-done.2 = f32[264,128]{1,0:T(8,128)S(1)} collective-permute-done((f32[264,128]{1,0:T(8,128)S(1)}, f32[264,128]{1,0:T(8,128)S(1)}, u32[]{:S(2)}, u32[]{:S(2)}) %collective-permute-start.2) | collective-permute-done | bytes 135200 | tf_op jit(solution)/shard_map/ppermute | solution.py:688
  72.9 0.0 collective-permute-done.3
  73.0 1.6 %collective-permute-start.4 = (f32[264,128]{1,0:T(8,128)S(1)}, f32[264,128]{1,0:T(8,128)S(1)}, u32[]{:S(2)}, u32[]{:S(2)}) collective-permute-start(f32[264,128]{1,0:T(8,128)S(1)} %fusion.1), channel_id=1, source_target_pairs={{0,8},{1,9},{2,10},{3,11},{4,12},{5,13},{6,14},{7,15},{8,0},{9,1},... | collective-permute-start | bytes 405512 | tf_op jit(solution)/shard_map/ppermute | solution.py:688
  74.6 3.4 %collective-permute-done.4 = f32[264,128]{1,0:T(8,128)S(1)} collective-permute-done((f32[264,128]{1,0:T(8,128)S(1)}, f32[264,128]{1,0:T(8,128)S(1)}, u32[]{:S(2)}, u32[]{:S(2)}) %collective-permute-start.4) | collective-permute-done | bytes 135200 | tf_op jit(solution)/shard_map/ppermute | solution.py:688
  78.1 2.6 %collective-permute-start.5 = (f32[264,128]{1,0:T(8,128)S(1)}, f32[264,128]{1,0:T(8,128)S(1)}, u32[]{:S(2)}, u32[]{:S(2)}) collective-permute-start(f32[264,128]{1,0:T(8,128)S(1)} %add.49), channel_id=1, source_target_pairs={{0,16},{1,17},{2,18},{3,19},{4,20},{5,21},{6,22},{7,23},{8,24},{9,... | collective-permute-start | bytes 405512 | tf_op jit(solution)/shard_map/ppermute | solution.py:688
  80.7 4.8 %collective-permute-done.5 = f32[264,128]{1,0:T(8,128)S(1)} collective-permute-done((f32[264,128]{1,0:T(8,128)S(1)}, f32[264,128]{1,0:T(8,128)S(1)}, u32[]{:S(2)}, u32[]{:S(2)}) %collective-permute-start.5) | collective-permute-done | bytes 135200 | tf_op jit(solution)/shard_map/ppermute | solution.py:688
  85.5 1.4 %collective-permute-start.6 = (f32[264,128]{1,0:T(8,128)S(1)}, f32[264,128]{1,0:T(8,128)S(1)}, u32[]{:S(2)}, u32[]{:S(2)}) collective-permute-start(f32[264,128]{1,0:T(8,128)S(1)} %add.50), channel_id=1, source_target_pairs={{0,2},{1,3},{2,0},{3,1},{4,6},{5,7},{6,4},{7,5},{8,10},{9,11},{10,... | collective-permute-start | bytes 405512 | tf_op jit(solution)/shard_map/ppermute | solution.py:688
  86.9 0.7 collective-permute-start.7
  87.6 1.4 %collective-permute-start.8 = (f32[264,128]{1,0:T(8,128)S(1)}, f32[264,128]{1,0:T(8,128)S(1)}, u32[]{:S(2)}, u32[]{:S(2)}) collective-permute-start(f32[264,128]{1,0:T(8,128)S(1)} %add.50), channel_id=1, source_target_pairs={{0,6},{1,7},{2,4},{3,5},{4,2},{5,3},{6,0},{7,1},{8,14},{9,15},{10,... | collective-permute-start | bytes 405512 | tf_op jit(solution)/shard_map/ppermute | solution.py:688
  89.1 1.5 %collective-permute-done.6 = f32[264,128]{1,0:T(8,128)S(1)} collective-permute-done((f32[264,128]{1,0:T(8,128)S(1)}, f32[264,128]{1,0:T(8,128)S(1)}, u32[]{:S(2)}, u32[]{:S(2)}) %collective-permute-start.6) | collective-permute-done | bytes 135200 | tf_op jit(solution)/shard_map/ppermute | solution.py:688
  90.6 1.3 %collective-permute-done.7 = f32[264,128]{1,0:T(8,128)S(1)} collective-permute-done((f32[264,128]{1,0:T(8,128)S(1)}, f32[264,128]{1,0:T(8,128)S(1)}, u32[]{:S(2)}, u32[]{:S(2)}) %collective-permute-start.7) | collective-permute-done | bytes 135200 | tf_op jit(solution)/shard_map/ppermute | solution.py:688
  91.9 1.6 %collective-permute-done.8 = f32[264,128]{1,0:T(8,128)S(1)} collective-permute-done((f32[264,128]{1,0:T(8,128)S(1)}, f32[264,128]{1,0:T(8,128)S(1)}, u32[]{:S(2)}, u32[]{:S(2)}) %collective-permute-start.8) | collective-permute-done | bytes 135200 | tf_op jit(solution)/shard_map/ppermute | solution.py:688
  93.6 0.1 collective-permute-start.9
  93.7 0.1 pad_add_fusion.where_ref
  93.8 1.8 %collective-permute-done.9.far_ref = f32[1056,128]{1,0:T(8,128)S(1)} collective-permute-done((f32[1056,128]{1,0:T(8,128)S(1)}, f32[1056,128]{1,0:T(8,128)S(1)}, u32[]{:S(2)}, u32[]{:S(2)}) %collective-permute-start.9) | collective-permute-done | bytes 540704 | tf_op jit(solution)/shard_map/ppermute | solution.py:688
  95.6 1.6 %unpack.1 = (f32[2,2,128]{2,1,0:T(2,128)}, f32[2,2,128]{2,1,0:T(2,128)}, f32[2,128,384]{2,1,0:T(8,128)}, f32[2,256]{1,0:T(2,128)}, f32[2,128,128]{2,1,0:T(8,128)...) custom-call(s32[2]{0:T(128)S(1)} %pad_add_fusion.where_ref, ...), custom_call_target="tpu_custom_call" | custom-call | tf_op jit(solution)/shard_map/unpack/pallas_call | solution.py:672
  (5 shorter events, 0.2 us)
Async XLA Ops:
  58.4 3.3 %copy-start = (f32[2,1056,128]{2,1,0:T(8,128)S(1)}, f32[2,1056,128]{2,1,0:T(8,128)}, u32[]{:S(2)}) copy-start(f32[2,1056,128]{2,1,0:T(8,128)} %get-tuple-element.29) | copy-start | bytes 3244036
  59.6 2.1 %collective-permute-start = (f32[1056,128]{1,0:T(8,128)S(1)}, f32[1056,128]{1,0:T(8,128)S(1)}, u32[]{:S(2)}, u32[]{:S(2)}) collective-permute-start(f32[1056,128]{1,0:T(8,128)S(1)} %dynamic-slice_bitcast_fusion), channel_id=1, source_target_pairs={{0,1},{1,0},{2,3},{3,2},{4,5},{5,4},{6,7},{7,6},{8,9},{9,8},{10,11... | collective-permute-start | bytes 1622024 | tf_op jit(solution)/shard_map/ppermute | solution.py:688
  61.8 7.0 %collective-permute-start.1 = (f32[264,128]{1,0:T(8,128)S(1)}, f32[264,128]{1,0:T(8,128)S(1)}, u32[]{:S(2)}, u32[]{:S(2)}) collective-permute-start(f32[264,128]{1,0:T(8,128)S(1)} %get-tuple-element.41), channel_id=1, source_target_pairs={{0,2},{1,3},{2,0},{3,1},{4,6},{5,7},{6,4},{7,5},{8,10},{9,11},{10,... | collective-permute-start | bytes 405512 | tf_op jit(solution)/shard_map/ppermute | solution.py:688
  64.7 8.2 %collective-permute-start.2 = (f32[264,128]{1,0:T(8,128)S(1)}, f32[264,128]{1,0:T(8,128)S(1)}, u32[]{:S(2)}, u32[]{:S(2)}) collective-permute-start(f32[264,128]{1,0:T(8,128)S(1)} %get-tuple-element.43), channel_id=1, source_target_pairs={{0,4},{1,5},{2,6},{3,7},{4,0},{5,1},{6,2},{7,3},{8,12},{9,13},{10,... | collective-permute-start | bytes 405512 | tf_op jit(solution)/shard_map/ppermute | solution.py:688
  66.2 6.7 %collective-permute-start.3 = (f32[264,128]{1,0:T(8,128)S(1)}, f32[264,128]{1,0:T(8,128)S(1)}, u32[]{:S(2)}, u32[]{:S(2)}) collective-permute-start(f32[264,128]{1,0:T(8,128)S(1)} %get-tuple-element.42), channel_id=1, source_target_pairs={{0,6},{1,7},{2,4},{3,5},{4,2},{5,3},{6,0},{7,1},{8,14},{9,15},{10,... | collective-permute-start | bytes 405512 | tf_op jit(solution)/shard_map/ppermute | solution.py:688
  73.0 5.1 %collective-permute-start.4 = (f32[264,128]{1,0:T(8,128)S(1)}, f32[264,128]{1,0:T(8,128)S(1)}, u32[]{:S(2)}, u32[]{:S(2)}) collective-permute-start(f32[264,128]{1,0:T(8,128)S(1)} %fusion.1), channel_id=1, source_target_pairs={{0,8},{1,9},{2,10},{3,11},{4,12},{5,13},{6,14},{7,15},{8,0},{9,1},... | collective-permute-start | bytes 405512 | tf_op jit(solution)/shard_map/ppermute | solution.py:688
  78.1 7.4 %collective-permute-start.5 = (f32[264,128]{1,0:T(8,128)S(1)}, f32[264,128]{1,0:T(8,128)S(1)}, u32[]{:S(2)}, u32[]{:S(2)}) collective-permute-start(f32[264,128]{1,0:T(8,128)S(1)} %add.49), channel_id=1, source_target_pairs={{0,16},{1,17},{2,18},{3,19},{4,20},{5,21},{6,22},{7,23},{8,24},{9,... | collective-permute-start | bytes 405512 | tf_op jit(solution)/shard_map/ppermute | solution.py:688
  85.5 5.1 %collective-permute-start.6 = (f32[264,128]{1,0:T(8,128)S(1)}, f32[264,128]{1,0:T(8,128)S(1)}, u32[]{:S(2)}, u32[]{:S(2)}) collective-permute-start(f32[264,128]{1,0:T(8,128)S(1)} %add.50), channel_id=1, source_target_pairs={{0,2},{1,3},{2,0},{3,1},{4,6},{5,7},{6,4},{7,5},{8,10},{9,11},{10,... | collective-permute-start | bytes 405512 | tf_op jit(solution)/shard_map/ppermute | solution.py:688
  86.9 5.0 %collective-permute-start.7 = (f32[264,128]{1,0:T(8,128)S(1)}, f32[264,128]{1,0:T(8,128)S(1)}, u32[]{:S(2)}, u32[]{:S(2)}) collective-permute-start(f32[264,128]{1,0:T(8,128)S(1)} %add.50), channel_id=1, source_target_pairs={{0,4},{1,5},{2,6},{3,7},{4,0},{5,1},{6,2},{7,3},{8,12},{9,13},{10,... | collective-permute-start | bytes 405512 | tf_op jit(solution)/shard_map/ppermute | solution.py:688
  87.6 5.9 %collective-permute-start.8 = (f32[264,128]{1,0:T(8,128)S(1)}, f32[264,128]{1,0:T(8,128)S(1)}, u32[]{:S(2)}, u32[]{:S(2)}) collective-permute-start(f32[264,128]{1,0:T(8,128)S(1)} %add.50), channel_id=1, source_target_pairs={{0,6},{1,7},{2,4},{3,5},{4,2},{5,3},{6,0},{7,1},{8,14},{9,15},{10,... | collective-permute-start | bytes 405512 | tf_op jit(solution)/shard_map/ppermute | solution.py:688
  93.6 2.0 %collective-permute-start.9 = (f32[1056,128]{1,0:T(8,128)S(1)}, f32[1056,128]{1,0:T(8,128)S(1)}, u32[]{:S(2)}, u32[]{:S(2)}) collective-permute-start(f32[1056,128]{1,0:T(8,128)S(1)} %pad_maximum_fusion.near_ref), channel_id=1, source_target_pairs={{0,1},{1,0},{2,3},{3,2},{4,5},{5,4},{6,7},{7,6},{8,9},{9,8},{10,11... | collective-permute-start | bytes 1622024 | tf_op jit(solution)/shard_map/ppermute | solution.py:688

commit v4 on v3

--- a/solution.py
+++ b/solution.py
@@ -11,7 +11,8 @@
 FF = 256
 LEN = 256
 HALF = 128
-CHUNK = 128
+CHUNK = 256
+AHEAD = 44
 QUARTER = 64
 WINDOWS = ((0, 128), (0, 192), (64, 256), (128, 256))
 PLACES = ((0, 128), (256, 448), (640, 832), (1024, 1152))
@@ -153,12 +154,16 @@
         yield
 
 
-def together(parts):
-    running, waiting = [], list(parts)
+def together(parts, late=(), wait=0):
+    running, waiting, turn = [], list(parts), 0
     while running or waiting:
         if waiting:
             running.append(waiting.pop(0))
+        if turn >= wait and late:
+            running.append(late.pop(0))
         running = [part for part in running if next(part, "end") != "end"]
+        turn += 1
+    assert not late
 
 
 def segment_masks(segments):
@@ -213,19 +218,20 @@
     )
 
 
-def forward_layer(
-    layer, hidden, segments, masks, weights, columns, power_ref, mixed_ref, scale_ref, gated_ref, twice_ref
-):
-    qkv_t, out_t, up_t, down_t = weights
+def project(layer, hidden, weights, columns):
     column = lambda which: both(columns[layer, which])
     xhat, spread_one = norm_parts(hidden)
     normed = (xhat * column(GAIN_ONE) + column(SHIFT_ONE)).astype(BF16)
     yield
-    projected = dot(qkv_t[layer][:, :EXTENDED], jnp.concatenate([normed, ones(16)], axis=0))
-    yield
-    query = projected[:WIDTH].astype(BF16)
-    keys = projected[WIDTH : 2 * WIDTH].astype(BF16)
-    values = projected[2 * WIDTH :].astype(BF16)
+    projected = dot(weights[0][layer][:, :EXTENDED], jnp.concatenate([normed, ones(16)], axis=0))
+    yield
+    return xhat, spread_one, normed, projected.astype(BF16)
+
+
+def forward_layer(layer, hidden, projected, segments, masks, weights, columns, power_ref, mixed_ref, scale_ref):
+    unused, out_t, up_t, unused = weights
+    column = lambda which: both(columns[layer, which])
+    query, keys, values = (projected[part * WIDTH : (part + 1) * WIDTH] for part in range(3))
     yield from attention_forward(query, keys, values, segments, masks, power_ref, mixed_ref, scale_ref)
     mixed = mixed_ref[...]
     middle = hidden + dot(out_t[layer][:, :EXTENDED], jnp.concatenate([mixed.astype(BF16), ones(16)], axis=0))
@@ -235,20 +241,29 @@
     yield
     inner = dot(up_t[layer][:, :EXTENDED], jnp.concatenate([normed_two, ones(16)], axis=0))
     yield
-    logit = inner[FF : FF + 1]
-    gate = jax.nn.sigmoid(logit)
+    gate = jax.nn.sigmoid(inner[FF : FF + 1])
+    return middle, inner[:FF], mixed, xhat_two, spread_two, normed_two, gate
+
+
+def gated_unit(inner, gate):
+    gated = inner * gate
+    return gated, 1.0 + jnp.tanh(gated * (GELU_A + (GELU_A * GELU_B) * (gated * gated)))
+
+
+def feed_forward(layer, middle, inner, gate, weights, columns, gated_ref, twice_ref):
     parts = []
     for start in range(0, FF, CHUNK):
-        gated = inner[start : start + CHUNK] * gate
-        twice_up = 1.0 + jnp.tanh(gated * (GELU_A + (GELU_A * GELU_B) * (gated * gated)))
-        gated_ref[start : start + CHUNK] = gated
-        twice_ref[start : start + CHUNK] = twice_up
+        rows = slice(start, start + CHUNK)
+        gated, twice_up = gated_unit(inner[rows], gate)
+        gated_ref[rows] = gated
+        twice_ref[rows] = twice_up
         parts.append((gated * twice_up).astype(BF16))
         yield
-    active = jnp.concatenate(parts, axis=0)
-    output = middle + (dot(down_t[layer], active) + column(DOWN_BIAS))
-    rows = jnp.concatenate([spread_one, spread_two, gate, jnp.zeros((5, LEN), F32)], axis=0)
-    return output, (normed, query, keys, values, mixed, xhat, xhat_two, normed_two, rows)
+    return feed_output(layer, middle, jnp.concatenate(parts, axis=0), weights, columns)
+
+
+def feed_output(layer, middle, active, weights, columns):
+    return middle + (dot(weights[3][layer], active) + both(columns[layer, DOWN_BIAS]))
 
 
 def norm_backward(gradient, xhat, scale, gain):
@@ -258,7 +273,7 @@
     return scale * (inner - first - xhat * second)
 
 
-def backward_unit(block, values_rows, query_variants, grad_variants, keys, deltas, power_ref, results, dq_ref):
+def backward_unit(block, values_rows, query_variants, grad_variants, keys, deltas, power_ref, results, dq_ref, turned_ref):
     first, last = WINDOWS[block]
     query_blocks = [head_block(query_variants, block, group) for group in range(2)]
     grad_blocks = [head_block(grad_variants, block, group) for group in range(2)]
@@ -284,7 +299,11 @@
         return jnp.concatenate([low, high], axis=1)
 
     grad_keys = dot(jnp.concatenate(grad_scores, axis=1), together_rows(query_blocks).T)
-    grad_values = dot(jnp.concatenate(powers, axis=1), together_rows(grad_blocks).T)
+    flipped = []
+    for group in range(2):
+        turned_ref[0 + 2 * block + group, :, : last - first] = powers[group].T
+        flipped.append(dot(grad_blocks[group], turned_ref[0 + 2 * block + group, :, : last - first]))
+    grad_values = jnp.concatenate(flipped, axis=0)
     results[block] = (grad_keys, grad_values, mixed)
     yield
     if block % 2 == 0:
@@ -299,7 +318,7 @@
             dq_ref[place : place + 16, lanes] = join_blocks(even[rows, tile], odd[rows, tile], head)
 
 
-def attention_backward(query, keys, values, mixed, scale, grad_mixed, masks, power_ref, dq_ref):
+def attention_backward(query, keys, values, mixed, scale, grad_mixed, masks, power_ref, dq_ref, turned_ref):
     factors = [scale[8 * head : 8 * head + 8] for head in range(HEADS)]
     grad = (grad_mixed * jnp.concatenate([row for factor in factors for row in (factor, factor)], axis=0)).astype(BF16)
     product = grad.astype(F32) * mixed
@@ -320,9 +339,17 @@
     yield
     results = {}
     yield from skewed(
-        backward_unit(block, rows, query_variants, grad_variants, keys, deltas, power_ref, results, dq_ref)
+        backward_unit(block, rows, query_variants, grad_variants, keys, deltas, power_ref, results, dq_ref, turned_ref)
         for block in range(4)
     )
+
+    def collect_lanes(which):
+        parts = [results[block][which] for block in range(4)]
+        gap = jnp.zeros((WIDTH, QUARTER), F32)
+        first = jnp.concatenate([parts[0], parts[3]], axis=1)
+        second = jnp.concatenate([parts[1], gap], axis=1)
+        third = jnp.concatenate([gap, parts[2]], axis=1)
+        return (first + second + third).astype(BF16)
 
     def collect(which):
         parts = [results[block][which] for block in range(4)]
@@ -336,11 +363,11 @@
             axis=0,
         ).astype(BF16)
 
-    return (dq_ref[...] * 0.25).astype(BF16), collect(0), collect(1)
+    return (dq_ref[...] * 0.25).astype(BF16), collect(0), collect_lanes(1).T
 
 
 def backward_layer(
-    layer, gradient, masks, kept, power_ref, scale_ref, gated_ref, twice_ref, raw, columns, totals, dq_ref
+    layer, gradient, masks, kept, power_ref, scale_ref, units, use_active, raw, columns, totals, dq_ref, turned_ref
 ):
     w_qkv, w_out, w_up, w_down = raw
     normed, query, keys, values, mixed, xhat, xhat_two, normed_two, rows = kept
@@ -355,8 +382,7 @@
     logit_sum = jnp.zeros((1, LEN), F32)
     for start in range(0, FF, CHUNK):
         rows = slice(start, start + CHUNK)
-        gated = gated_ref[rows]
-        twice_up = twice_ref[rows]
+        gated, twice_up = units(rows)
         active = gated * twice_up
         curve = GELU_A + (3.0 * GELU_A * GELU_B) * (gated * gated)
         slope = twice_up + (active * (2.0 - twice_up)) * curve
@@ -367,6 +393,7 @@
         yield
     grad_logit = logit_sum * (1.0 - gate)
     active = jnp.concatenate(actives, axis=0)
+    use_active(active)
     grad_inner = jnp.concatenate(inners, axis=0)
     grad_two = dot(w_up[layer], grad_inner) + column(GATE) * grad_logit
     down_total[...] += dot(branch, active.T)
@@ -381,7 +408,7 @@
     out_total[...] += dot(jnp.concatenate([mixed.astype(BF16), ones(16)], axis=0), attended.T)
     yield
     grad_query, grad_keys, grad_values = yield from attention_backward(
-        query, keys, values, mixed, scale_ref[...], grad_mixed, masks, power_ref, dq_ref
+        query, keys, values, mixed, scale_ref[...], grad_mixed, masks, power_ref, dq_ref, turned_ref
     )
     yield
     grad_rows = jnp.concatenate([grad_query.T, grad_keys, grad_values], axis=1)
@@ -457,9 +484,9 @@
 
 def kernel(
     per_step, steps,
-    x_ref, seg_ref, cot_ref, gains, shifts, w_qkv, qv_bias, w_out, out_bias, w_gate, w_up, up_bias, w_down, down_bias,
+    x_ref, x_next_ref, seg_ref, cot_ref, gains, shifts, w_qkv, qv_bias, w_out, out_bias, w_gate, w_up, up_bias, w_down, down_bias,
     result_ref, grad_inputs_ref, grads_ref,
-    columns, qkv_t, out_t, up_t, down_t, half_down, mixed_scratch, dq_ref, power_last, scale_last, gated_last, twice_last,
+    columns, qkv_t, out_t, up_t, down_t, half_down, mixed_scratch, dq_ref, turned_ref, power_last, scale_last,
     grad_kept, normed_kept, qkv_kept, mixed_kept, scale_kept, xhat_kept, xhat_two_kept, normed_two_kept, rows_kept,
     power_kept, gated_kept, twice_kept, *totals,
 ):
@@ -494,34 +521,52 @@
     weights = (qkv_t, out_t, up_t, down_t)
     raw = (w_qkv, w_out, w_up, half_down)
 
+    def ahead(item, ref, group):
+        place = group * per_step + item
+        hidden = ref[item * LEN : (item + 1) * LEN].astype(F32).T
+        xhat, spread_one, normed, projected = yield from project(0, hidden, weights, columns)
+        xhat_kept[place] = xhat
+        rows_kept[place, 0:1] = spread_one
+        normed_kept[place] = normed
+        qkv_kept[place] = projected
+
     def upward(item):
         tokens = slice(item * LEN, (item + 1) * LEN)
         place = step * per_step + item
         segments = segment_masks(seg_ref[pl.ds(place, 1)])
         hidden = x_ref[tokens].astype(F32).T
-        middle_hidden, kept = yield from forward_layer(
-            0, hidden, segments, masks, weights, columns, power_kept.at[place], mixed_scratch.at[item],
-            scale_kept.at[place], gated_kept.at[place], twice_kept.at[place],
+        middle, inner, mixed, xhat_two, spread_two, normed_two, gate = yield from forward_layer(
+            0, hidden, qkv_kept[place], segments, masks, weights, columns, power_kept.at[place], mixed_scratch.at[item],
+            scale_kept.at[place],
         )
-        normed, query, keys, values, mixed, xhat, xhat_two, normed_two, rows = kept
-        normed_kept[place] = normed
-        qkv_kept[place, :WIDTH] = query
-        qkv_kept[place, WIDTH : 2 * WIDTH] = keys
-        qkv_kept[place, 2 * WIDTH :] = values
         mixed_kept[place] = mixed
-        xhat_kept[place] = xhat
         xhat_two_kept[place] = xhat_two
         normed_two_kept[place] = normed_two
-        rows_kept[place] = rows
-        output, kept = yield from forward_layer(
-            1, middle_hidden, segments, masks, weights, columns, power_last.at[item], mixed_scratch.at[item],
-            scale_last.at[item], gated_last.at[item], twice_last.at[item],
+        rows_kept[place, 1:2] = spread_two
+        rows_kept[place, 2:3] = gate
+        hidden = yield from feed_forward(
+            0, middle, inner, gate, weights, columns, gated_kept.at[place], twice_kept.at[place]
         )
-        result_ref[tokens] = output.T.astype(BF16)
+        xhat, spread_one, normed, projected = yield from project(1, hidden, weights, columns)
+        middle, inner, mixed, xhat_two, spread_two, normed_two, gate = yield from forward_layer(
+            1, hidden, projected, segments, masks, weights, columns, power_last.at[item], mixed_scratch.at[item],
+            scale_last.at[item],
+        )
+        kept = (
+            normed, projected[:WIDTH], projected[WIDTH : 2 * WIDTH], projected[2 * WIDTH :], mixed, xhat, xhat_two,
+            normed_two, jnp.concatenate([spread_one, spread_two, gate], axis=0),
+        )
+
+        def last_units(rows):
+            return gated_unit(inner[rows], gate)
+
+        def write_result(active):
+            result_ref[tokens] = feed_output(1, middle, active, weights, columns).T.astype(BF16)
+
         gradient = cot_ref[tokens].astype(F32).T
         grad_kept[place] = yield from backward_layer(
-            1, gradient, masks, kept, power_last.at[item], scale_last.at[item], gated_last.at[item],
-            twice_last.at[item], raw, columns, totals_one, dq_ref.at[item],
+            1, gradient, masks, kept, power_last.at[item], scale_last.at[item], last_units, write_result, raw, columns,
+            totals_one, dq_ref.at[item], turned_ref.at[item],
         )
 
     def downward(item):
@@ -533,14 +578,24 @@
             normed_two_kept[place], rows_kept[place],
         )
         gradient = yield from backward_layer(
-            0, grad_kept[place], masks, kept, power_kept.at[place], scale_kept.at[place], gated_kept.at[place],
-            twice_kept.at[place], raw, columns, totals_zero, dq_ref.at[item],
+            0, grad_kept[place], masks, kept, power_kept.at[place], scale_kept.at[place],
+            lambda rows: (gated_kept[place, rows], twice_kept[place, rows]), lambda active: None, raw, columns,
+            totals_zero, dq_ref.at[item], turned_ref.at[item],
         )
         grad_inputs_ref[tokens] = gradient.T
 
+    @pl.when(step == 0)
+    def begin():
+        together([ahead(item, x_ref, 0) for item in range(per_step)])
+
     @pl.when(step < steps)
     def first_half():
-        together([upward(item) for item in range(per_step)])
+        following = lax.rem(step + 1, steps)
+        together(
+            [upward(item) for item in range(per_step)],
+            [ahead(item, x_next_ref, following) for item in range(per_step)],
+            AHEAD,
+        )
 
     @pl.when(step >= steps)
     def second_half():
@@ -583,6 +638,7 @@
         grid=(2 * steps,),
         in_specs=[
             pl.BlockSpec(rows, lambda i: (jnp.minimum(i, steps - 1), 0)),
+            pl.BlockSpec(rows, lambda i: (jnp.minimum(i + 1, steps) % steps, 0)),
             whole(segment_ids),
             pl.BlockSpec(rows, lambda i: (jnp.minimum(i, steps - 1), 0)),
         ]
@@ -606,10 +662,9 @@
             pltpu.VMEM((LAYERS, FF, WIDTH), BF16),
             kept(WIDTH, F32, per_step),
             kept(WIDTH, F32, per_step),
+            pltpu.VMEM((per_step, 8, LEN, LEN), BF16),
             kept(POWER_ROWS, BF16, per_step),
             kept(8 * HEADS, F32, per_step),
-            kept(FF, F32, per_step),
-            kept(FF, F32, per_step),
             kept(WIDTH, F32),
             kept(WIDTH, BF16),
             kept(3 * WIDTH, BF16),
@@ -627,7 +682,7 @@
         + totals_scratch(),
         compiler_params=pltpu.CompilerParams(vmem_limit_bytes=60 * 1024 * 1024),
         name="layers",
-    )(inputs, segment_ids, cotangent, *parameters)
+    )(inputs, inputs, segment_ids, cotangent, *parameters)
 
 
 def unpack_kernel(

time: 97.4 us -> 96.2 us (0.988)
  Pallas kernels: 59.3 us -> 58.2 us
    pallas_call x1, Pallas kernels: 57.7 us -> 56.5 us  [local_part(): pl.pallas_call(lambda *refs: kernel(per_step, steps, *refs), grid=(2 * st...]
where the time goes in v4:
time: 96.2 us; the launch traced here: 96 us
  Pallas kernels  58.2 us (60%)
  waiting for transfers between devices  22.8 us (24%)
  starting transfers between devices  12.9 us (13%)
  local copies, waits for them, and re-layouts  1.23 us (1%)
    pallas_call x1, Pallas kernels, local_part(): pl.pallas_call(lambda *refs: kernel(per_step, steps, *refs), grid=(2 * st...  56.5 us
    ppermute x10, waiting for transfers between devices, swap(): return lax.ppermute(value, 'seq', [(i, i ^ mask) for i in range(size)])  22.8 us
    ppermute x10, starting transfers between devices, swap(): return lax.ppermute(value, 'seq', [(i, i ^ mask) for i in range(size)])  12.9 us
  transfers between devices with their start and end apart: 10, of which 9 were waited for; matrix products, arithmetic and copies ran while one was open for 0% of the time, Pallas kernels for 0%

profile of v4, /device:TPU:0, one launch (start us, length us, event | category | flops | bytes accessed | tf_op | source)
XLA Modules:
  0.0 96.0 jit_solution(5899530484532027089)
XLA Ops:
  0.7 56.5 %layers.1 = (bf16[4096,128]{1,0:T(8,128)(2,1)}, f32[4096,128]{1,0:T(8,128)}, f32[2,1056,128]{2,1,0:T(8,128)}) custom-call(bf16[4096,128]{1,0:T(8,128)(2,1)} %refs_1_.1, bf16[4096,128]{1,0:T(8,128)(2,1)} %refs_1_.1, s32[16,256]{1,0:T(8,128)} %refs_2_.1, bf16[4096,128]{1,0:T(8,128)(2,1)} %refs_3_.1, f32[2,2,128]{2,1,0:T(2,128)} %refs_4_.1, ...), custom_call_target="tpu_custom_call" | custom-call | tf_op jit(solution)/shard_map/layers/pallas_call | solution.py:636
  57.2 0.0 copy-start
  57.2 1.2 %dynamic-slice_bitcast_fusion = f32[1056,128]{1,0:T(8,128)S(1)} fusion(f32[2,1056,128]{2,1,0:T(8,128)} %get-tuple-element.29, s32[]{:T(128)S(6)} %select_n.21), kind=kLoop, calls=%fused_computation.2 | loop fusion | bytes 1081348 | tf_op jit(solution)/shard_map/jit(dynamic_index_in_dim)/squeeze | solution.py:746
  58.4 0.5 collective-permute-start
  58.9 1.6 %collective-permute-done = f32[1056,128]{1,0:T(8,128)S(1)} collective-permute-done((f32[1056,128]{1,0:T(8,128)S(1)}, f32[1056,128]{1,0:T(8,128)S(1)}, u32[]{:S(2)}, u32[]{:S(2)}) %collective-permute-start) | collective-permute-done | bytes 540704 | tf_op jit(solution)/shard_map/ppermute | solution.py:743
  60.5 0.0 copy-done
  60.5 0.1 bitcast_add_fusion
  60.6 2.9 %collective-permute-start.1 = (f32[264,128]{1,0:T(8,128)S(1)}, f32[264,128]{1,0:T(8,128)S(1)}, u32[]{:S(2)}, u32[]{:S(2)}) collective-permute-start(f32[264,128]{1,0:T(8,128)S(1)} %get-tuple-element.41), channel_id=1, source_target_pairs={{0,2},{1,3},{2,0},{3,1},{4,6},{5,7},{6,4},{7,5},{8,10},{9,11},{10,... | collective-permute-start | bytes 405512 | tf_op jit(solution)/shard_map/ppermute | solution.py:743
  63.5 1.5 %collective-permute-start.2 = (f32[264,128]{1,0:T(8,128)S(1)}, f32[264,128]{1,0:T(8,128)S(1)}, u32[]{:S(2)}, u32[]{:S(2)}) collective-permute-start(f32[264,128]{1,0:T(8,128)S(1)} %get-tuple-element.43), channel_id=1, source_target_pairs={{0,4},{1,5},{2,6},{3,7},{4,0},{5,1},{6,2},{7,3},{8,12},{9,13},{10,... | collective-permute-start | bytes 405512 | tf_op jit(solution)/shard_map/ppermute | solution.py:743
  65.0 0.0 collective-permute-start.3
  65.1 2.5 %collective-permute-done.1 = f32[264,128]{1,0:T(8,128)S(1)} collective-permute-done((f32[264,128]{1,0:T(8,128)S(1)}, f32[264,128]{1,0:T(8,128)S(1)}, u32[]{:S(2)}, u32[]{:S(2)}) %collective-permute-start.1) | collective-permute-done | bytes 135200 | tf_op jit(solution)/shard_map/ppermute | solution.py:743
  67.6 4.2 %collective-permute-done.2 = f32[264,128]{1,0:T(8,128)S(1)} collective-permute-done((f32[264,128]{1,0:T(8,128)S(1)}, f32[264,128]{1,0:T(8,128)S(1)}, u32[]{:S(2)}, u32[]{:S(2)}) %collective-permute-start.2) | collective-permute-done | bytes 135200 | tf_op jit(solution)/shard_map/ppermute | solution.py:743
  71.8 0.0 collective-permute-done.3
  71.8 1.6 %collective-permute-start.4 = (f32[264,128]{1,0:T(8,128)S(1)}, f32[264,128]{1,0:T(8,128)S(1)}, u32[]{:S(2)}, u32[]{:S(2)}) collective-permute-start(f32[264,128]{1,0:T(8,128)S(1)} %fusion.1), channel_id=1, source_target_pairs={{0,8},{1,9},{2,10},{3,11},{4,12},{5,13},{6,14},{7,15},{8,0},{9,1},... | collective-permute-start | bytes 405512 | tf_op jit(solution)/shard_map/ppermute | solution.py:743
  73.4 3.4 %collective-permute-done.4 = f32[264,128]{1,0:T(8,128)S(1)} collective-permute-done((f32[264,128]{1,0:T(8,128)S(1)}, f32[264,128]{1,0:T(8,128)S(1)}, u32[]{:S(2)}, u32[]{:S(2)}) %collective-permute-start.4) | collective-permute-done | bytes 135200 | tf_op jit(solution)/shard_map/ppermute | solution.py:743
  76.9 2.6 %collective-permute-start.5 = (f32[264,128]{1,0:T(8,128)S(1)}, f32[264,128]{1,0:T(8,128)S(1)}, u32[]{:S(2)}, u32[]{:S(2)}) collective-permute-start(f32[264,128]{1,0:T(8,128)S(1)} %add.49), channel_id=1, source_target_pairs={{0,16},{1,17},{2,18},{3,19},{4,20},{5,21},{6,22},{7,23},{8,24},{9,... | collective-permute-start | bytes 405512 | tf_op jit(solution)/shard_map/ppermute | solution.py:743
  79.5 4.8 %collective-permute-done.5 = f32[264,128]{1,0:T(8,128)S(1)} collective-permute-done((f32[264,128]{1,0:T(8,128)S(1)}, f32[264,128]{1,0:T(8,128)S(1)}, u32[]{:S(2)}, u32[]{:S(2)}) %collective-permute-start.5) | collective-permute-done | bytes 135200 | tf_op jit(solution)/shard_map/ppermute | solution.py:743
  84.3 1.4 %collective-permute-start.6 = (f32[264,128]{1,0:T(8,128)S(1)}, f32[264,128]{1,0:T(8,128)S(1)}, u32[]{:S(2)}, u32[]{:S(2)}) collective-permute-start(f32[264,128]{1,0:T(8,128)S(1)} %add.50), channel_id=1, source_target_pairs={{0,2},{1,3},{2,0},{3,1},{4,6},{5,7},{6,4},{7,5},{8,10},{9,11},{10,... | collective-permute-start | bytes 405512 | tf_op jit(solution)/shard_map/ppermute | solution.py:743
  85.7 0.7 collective-permute-start.7
  86.5 1.4 %collective-permute-start.8 = (f32[264,128]{1,0:T(8,128)S(1)}, f32[264,128]{1,0:T(8,128)S(1)}, u32[]{:S(2)}, u32[]{:S(2)}) collective-permute-start(f32[264,128]{1,0:T(8,128)S(1)} %add.50), channel_id=1, source_target_pairs={{0,6},{1,7},{2,4},{3,5},{4,2},{5,3},{6,0},{7,1},{8,14},{9,15},{10,... | collective-permute-start | bytes 405512 | tf_op jit(solution)/shard_map/ppermute | solution.py:743
  87.9 1.5 %collective-permute-done.6 = f32[264,128]{1,0:T(8,128)S(1)} collective-permute-done((f32[264,128]{1,0:T(8,128)S(1)}, f32[264,128]{1,0:T(8,128)S(1)}, u32[]{:S(2)}, u32[]{:S(2)}) %collective-permute-start.6) | collective-permute-done | bytes 135200 | tf_op jit(solution)/shard_map/ppermute | solution.py:743
  89.4 1.3 %collective-permute-done.7 = f32[264,128]{1,0:T(8,128)S(1)} collective-permute-done((f32[264,128]{1,0:T(8,128)S(1)}, f32[264,128]{1,0:T(8,128)S(1)}, u32[]{:S(2)}, u32[]{:S(2)}) %collective-permute-start.7) | collective-permute-done | bytes 135200 | tf_op jit(solution)/shard_map/ppermute | solution.py:743
  90.7 1.6 %collective-permute-done.8 = f32[264,128]{1,0:T(8,128)S(1)} collective-permute-done((f32[264,128]{1,0:T(8,128)S(1)}, f32[264,128]{1,0:T(8,128)S(1)}, u32[]{:S(2)}, u32[]{:S(2)}) %collective-permute-start.8) | collective-permute-done | bytes 135200 | tf_op jit(solution)/shard_map/ppermute | solution.py:743
  92.4 0.1 collective-permute-start.9
  92.5 0.1 pad_add_fusion.where_ref
  92.6 1.8 %collective-permute-done.9.far_ref = f32[1056,128]{1,0:T(8,128)S(1)} collective-permute-done((f32[1056,128]{1,0:T(8,128)S(1)}, f32[1056,128]{1,0:T(8,128)S(1)}, u32[]{:S(2)}, u32[]{:S(2)}) %collective-permute-start.9) | collective-permute-done | bytes 540704 | tf_op jit(solution)/shard_map/ppermute | solution.py:743
  94.4 1.6 %unpack.1 = (f32[2,2,128]{2,1,0:T(2,128)}, f32[2,2,128]{2,1,0:T(2,128)}, f32[2,128,384]{2,1,0:T(8,128)}, f32[2,256]{1,0:T(2,128)}, f32[2,128,128]{2,1,0:T(8,128)...) custom-call(s32[2]{0:T(128)S(1)} %pad_add_fusion.where_ref, ...), custom_call_target="tpu_custom_call" | custom-call | tf_op jit(solution)/shard_map/unpack/pallas_call | solution.py:727
  (5 shorter events, 0.2 us)
Async XLA Ops:
  57.2 3.3 %copy-start = (f32[2,1056,128]{2,1,0:T(8,128)S(1)}, f32[2,1056,128]{2,1,0:T(8,128)}, u32[]{:S(2)}) copy-start(f32[2,1056,128]{2,1,0:T(8,128)} %get-tuple-element.29) | copy-start | bytes 3244036
  58.4 2.1 %collective-permute-start = (f32[1056,128]{1,0:T(8,128)S(1)}, f32[1056,128]{1,0:T(8,128)S(1)}, u32[]{:S(2)}, u32[]{:S(2)}) collective-permute-start(f32[1056,128]{1,0:T(8,128)S(1)} %dynamic-slice_bitcast_fusion), channel_id=1, source_target_pairs={{0,1},{1,0},{2,3},{3,2},{4,5},{5,4},{6,7},{7,6},{8,9},{9,8},{10,11... | collective-permute-start | bytes 1622024 | tf_op jit(solution)/shard_map/ppermute | solution.py:743
  60.6 7.0 %collective-permute-start.1 = (f32[264,128]{1,0:T(8,128)S(1)}, f32[264,128]{1,0:T(8,128)S(1)}, u32[]{:S(2)}, u32[]{:S(2)}) collective-permute-start(f32[264,128]{1,0:T(8,128)S(1)} %get-tuple-element.41), channel_id=1, source_target_pairs={{0,2},{1,3},{2,0},{3,1},{4,6},{5,7},{6,4},{7,5},{8,10},{9,11},{10,... | collective-permute-start | bytes 405512 | tf_op jit(solution)/shard_map/ppermute | solution.py:743
  63.5 8.2 %collective-permute-start.2 = (f32[264,128]{1,0:T(8,128)S(1)}, f32[264,128]{1,0:T(8,128)S(1)}, u32[]{:S(2)}, u32[]{:S(2)}) collective-permute-start(f32[264,128]{1,0:T(8,128)S(1)} %get-tuple-element.43), channel_id=1, source_target_pairs={{0,4},{1,5},{2,6},{3,7},{4,0},{5,1},{6,2},{7,3},{8,12},{9,13},{10,... | collective-permute-start | bytes 405512 | tf_op jit(solution)/shard_map/ppermute | solution.py:743
  65.0 6.7 %collective-permute-start.3 = (f32[264,128]{1,0:T(8,128)S(1)}, f32[264,128]{1,0:T(8,128)S(1)}, u32[]{:S(2)}, u32[]{:S(2)}) collective-permute-start(f32[264,128]{1,0:T(8,128)S(1)} %get-tuple-element.42), channel_id=1, source_target_pairs={{0,6},{1,7},{2,4},{3,5},{4,2},{5,3},{6,0},{7,1},{8,14},{9,15},{10,... | collective-permute-start | bytes 405512 | tf_op jit(solution)/shard_map/ppermute | solution.py:743
  71.8 5.1 %collective-permute-start.4 = (f32[264,128]{1,0:T(8,128)S(1)}, f32[264,128]{1,0:T(8,128)S(1)}, u32[]{:S(2)}, u32[]{:S(2)}) collective-permute-start(f32[264,128]{1,0:T(8,128)S(1)} %fusion.1), channel_id=1, source_target_pairs={{0,8},{1,9},{2,10},{3,11},{4,12},{5,13},{6,14},{7,15},{8,0},{9,1},... | collective-permute-start | bytes 405512 | tf_op jit(solution)/shard_map/ppermute | solution.py:743
  76.9 7.4 %collective-permute-start.5 = (f32[264,128]{1,0:T(8,128)S(1)}, f32[264,128]{1,0:T(8,128)S(1)}, u32[]{:S(2)}, u32[]{:S(2)}) collective-permute-start(f32[264,128]{1,0:T(8,128)S(1)} %add.49), channel_id=1, source_target_pairs={{0,16},{1,17},{2,18},{3,19},{4,20},{5,21},{6,22},{7,23},{8,24},{9,... | collective-permute-start | bytes 405512 | tf_op jit(solution)/shard_map/ppermute | solution.py:743
  84.3 5.1 %collective-permute-start.6 = (f32[264,128]{1,0:T(8,128)S(1)}, f32[264,128]{1,0:T(8,128)S(1)}, u32[]{:S(2)}, u32[]{:S(2)}) collective-permute-start(f32[264,128]{1,0:T(8,128)S(1)} %add.50), channel_id=1, source_target_pairs={{0,2},{1,3},{2,0},{3,1},{4,6},{5,7},{6,4},{7,5},{8,10},{9,11},{10,... | collective-permute-start | bytes 405512 | tf_op jit(solution)/shard_map/ppermute | solution.py:743
  85.7 5.0 %collective-permute-start.7 = (f32[264,128]{1,0:T(8,128)S(1)}, f32[264,128]{1,0:T(8,128)S(1)}, u32[]{:S(2)}, u32[]{:S(2)}) collective-permute-start(f32[264,128]{1,0:T(8,128)S(1)} %add.50), channel_id=1, source_target_pairs={{0,4},{1,5},{2,6},{3,7},{4,0},{5,1},{6,2},{7,3},{8,12},{9,13},{10,... | collective-permute-start | bytes 405512 | tf_op jit(solution)/shard_map/ppermute | solution.py:743
  86.5 5.9 %collective-permute-start.8 = (f32[264,128]{1,0:T(8,128)S(1)}, f32[264,128]{1,0:T(8,128)S(1)}, u32[]{:S(2)}, u32[]{:S(2)}) collective-permute-start(f32[264,128]{1,0:T(8,128)S(1)} %add.50), channel_id=1, source_target_pairs={{0,6},{1,7},{2,4},{3,5},{4,2},{5,3},{6,0},{7,1},{8,14},{9,15},{10,... | collective-permute-start | bytes 405512 | tf_op jit(solution)/shard_map/ppermute | solution.py:743
  92.4 2.0 %collective-permute-start.9 = (f32[1056,128]{1,0:T(8,128)S(1)}, f32[1056,128]{1,0:T(8,128)S(1)}, u32[]{:S(2)}, u32[]{:S(2)}) collective-permute-start(f32[1056,128]{1,0:T(8,128)S(1)} %pad_maximum_fusion.near_ref), channel_id=1, source_target_pairs={{0,1},{1,0},{2,3},{3,2},{4,5},{5,4},{6,7},{7,6},{8,9},{9,8},{10,11... | collective-permute-start | bytes 1622024 | tf_op jit(solution)/shard_map/ppermute | solution.py:743

commit v5 on v4

--- a/solution.py
+++ b/solution.py
@@ -646,12 +646,12 @@
         out_specs=[
             pl.BlockSpec(rows, lambda i: (jnp.minimum(i, steps - 1), 0)),
             pl.BlockSpec(rows, lambda i: (jnp.maximum(i - steps, 0), 0)),
-            pl.BlockSpec((LAYERS, ROWS, WIDTH), lambda i: (0, 0, 0)),
+            pl.BlockSpec(memory_space=pltpu.VMEM),
         ],
         out_shape=[
             jax.ShapeDtypeStruct(inputs.shape, BF16),
             jax.ShapeDtypeStruct(inputs.shape, F32),
-            jax.ShapeDtypeStruct((LAYERS, ROWS, WIDTH), F32),
+            pltpu.VMEM((LAYERS, ROWS, WIDTH), F32),
         ],
         scratch_shapes=[
             pltpu.VMEM((LAYERS, COLUMNS, WIDTH, WIDTH), F32),

time: 96.2 us -> 94.6 us (0.983)
  local copies, waits for them, and re-layouts: 1.23 us -> 0.08 us
    squeeze x2, local copies, waits for them, and re-layouts: 1.22 us -> 0.08 us  [pick(): return lax.dynamic_index_in_dim(value, index, 0, keepdims=False)]
where the time goes in v5:
time: 94.6 us; the launch traced here: 94.5 us
  Pallas kernels  57.8 us (61%)
  waiting for transfers between devices  22.8 us (24%)
  starting transfers between devices  12.9 us (14%)
    pallas_call x1, Pallas kernels, local_part(): pl.pallas_call(lambda *refs: kernel(per_step, steps, *refs), grid=(2 * st...  56.2 us
    ppermute x10, waiting for transfers between devices, swap(): return lax.ppermute(value, 'seq', [(i, i ^ mask) for i in range(size)])  22.8 us
    ppermute x10, starting transfers between devices, swap(): return lax.ppermute(value, 'seq', [(i, i ^ mask) for i in range(size)])  12.9 us
  transfers between devices with their start and end apart: 10, of which 9 were waited for; matrix products, arithmetic and copies ran while one was open for 0% of the time, Pallas kernels for 0%

profile of v5, /device:TPU:0, one launch (start us, length us, event | category | flops | bytes accessed | tf_op | source)
XLA Modules:
  0.0 94.5 jit_solution(17545267487553495591)
XLA Ops:
  0.7 56.2 %layers.1 = (bf16[4096,128]{1,0:T(8,128)(2,1)}, f32[4096,128]{1,0:T(8,128)}, f32[2,1056,128]{2,1,0:T(8,128)S(1)}) custom-call(bf16[4096,128]{1,0:T(8,128)(2,1)} %refs_1_.1, bf16[4096,128]{1,0:T(8,128)(2,1)} %refs_1_.1, s32[16,256]{1,0:T(8,128)} %refs_2_.1, bf16[4096,128]{1,0:T(8,128)(2,1)} %refs_3_.1, f32[2,2,128]{2,1,0:T(2,128)} %refs_4_.1, ...), custom_call_target="tpu_custom_call" | custom-call | tf_op jit(solution)/shard_map/layers/pallas_call | solution.py:636
  56.8 0.5 collective-permute-start
  57.4 1.6 %collective-permute-done = f32[1056,128]{1,0:T(8,128)S(1)} collective-permute-done((f32[1056,128]{1,0:T(8,128)S(1)}, f32[1056,128]{1,0:T(8,128)S(1)}, u32[]{:S(2)}, u32[]{:S(2)}) %collective-permute-start) | collective-permute-done | bytes 540704 | tf_op jit(solution)/shard_map/ppermute | solution.py:743
  58.9 0.1 bitcast_add_fusion
  59.0 2.9 %collective-permute-start.1 = (f32[264,128]{1,0:T(8,128)S(1)}, f32[264,128]{1,0:T(8,128)S(1)}, u32[]{:S(2)}, u32[]{:S(2)}) collective-permute-start(f32[264,128]{1,0:T(8,128)S(1)} %get-tuple-element.41), channel_id=1, source_target_pairs={{0,2},{1,3},{2,0},{3,1},{4,6},{5,7},{6,4},{7,5},{8,10},{9,11},{10,... | collective-permute-start | bytes 405512 | tf_op jit(solution)/shard_map/ppermute | solution.py:743
  62.0 1.5 %collective-permute-start.2 = (f32[264,128]{1,0:T(8,128)S(1)}, f32[264,128]{1,0:T(8,128)S(1)}, u32[]{:S(2)}, u32[]{:S(2)}) collective-permute-start(f32[264,128]{1,0:T(8,128)S(1)} %get-tuple-element.43), channel_id=1, source_target_pairs={{0,4},{1,5},{2,6},{3,7},{4,0},{5,1},{6,2},{7,3},{8,12},{9,13},{10,... | collective-permute-start | bytes 405512 | tf_op jit(solution)/shard_map/ppermute | solution.py:743
  63.5 0.0 collective-permute-start.3
  63.5 2.5 %collective-permute-done.1 = f32[264,128]{1,0:T(8,128)S(1)} collective-permute-done((f32[264,128]{1,0:T(8,128)S(1)}, f32[264,128]{1,0:T(8,128)S(1)}, u32[]{:S(2)}, u32[]{:S(2)}) %collective-permute-start.1) | collective-permute-done | bytes 135200 | tf_op jit(solution)/shard_map/ppermute | solution.py:743
  66.0 4.2 %collective-permute-done.2 = f32[264,128]{1,0:T(8,128)S(1)} collective-permute-done((f32[264,128]{1,0:T(8,128)S(1)}, f32[264,128]{1,0:T(8,128)S(1)}, u32[]{:S(2)}, u32[]{:S(2)}) %collective-permute-start.2) | collective-permute-done | bytes 135200 | tf_op jit(solution)/shard_map/ppermute | solution.py:743
  70.2 0.0 collective-permute-done.3
  70.2 1.6 %collective-permute-start.4 = (f32[264,128]{1,0:T(8,128)S(1)}, f32[264,128]{1,0:T(8,128)S(1)}, u32[]{:S(2)}, u32[]{:S(2)}) collective-permute-start(f32[264,128]{1,0:T(8,128)S(1)} %fusion.1), channel_id=1, source_target_pairs={{0,8},{1,9},{2,10},{3,11},{4,12},{5,13},{6,14},{7,15},{8,0},{9,1},... | collective-permute-start | bytes 405512 | tf_op jit(solution)/shard_map/ppermute | solution.py:743
  71.9 3.4 %collective-permute-done.4 = f32[264,128]{1,0:T(8,128)S(1)} collective-permute-done((f32[264,128]{1,0:T(8,128)S(1)}, f32[264,128]{1,0:T(8,128)S(1)}, u32[]{:S(2)}, u32[]{:S(2)}) %collective-permute-start.4) | collective-permute-done | bytes 135200 | tf_op jit(solution)/shard_map/ppermute | solution.py:743
  75.3 2.7 %collective-permute-start.5 = (f32[264,128]{1,0:T(8,128)S(1)}, f32[264,128]{1,0:T(8,128)S(1)}, u32[]{:S(2)}, u32[]{:S(2)}) collective-permute-start(f32[264,128]{1,0:T(8,128)S(1)} %add.49), channel_id=1, source_target_pairs={{0,16},{1,17},{2,18},{3,19},{4,20},{5,21},{6,22},{7,23},{8,24},{9,... | collective-permute-start | bytes 405512 | tf_op jit(solution)/shard_map/ppermute | solution.py:743
  78.0 4.8 %collective-permute-done.5 = f32[264,128]{1,0:T(8,128)S(1)} collective-permute-done((f32[264,128]{1,0:T(8,128)S(1)}, f32[264,128]{1,0:T(8,128)S(1)}, u32[]{:S(2)}, u32[]{:S(2)}) %collective-permute-start.5) | collective-permute-done | bytes 135200 | tf_op jit(solution)/shard_map/ppermute | solution.py:743
  82.8 1.4 %collective-permute-start.6 = (f32[264,128]{1,0:T(8,128)S(1)}, f32[264,128]{1,0:T(8,128)S(1)}, u32[]{:S(2)}, u32[]{:S(2)}) collective-permute-start(f32[264,128]{1,0:T(8,128)S(1)} %add.50), channel_id=1, source_target_pairs={{0,2},{1,3},{2,0},{3,1},{4,6},{5,7},{6,4},{7,5},{8,10},{9,11},{10,... | collective-permute-start | bytes 405512 | tf_op jit(solution)/shard_map/ppermute | solution.py:743
  84.2 0.7 collective-permute-start.7
  84.9 1.4 %collective-permute-start.8 = (f32[264,128]{1,0:T(8,128)S(1)}, f32[264,128]{1,0:T(8,128)S(1)}, u32[]{:S(2)}, u32[]{:S(2)}) collective-permute-start(f32[264,128]{1,0:T(8,128)S(1)} %add.50), channel_id=1, source_target_pairs={{0,6},{1,7},{2,4},{3,5},{4,2},{5,3},{6,0},{7,1},{8,14},{9,15},{10,... | collective-permute-start | bytes 405512 | tf_op jit(solution)/shard_map/ppermute | solution.py:743
  86.3 1.5 %collective-permute-done.6 = f32[264,128]{1,0:T(8,128)S(1)} collective-permute-done((f32[264,128]{1,0:T(8,128)S(1)}, f32[264,128]{1,0:T(8,128)S(1)}, u32[]{:S(2)}, u32[]{:S(2)}) %collective-permute-start.6) | collective-permute-done | bytes 135200 | tf_op jit(solution)/shard_map/ppermute | solution.py:743
  87.9 1.3 %collective-permute-done.7 = f32[264,128]{1,0:T(8,128)S(1)} collective-permute-done((f32[264,128]{1,0:T(8,128)S(1)}, f32[264,128]{1,0:T(8,128)S(1)}, u32[]{:S(2)}, u32[]{:S(2)}) %collective-permute-start.7) | collective-permute-done | bytes 135200 | tf_op jit(solution)/shard_map/ppermute | solution.py:743
  89.2 1.6 %collective-permute-done.8 = f32[264,128]{1,0:T(8,128)S(1)} collective-permute-done((f32[264,128]{1,0:T(8,128)S(1)}, f32[264,128]{1,0:T(8,128)S(1)}, u32[]{:S(2)}, u32[]{:S(2)}) %collective-permute-start.8) | collective-permute-done | bytes 135200 | tf_op jit(solution)/shard_map/ppermute | solution.py:743
  90.9 0.1 collective-permute-start.9
  90.9 0.1 pad_add_fusion.where_ref
  91.0 1.8 %collective-permute-done.9.far_ref = f32[1056,128]{1,0:T(8,128)S(1)} collective-permute-done((f32[1056,128]{1,0:T(8,128)S(1)}, f32[1056,128]{1,0:T(8,128)S(1)}, u32[]{:S(2)}, u32[]{:S(2)}) %collective-permute-start.9) | collective-permute-done | bytes 540704 | tf_op jit(solution)/shard_map/ppermute | solution.py:743
  92.9 1.6 %unpack.1 = (f32[2,2,128]{2,1,0:T(2,128)}, f32[2,2,128]{2,1,0:T(2,128)}, f32[2,128,384]{2,1,0:T(8,128)}, f32[2,256]{1,0:T(2,128)}, f32[2,128,128]{2,1,0:T(8,128)...) custom-call(s32[2]{0:T(128)S(1)} %pad_add_fusion.where_ref, ...), custom_call_target="tpu_custom_call" | custom-call | tf_op jit(solution)/shard_map/unpack/pallas_call | solution.py:727
  (6 shorter events, 0.2 us)
Async XLA Ops:
  56.8 2.1 %collective-permute-start = (f32[1056,128]{1,0:T(8,128)S(1)}, f32[1056,128]{1,0:T(8,128)S(1)}, u32[]{:S(2)}, u32[]{:S(2)}) collective-permute-start(f32[1056,128]{1,0:T(8,128)S(1)} %dynamic-slice_bitcast_fusion), channel_id=1, source_target_pairs={{0,1},{1,0},{2,3},{3,2},{4,5},{5,4},{6,7},{7,6},{8,9},{9,8},{10,11... | collective-permute-start | bytes 1622024 | tf_op jit(solution)/shard_map/ppermute | solution.py:743
  59.0 7.0 %collective-permute-start.1 = (f32[264,128]{1,0:T(8,128)S(1)}, f32[264,128]{1,0:T(8,128)S(1)}, u32[]{:S(2)}, u32[]{:S(2)}) collective-permute-start(f32[264,128]{1,0:T(8,128)S(1)} %get-tuple-element.41), channel_id=1, source_target_pairs={{0,2},{1,3},{2,0},{3,1},{4,6},{5,7},{6,4},{7,5},{8,10},{9,11},{10,... | collective-permute-start | bytes 405512 | tf_op jit(solution)/shard_map/ppermute | solution.py:743
  62.0 8.2 %collective-permute-start.2 = (f32[264,128]{1,0:T(8,128)S(1)}, f32[264,128]{1,0:T(8,128)S(1)}, u32[]{:S(2)}, u32[]{:S(2)}) collective-permute-start(f32[264,128]{1,0:T(8,128)S(1)} %get-tuple-element.43), channel_id=1, source_target_pairs={{0,4},{1,5},{2,6},{3,7},{4,0},{5,1},{6,2},{7,3},{8,12},{9,13},{10,... | collective-permute-start | bytes 405512 | tf_op jit(solution)/shard_map/ppermute | solution.py:743
  63.5 6.7 %collective-permute-start.3 = (f32[264,128]{1,0:T(8,128)S(1)}, f32[264,128]{1,0:T(8,128)S(1)}, u32[]{:S(2)}, u32[]{:S(2)}) collective-permute-start(f32[264,128]{1,0:T(8,128)S(1)} %get-tuple-element.42), channel_id=1, source_target_pairs={{0,6},{1,7},{2,4},{3,5},{4,2},{5,3},{6,0},{7,1},{8,14},{9,15},{10,... | collective-permute-start | bytes 405512 | tf_op jit(solution)/shard_map/ppermute | solution.py:743
  70.2 5.1 %collective-permute-start.4 = (f32[264,128]{1,0:T(8,128)S(1)}, f32[264,128]{1,0:T(8,128)S(1)}, u32[]{:S(2)}, u32[]{:S(2)}) collective-permute-start(f32[264,128]{1,0:T(8,128)S(1)} %fusion.1), channel_id=1, source_target_pairs={{0,8},{1,9},{2,10},{3,11},{4,12},{5,13},{6,14},{7,15},{8,0},{9,1},... | collective-permute-start | bytes 405512 | tf_op jit(solution)/shard_map/ppermute | solution.py:743
  75.3 7.4 %collective-permute-start.5 = (f32[264,128]{1,0:T(8,128)S(1)}, f32[264,128]{1,0:T(8,128)S(1)}, u32[]{:S(2)}, u32[]{:S(2)}) collective-permute-start(f32[264,128]{1,0:T(8,128)S(1)} %add.49), channel_id=1, source_target_pairs={{0,16},{1,17},{2,18},{3,19},{4,20},{5,21},{6,22},{7,23},{8,24},{9,... | collective-permute-start | bytes 405512 | tf_op jit(solution)/shard_map/ppermute | solution.py:743
  82.8 5.1 %collective-permute-start.6 = (f32[264,128]{1,0:T(8,128)S(1)}, f32[264,128]{1,0:T(8,128)S(1)}, u32[]{:S(2)}, u32[]{:S(2)}) collective-permute-start(f32[264,128]{1,0:T(8,128)S(1)} %add.50), channel_id=1, source_target_pairs={{0,2},{1,3},{2,0},{3,1},{4,6},{5,7},{6,4},{7,5},{8,10},{9,11},{10,... | collective-permute-start | bytes 405512 | tf_op jit(solution)/shard_map/ppermute | solution.py:743
  84.2 5.0 %collective-permute-start.7 = (f32[264,128]{1,0:T(8,128)S(1)}, f32[264,128]{1,0:T(8,128)S(1)}, u32[]{:S(2)}, u32[]{:S(2)}) collective-permute-start(f32[264,128]{1,0:T(8,128)S(1)} %add.50), channel_id=1, source_target_pairs={{0,4},{1,5},{2,6},{3,7},{4,0},{5,1},{6,2},{7,3},{8,12},{9,13},{10,... | collective-permute-start | bytes 405512 | tf_op jit(solution)/shard_map/ppermute | solution.py:743
  84.9 5.9 %collective-permute-start.8 = (f32[264,128]{1,0:T(8,128)S(1)}, f32[264,128]{1,0:T(8,128)S(1)}, u32[]{:S(2)}, u32[]{:S(2)}) collective-permute-start(f32[264,128]{1,0:T(8,128)S(1)} %add.50), channel_id=1, source_target_pairs={{0,6},{1,7},{2,4},{3,5},{4,2},{5,3},{6,0},{7,1},{8,14},{9,15},{10,... | collective-permute-start | bytes 405512 | tf_op jit(solution)/shard_map/ppermute | solution.py:743
  90.9 2.0 %collective-permute-start.9 = (f32[1056,128]{1,0:T(8,128)S(1)}, f32[1056,128]{1,0:T(8,128)S(1)}, u32[]{:S(2)}, u32[]{:S(2)}) collective-permute-start(f32[1056,128]{1,0:T(8,128)S(1)} %pad_maximum_fusion.near_ref), channel_id=1, source_target_pairs={{0,1},{1,0},{2,3},{3,2},{4,5},{5,4},{6,7},{7,6},{8,9},{9,8},{10,11... | collective-permute-start | bytes 1622024 | tf_op jit(solution)/shard_map/ppermute | solution.py:743

commit v6 on v5

--- a/solution.py
+++ b/solution.py
@@ -686,18 +686,18 @@
 
 
 def unpack_kernel(
-    where_ref, near_ref, far_ref,
+    where_ref, near_zero, near_one, near_two, near_three, far_zero, far_one, far_two, far_three,
     gains_ref, shifts_ref, qkv_ref, qv_bias_ref, out_ref, out_bias_ref, gate_ref, up_ref, up_bias_ref, down_ref,
     down_bias_ref,
     grads,
 ):
     core, part = where_ref[0], where_ref[1]
     quarter = ROWS // 4
+    near, far = (near_zero, near_one, near_two, near_three), (far_zero, far_one, far_two, far_three)
     for mask in range(4):
         place = pl.ds(pl.multiple_of((part ^ mask) * quarter, 8), quarter)
-        rows = slice(mask * quarter, (mask + 1) * quarter)
-        grads[core, place] = near_ref[rows]
-        grads[1 - core, place] = far_ref[rows]
+        grads[core, place] = near[mask][...]
+        grads[1 - core, place] = far[mask][...]
     for layer in range(LAYERS):
         for part in range(3):
             lanes = slice(part * WIDTH, (part + 1) * WIDTH)
@@ -719,19 +719,19 @@
         up_bias_ref[one, :WIDTH], up_bias_ref[one, WIDTH:] = row(S_UP_LOW), row(S_UP_HIGH)
 
 
-def unpack(where, near, far):
+def unpack(where, *quarters):
     shapes = [
         (LAYERS, 2, WIDTH), (LAYERS, 2, WIDTH), (LAYERS, WIDTH, 3 * WIDTH), (LAYERS, 2 * WIDTH), (LAYERS, WIDTH, WIDTH),
         (LAYERS, WIDTH), (LAYERS, WIDTH), (LAYERS, WIDTH, FF), (LAYERS, FF), (LAYERS, FF, WIDTH), (LAYERS, WIDTH),
     ]
     return pl.pallas_call(
         unpack_kernel,
-        in_specs=[pl.BlockSpec(memory_space=pltpu.SMEM), pl.BlockSpec(), pl.BlockSpec()],
+        in_specs=[pl.BlockSpec(memory_space=pltpu.SMEM)] + [pl.BlockSpec()] * 8,
         out_shape=[jax.ShapeDtypeStruct(shape, F32) for shape in shapes],
         scratch_shapes=[pltpu.VMEM((LAYERS, ROWS, WIDTH), F32)],
         compiler_params=pltpu.CompilerParams(vmem_limit_bytes=16 * 1024 * 1024),
         name="unpack",
-    )(where, near, far)
+    )(where, *quarters)
 
 
 def all_sum(grads, size):
@@ -751,15 +751,15 @@
     mine = pick(quarters, part) + others[0] + others[1] + others[2]
     for bit in range(3, bits):
         mine = mine + swap(mine, 1 << bit)
-    near = jnp.concatenate([mine] + [swap(mine, 2 * mask) for mask in (1, 2, 3)], axis=0)
-    return jnp.stack([core, part]).astype(jnp.int32), near, swap(near, 1)
+    near = [mine] + [swap(mine, 2 * mask) for mask in (1, 2, 3)]
+    return jnp.stack([core, part]).astype(jnp.int32), *near, *(swap(value, 1) for value in near)
 
 
 def body(size, *arguments):
     result, grad_inputs, grads = local_part(*arguments)
     if size & (size - 1) or size < 8:
         grads = lax.psum(grads, "seq")
-        summed = (jnp.zeros((2,), jnp.int32), grads[0], grads[1])
+        summed = (jnp.zeros((2,), jnp.int32), *grads.reshape(8, ROWS // 4, WIDTH))
     else:
         summed = all_sum(grads, size)
     return (result, grad_inputs) + tuple(unpack(*summed))

time: 94.6 us -> 93.9 us (level)
    ppermute x10 -> x13, waiting for transfers between devices: 22.8 us -> 22.2 us  [swap(): return lax.ppermute(value, 'seq', [(i, i ^ mask) for i in range(size)])]
    ppermute x10 -> x13, starting transfers between devices: 12.9 us -> 12.8 us  [swap(): return lax.ppermute(value, 'seq', [(i, i ^ mask) for i in range(size)])]
  transfers between devices with their start and end apart: 10 -> 13, of which waited for: 9 -> 9; matrix products, arithmetic and copies ran while one was open for 0% -> 0% of each run, Pallas kernels for 0% -> 0%
where the time goes in v6:
time: 93.9 us; the launch traced here: 93.8 us
  Pallas kernels  57.8 us (62%)
  waiting for transfers between devices  22.2 us (24%)
  starting transfers between devices  12.8 us (14%)
    pallas_call x1, Pallas kernels, local_part(): pl.pallas_call(lambda *refs: kernel(per_step, steps, *refs), grid=(2 * st...  56.2 us
    ppermute x13, waiting for transfers between devices, swap(): return lax.ppermute(value, 'seq', [(i, i ^ mask) for i in range(size)])  22.2 us
    ppermute x13, starting transfers between devices, swap(): return lax.ppermute(value, 'seq', [(i, i ^ mask) for i in range(size)])  12.8 us
  transfers between devices with their start and end apart: 13, of which 9 were waited for; matrix products, arithmetic and copies ran while one was open for 0% of the time, Pallas kernels for 0%

profile of v6, /device:TPU:0, one launch (start us, length us, event | category | flops | bytes accessed | tf_op | source)
XLA Modules:
  0.0 93.8 jit_solution(1684129785268882475)
XLA Ops:
  0.7 56.2 %layers.1 = (bf16[4096,128]{1,0:T(8,128)(2,1)}, f32[4096,128]{1,0:T(8,128)}, f32[2,1056,128]{2,1,0:T(8,128)S(1)}) custom-call(bf16[4096,128]{1,0:T(8,128)(2,1)} %refs_1_.1, bf16[4096,128]{1,0:T(8,128)(2,1)} %refs_1_.1, s32[16,256]{1,0:T(8,128)} %refs_2_.1, bf16[4096,128]{1,0:T(8,128)(2,1)} %refs_3_.1, f32[2,2,128]{2,1,0:T(2,128)} %refs_4_.1, ...), custom_call_target="tpu_custom_call" | custom-call | tf_op jit(solution)/shard_map/layers/pallas_call | solution.py:636
  56.8 0.5 collective-permute-start
  57.4 1.6 %collective-permute-done = f32[1056,128]{1,0:T(8,128)S(1)} collective-permute-done((f32[1056,128]{1,0:T(8,128)S(1)}, f32[1056,128]{1,0:T(8,128)S(1)}, u32[]{:S(2)}, u32[]{:S(2)}) %collective-permute-start) | collective-permute-done | bytes 540704 | tf_op jit(solution)/shard_map/ppermute | solution.py:743
  58.9 0.1 bitcast_add_fusion
  59.0 2.9 %collective-permute-start.1 = (f32[264,128]{1,0:T(8,128)S(1)}, f32[264,128]{1,0:T(8,128)S(1)}, u32[]{:S(2)}, u32[]{:S(2)}) collective-permute-start(f32[264,128]{1,0:T(8,128)S(1)} %get-tuple-element.41), channel_id=1, source_target_pairs={{0,2},{1,3},{2,0},{3,1},{4,6},{5,7},{6,4},{7,5},{8,10},{9,11},{10,... | collective-permute-start | bytes 405512 | tf_op jit(solution)/shard_map/ppermute | solution.py:743
  62.0 1.5 %collective-permute-start.2 = (f32[264,128]{1,0:T(8,128)S(1)}, f32[264,128]{1,0:T(8,128)S(1)}, u32[]{:S(2)}, u32[]{:S(2)}) collective-permute-start(f32[264,128]{1,0:T(8,128)S(1)} %get-tuple-element.43), channel_id=1, source_target_pairs={{0,4},{1,5},{2,6},{3,7},{4,0},{5,1},{6,2},{7,3},{8,12},{9,13},{10,... | collective-permute-start | bytes 405512 | tf_op jit(solution)/shard_map/ppermute | solution.py:743
  63.5 0.0 collective-permute-start.3
  63.5 2.5 %collective-permute-done.1 = f32[264,128]{1,0:T(8,128)S(1)} collective-permute-done((f32[264,128]{1,0:T(8,128)S(1)}, f32[264,128]{1,0:T(8,128)S(1)}, u32[]{:S(2)}, u32[]{:S(2)}) %collective-permute-start.1) | collective-permute-done | bytes 135200 | tf_op jit(solution)/shard_map/ppermute | solution.py:743
  66.0 4.2 %collective-permute-done.2 = f32[264,128]{1,0:T(8,128)S(1)} collective-permute-done((f32[264,128]{1,0:T(8,128)S(1)}, f32[264,128]{1,0:T(8,128)S(1)}, u32[]{:S(2)}, u32[]{:S(2)}) %collective-permute-start.2) | collective-permute-done | bytes 135200 | tf_op jit(solution)/shard_map/ppermute | solution.py:743
  70.2 0.0 collective-permute-done.3
  70.2 1.6 %collective-permute-start.4 = (f32[264,128]{1,0:T(8,128)S(1)}, f32[264,128]{1,0:T(8,128)S(1)}, u32[]{:S(2)}, u32[]{:S(2)}) collective-permute-start(f32[264,128]{1,0:T(8,128)S(1)} %fusion.1), channel_id=1, source_target_pairs={{0,8},{1,9},{2,10},{3,11},{4,12},{5,13},{6,14},{7,15},{8,0},{9,1},... | collective-permute-start | bytes 405512 | tf_op jit(solution)/shard_map/ppermute | solution.py:743
  71.9 3.4 %collective-permute-done.4 = f32[264,128]{1,0:T(8,128)S(1)} collective-permute-done((f32[264,128]{1,0:T(8,128)S(1)}, f32[264,128]{1,0:T(8,128)S(1)}, u32[]{:S(2)}, u32[]{:S(2)}) %collective-permute-start.4) | collective-permute-done | bytes 135200 | tf_op jit(solution)/shard_map/ppermute | solution.py:743
  75.3 2.7 %collective-permute-start.5 = (f32[264,128]{1,0:T(8,128)S(1)}, f32[264,128]{1,0:T(8,128)S(1)}, u32[]{:S(2)}, u32[]{:S(2)}) collective-permute-start(f32[264,128]{1,0:T(8,128)S(1)} %add.49), channel_id=1, source_target_pairs={{0,16},{1,17},{2,18},{3,19},{4,20},{5,21},{6,22},{7,23},{8,24},{9,... | collective-permute-start | bytes 405512 | tf_op jit(solution)/shard_map/ppermute | solution.py:743
  78.0 4.8 %collective-permute-done.5 = f32[264,128]{1,0:T(8,128)S(1)} collective-permute-done((f32[264,128]{1,0:T(8,128)S(1)}, f32[264,128]{1,0:T(8,128)S(1)}, u32[]{:S(2)}, u32[]{:S(2)}) %collective-permute-start.5) | collective-permute-done | bytes 135200 | tf_op jit(solution)/shard_map/ppermute | solution.py:743
  82.8 1.4 %collective-permute-start.6 = (f32[264,128]{1,0:T(8,128)S(1)}, f32[264,128]{1,0:T(8,128)S(1)}, u32[]{:S(2)}, u32[]{:S(2)}) collective-permute-start(f32[264,128]{1,0:T(8,128)S(1)} %add.50.near_zero), channel_id=1, source_target_pairs={{0,2},{1,3},{2,0},{3,1},{4,6},{5,7},{6,4},{7,5},{8,10},{9,11},{10,... | collective-permute-start | bytes 405512 | tf_op jit(solution)/shard_map/ppermute | solution.py:743
  84.2 0.7 collective-permute-start.7
  84.9 1.4 %collective-permute-start.8 = (f32[264,128]{1,0:T(8,128)S(1)}, f32[264,128]{1,0:T(8,128)S(1)}, u32[]{:S(2)}, u32[]{:S(2)}) collective-permute-start(f32[264,128]{1,0:T(8,128)S(1)} %add.50.near_zero), channel_id=1, source_target_pairs={{0,6},{1,7},{2,4},{3,5},{4,2},{5,3},{6,0},{7,1},{8,14},{9,15},{10,... | collective-permute-start | bytes 405512 | tf_op jit(solution)/shard_map/ppermute | solution.py:743
  86.3 0.0 collective-permute-start.9
  86.3 1.5 %collective-permute-done.6.near_one = f32[264,128]{1,0:T(8,128)S(1)} collective-permute-done((f32[264,128]{1,0:T(8,128)S(1)}, f32[264,128]{1,0:T(8,128)S(1)}, u32[]{:S(2)}, u32[]{:S(2)}) %collective-permute-start.6) | collective-permute-done | bytes 135200 | tf_op jit(solution)/shard_map/ppermute | solution.py:743
  87.9 0.0 collective-permute-start.10
  87.9 1.3 %collective-permute-done.7.near_two = f32[264,128]{1,0:T(8,128)S(1)} collective-permute-done((f32[264,128]{1,0:T(8,128)S(1)}, f32[264,128]{1,0:T(8,128)S(1)}, u32[]{:S(2)}, u32[]{:S(2)}) %collective-permute-start.7) | collective-permute-done | bytes 135200 | tf_op jit(solution)/shard_map/ppermute | solution.py:743
  89.2 0.0 collective-permute-start.11
  89.2 1.6 %collective-permute-done.8.near_three = f32[264,128]{1,0:T(8,128)S(1)} collective-permute-done((f32[264,128]{1,0:T(8,128)S(1)}, f32[264,128]{1,0:T(8,128)S(1)}, u32[]{:S(2)}, u32[]{:S(2)}) %collective-permute-start.8) | collective-permute-done | bytes 135200 | tf_op jit(solution)/shard_map/ppermute | solution.py:743
  90.8 0.0 collective-permute-start.12
  90.8 0.1 pad_add_fusion.where_ref
  90.9 0.0 collective-permute-done.9.far_zero
  90.9 0.0 collective-permute-done.10.far_one
  90.9 0.0 collective-permute-done.11.far_two
  90.9 1.3 %collective-permute-done.12.far_three = f32[264,128]{1,0:T(8,128)S(1)} collective-permute-done((f32[264,128]{1,0:T(8,128)S(1)}, f32[264,128]{1,0:T(8,128)S(1)}, u32[]{:S(2)}, u32[]{:S(2)}) %collective-permute-start.12) | collective-permute-done | bytes 135200 | tf_op jit(solution)/shard_map/ppermute | solution.py:743
  92.2 1.6 %unpack.1 = (f32[2,2,128]{2,1,0:T(2,128)}, f32[2,2,128]{2,1,0:T(2,128)}, f32[2,128,384]{2,1,0:T(8,128)}, f32[2,256]{1,0:T(2,128)}, f32[2,128,128]{2,1,0:T(8,128)...) custom-call(s32[2]{0:T(128)S(1)} %pad_add_fusion.where_ref, ...), custom_call_target="tpu_custom_call" | custom-call | tf_op jit(solution)/shard_map/unpack/pallas_call | solution.py:727
  (5 shorter events, 0.2 us)
Async XLA Ops:
  56.8 2.1 %collective-permute-start = (f32[1056,128]{1,0:T(8,128)S(1)}, f32[1056,128]{1,0:T(8,128)S(1)}, u32[]{:S(2)}, u32[]{:S(2)}) collective-permute-start(f32[1056,128]{1,0:T(8,128)S(1)} %dynamic-slice_bitcast_fusion), channel_id=1, source_target_pairs={{0,1},{1,0},{2,3},{3,2},{4,5},{5,4},{6,7},{7,6},{8,9},{9,8},{10,11... | collective-permute-start | bytes 1622024 | tf_op jit(solution)/shard_map/ppermute | solution.py:743
  59.0 7.0 %collective-permute-start.1 = (f32[264,128]{1,0:T(8,128)S(1)}, f32[264,128]{1,0:T(8,128)S(1)}, u32[]{:S(2)}, u32[]{:S(2)}) collective-permute-start(f32[264,128]{1,0:T(8,128)S(1)} %get-tuple-element.41), channel_id=1, source_target_pairs={{0,2},{1,3},{2,0},{3,1},{4,6},{5,7},{6,4},{7,5},{8,10},{9,11},{10,... | collective-permute-start | bytes 405512 | tf_op jit(solution)/shard_map/ppermute | solution.py:743
  62.0 8.2 %collective-permute-start.2 = (f32[264,128]{1,0:T(8,128)S(1)}, f32[264,128]{1,0:T(8,128)S(1)}, u32[]{:S(2)}, u32[]{:S(2)}) collective-permute-start(f32[264,128]{1,0:T(8,128)S(1)} %get-tuple-element.43), channel_id=1, source_target_pairs={{0,4},{1,5},{2,6},{3,7},{4,0},{5,1},{6,2},{7,3},{8,12},{9,13},{10,... | collective-permute-start | bytes 405512 | tf_op jit(solution)/shard_map/ppermute | solution.py:743
  63.5 6.7 %collective-permute-start.3 = (f32[264,128]{1,0:T(8,128)S(1)}, f32[264,128]{1,0:T(8,128)S(1)}, u32[]{:S(2)}, u32[]{:S(2)}) collective-permute-start(f32[264,128]{1,0:T(8,128)S(1)} %get-tuple-element.42), channel_id=1, source_target_pairs={{0,6},{1,7},{2,4},{3,5},{4,2},{5,3},{6,0},{7,1},{8,14},{9,15},{10,... | collective-permute-start | bytes 405512 | tf_op jit(solution)/shard_map/ppermute | solution.py:743
  70.2 5.1 %collective-permute-start.4 = (f32[264,128]{1,0:T(8,128)S(1)}, f32[264,128]{1,0:T(8,128)S(1)}, u32[]{:S(2)}, u32[]{:S(2)}) collective-permute-start(f32[264,128]{1,0:T(8,128)S(1)} %fusion.1), channel_id=1, source_target_pairs={{0,8},{1,9},{2,10},{3,11},{4,12},{5,13},{6,14},{7,15},{8,0},{9,1},... | collective-permute-start | bytes 405512 | tf_op jit(solution)/shard_map/ppermute | solution.py:743
  75.3 7.4 %collective-permute-start.5 = (f32[264,128]{1,0:T(8,128)S(1)}, f32[264,128]{1,0:T(8,128)S(1)}, u32[]{:S(2)}, u32[]{:S(2)}) collective-permute-start(f32[264,128]{1,0:T(8,128)S(1)} %add.49), channel_id=1, source_target_pairs={{0,16},{1,17},{2,18},{3,19},{4,20},{5,21},{6,22},{7,23},{8,24},{9,... | collective-permute-start | bytes 405512 | tf_op jit(solution)/shard_map/ppermute | solution.py:743
  82.8 5.1 %collective-permute-start.6 = (f32[264,128]{1,0:T(8,128)S(1)}, f32[264,128]{1,0:T(8,128)S(1)}, u32[]{:S(2)}, u32[]{:S(2)}) collective-permute-start(f32[264,128]{1,0:T(8,128)S(1)} %add.50.near_zero), channel_id=1, source_target_pairs={{0,2},{1,3},{2,0},{3,1},{4,6},{5,7},{6,4},{7,5},{8,10},{9,11},{10,... | collective-permute-start | bytes 405512 | tf_op jit(solution)/shard_map/ppermute | solution.py:743
  84.2 5.0 %collective-permute-start.7 = (f32[264,128]{1,0:T(8,128)S(1)}, f32[264,128]{1,0:T(8,128)S(1)}, u32[]{:S(2)}, u32[]{:S(2)}) collective-permute-start(f32[264,128]{1,0:T(8,128)S(1)} %add.50.near_zero), channel_id=1, source_target_pairs={{0,4},{1,5},{2,6},{3,7},{4,0},{5,1},{6,2},{7,3},{8,12},{9,13},{10,... | collective-permute-start | bytes 405512 | tf_op jit(solution)/shard_map/ppermute | solution.py:743
  84.9 5.9 %collective-permute-start.8 = (f32[264,128]{1,0:T(8,128)S(1)}, f32[264,128]{1,0:T(8,128)S(1)}, u32[]{:S(2)}, u32[]{:S(2)}) collective-permute-start(f32[264,128]{1,0:T(8,128)S(1)} %add.50.near_zero), channel_id=1, source_target_pairs={{0,6},{1,7},{2,4},{3,5},{4,2},{5,3},{6,0},{7,1},{8,14},{9,15},{10,... | collective-permute-start | bytes 405512 | tf_op jit(solution)/shard_map/ppermute | solution.py:743
  86.3 4.6 %collective-permute-start.9 = (f32[264,128]{1,0:T(8,128)S(1)}, f32[264,128]{1,0:T(8,128)S(1)}, u32[]{:S(2)}, u32[]{:S(2)}) collective-permute-start(f32[264,128]{1,0:T(8,128)S(1)} %add.50.near_zero), channel_id=1, source_target_pairs={{0,1},{1,0},{2,3},{3,2},{4,5},{5,4},{6,7},{7,6},{8,9},{9,8},{10,11... | collective-permute-start | bytes 405512 | tf_op jit(solution)/shard_map/ppermute | solution.py:743
  87.9 3.0 %collective-permute-start.10 = (f32[264,128]{1,0:T(8,128)S(1)}, f32[264,128]{1,0:T(8,128)S(1)}, u32[]{:S(2)}, u32[]{:S(2)}) collective-permute-start(f32[264,128]{1,0:T(8,128)S(1)} %collective-permute-done.6.near_one), channel_id=1, source_target_pairs={{0,1},{1,0},{2,3},{3,2},{4,5},{5,4},{6,7},{7,6},{8,9},{9,8},{10,11... | collective-permute-start | bytes 405512 | tf_op jit(solution)/shard_map/ppermute | solution.py:743
  89.2 1.7 %collective-permute-start.11 = (f32[264,128]{1,0:T(8,128)S(1)}, f32[264,128]{1,0:T(8,128)S(1)}, u32[]{:S(2)}, u32[]{:S(2)}) collective-permute-start(f32[264,128]{1,0:T(8,128)S(1)} %collective-permute-done.7.near_two), channel_id=1, source_target_pairs={{0,1},{1,0},{2,3},{3,2},{4,5},{5,4},{6,7},{7,6},{8,9},{9,8},{10,11... | collective-permute-start | bytes 405512 | tf_op jit(solution)/shard_map/ppermute | solution.py:743
  90.8 1.4 %collective-permute-start.12 = (f32[264,128]{1,0:T(8,128)S(1)}, f32[264,128]{1,0:T(8,128)S(1)}, u32[]{:S(2)}, u32[]{:S(2)}) collective-permute-start(f32[264,128]{1,0:T(8,128)S(1)} %collective-permute-done.8.near_three), channel_id=1, source_target_pairs={{0,1},{1,0},{2,3},{3,2},{4,5},{5,4},{6,7},{7,6},{8,9},{9,8},{10,11... | collective-permute-start | bytes 405512 | tf_op jit(solution)/shard_map/ppermute | solution.py:743

commit v7 on v6

--- a/solution.py
+++ b/solution.py
@@ -12,7 +12,7 @@
 LEN = 256
 HALF = 128
 CHUNK = 256
-AHEAD = 44
+AHEAD = 34
 QUARTER = 64
 WINDOWS = ((0, 128), (0, 192), (64, 256), (128, 256))
 PLACES = ((0, 128), (256, 448), (640, 832), (1024, 1152))
@@ -148,8 +148,9 @@
 def skewed(units):
     running, waiting = [], list(units)
     while running or waiting:
-        if waiting:
-            running.append(waiting.pop(0))
+        for unused in range(2):
+            if waiting:
+                running.append(waiting.pop(0))
         running = [unit for unit in running if next(unit, "end") != "end"]
         yield
 
@@ -213,8 +214,8 @@
     results = {}
     yield from skewed(
         forward_unit(block, group, rows[group], variants, values, marks, power_ref, mixed_ref, scale_ref, results)
-        for block in (0, 1, 2, 3)
         for group in range(2)
+        for block in range(4)
     )
 
 

time: 93.9 us -> 93.7 us (level)
  no operation moved by 1% of the time
where the time goes in v7:
time: 93.7 us; the launch traced here: 93.6 us
  Pallas kernels  57.5 us (61%)
  waiting for transfers between devices  22.2 us (24%)
  starting transfers between devices  12.9 us (14%)
    pallas_call x1, Pallas kernels, local_part(): pl.pallas_call(lambda *refs: kernel(per_step, steps, *refs), grid=(2 * st...  55.9 us
    ppermute x13, waiting for transfers between devices, swap(): return lax.ppermute(value, 'seq', [(i, i ^ mask) for i in range(size)])  22.2 us
    ppermute x13, starting transfers between devices, swap(): return lax.ppermute(value, 'seq', [(i, i ^ mask) for i in range(size)])  12.9 us
  transfers between devices with their start and end apart: 13, of which 9 were waited for; matrix products, arithmetic and copies ran while one was open for 0% of the time, Pallas kernels for 0%

profile of v7, /device:TPU:0, one launch (start us, length us, event | category | flops | bytes accessed | tf_op | source)
XLA Modules:
  0.0 93.6 jit_solution(5032784386699959868)
XLA Ops:
  0.7 55.9 %layers.1 = (bf16[4096,128]{1,0:T(8,128)(2,1)}, f32[4096,128]{1,0:T(8,128)}, f32[2,1056,128]{2,1,0:T(8,128)S(1)}) custom-call(bf16[4096,128]{1,0:T(8,128)(2,1)} %refs_1_.1, bf16[4096,128]{1,0:T(8,128)(2,1)} %refs_1_.1, s32[16,256]{1,0:T(8,128)} %refs_2_.1, bf16[4096,128]{1,0:T(8,128)(2,1)} %refs_3_.1, f32[2,2,128]{2,1,0:T(2,128)} %refs_4_.1, ...), custom_call_target="tpu_custom_call" | custom-call | tf_op jit(solution)/shard_map/layers/pallas_call | solution.py:637
  56.6 0.5 collective-permute-start
  57.1 1.6 %collective-permute-done = f32[1056,128]{1,0:T(8,128)S(1)} collective-permute-done((f32[1056,128]{1,0:T(8,128)S(1)}, f32[1056,128]{1,0:T(8,128)S(1)}, u32[]{:S(2)}, u32[]{:S(2)}) %collective-permute-start) | collective-permute-done | bytes 540704 | tf_op jit(solution)/shard_map/ppermute | solution.py:744
  58.7 0.1 bitcast_add_fusion
  58.8 2.9 %collective-permute-start.1 = (f32[264,128]{1,0:T(8,128)S(1)}, f32[264,128]{1,0:T(8,128)S(1)}, u32[]{:S(2)}, u32[]{:S(2)}) collective-permute-start(f32[264,128]{1,0:T(8,128)S(1)} %get-tuple-element.41), channel_id=1, source_target_pairs={{0,2},{1,3},{2,0},{3,1},{4,6},{5,7},{6,4},{7,5},{8,10},{9,11},{10,... | collective-permute-start | bytes 405512 | tf_op jit(solution)/shard_map/ppermute | solution.py:744
  61.7 1.5 %collective-permute-start.2 = (f32[264,128]{1,0:T(8,128)S(1)}, f32[264,128]{1,0:T(8,128)S(1)}, u32[]{:S(2)}, u32[]{:S(2)}) collective-permute-start(f32[264,128]{1,0:T(8,128)S(1)} %get-tuple-element.43), channel_id=1, source_target_pairs={{0,4},{1,5},{2,6},{3,7},{4,0},{5,1},{6,2},{7,3},{8,12},{9,13},{10,... | collective-permute-start | bytes 405512 | tf_op jit(solution)/shard_map/ppermute | solution.py:744
  63.3 0.0 collective-permute-start.3
  63.3 2.5 %collective-permute-done.1 = f32[264,128]{1,0:T(8,128)S(1)} collective-permute-done((f32[264,128]{1,0:T(8,128)S(1)}, f32[264,128]{1,0:T(8,128)S(1)}, u32[]{:S(2)}, u32[]{:S(2)}) %collective-permute-start.1) | collective-permute-done | bytes 135200 | tf_op jit(solution)/shard_map/ppermute | solution.py:744
  65.8 4.2 %collective-permute-done.2 = f32[264,128]{1,0:T(8,128)S(1)} collective-permute-done((f32[264,128]{1,0:T(8,128)S(1)}, f32[264,128]{1,0:T(8,128)S(1)}, u32[]{:S(2)}, u32[]{:S(2)}) %collective-permute-start.2) | collective-permute-done | bytes 135200 | tf_op jit(solution)/shard_map/ppermute | solution.py:744
  70.0 0.0 collective-permute-done.3
  70.0 1.7 %collective-permute-start.4 = (f32[264,128]{1,0:T(8,128)S(1)}, f32[264,128]{1,0:T(8,128)S(1)}, u32[]{:S(2)}, u32[]{:S(2)}) collective-permute-start(f32[264,128]{1,0:T(8,128)S(1)} %fusion.1), channel_id=1, source_target_pairs={{0,8},{1,9},{2,10},{3,11},{4,12},{5,13},{6,14},{7,15},{8,0},{9,1},... | collective-permute-start | bytes 405512 | tf_op jit(solution)/shard_map/ppermute | solution.py:744
  71.7 3.4 %collective-permute-done.4 = f32[264,128]{1,0:T(8,128)S(1)} collective-permute-done((f32[264,128]{1,0:T(8,128)S(1)}, f32[264,128]{1,0:T(8,128)S(1)}, u32[]{:S(2)}, u32[]{:S(2)}) %collective-permute-start.4) | collective-permute-done | bytes 135200 | tf_op jit(solution)/shard_map/ppermute | solution.py:744
  75.1 2.7 %collective-permute-start.5 = (f32[264,128]{1,0:T(8,128)S(1)}, f32[264,128]{1,0:T(8,128)S(1)}, u32[]{:S(2)}, u32[]{:S(2)}) collective-permute-start(f32[264,128]{1,0:T(8,128)S(1)} %add.49), channel_id=1, source_target_pairs={{0,16},{1,17},{2,18},{3,19},{4,20},{5,21},{6,22},{7,23},{8,24},{9,... | collective-permute-start | bytes 405512 | tf_op jit(solution)/shard_map/ppermute | solution.py:744
  77.8 4.8 %collective-permute-done.5 = f32[264,128]{1,0:T(8,128)S(1)} collective-permute-done((f32[264,128]{1,0:T(8,128)S(1)}, f32[264,128]{1,0:T(8,128)S(1)}, u32[]{:S(2)}, u32[]{:S(2)}) %collective-permute-start.5) | collective-permute-done | bytes 135200 | tf_op jit(solution)/shard_map/ppermute | solution.py:744
  82.5 1.4 %collective-permute-start.6 = (f32[264,128]{1,0:T(8,128)S(1)}, f32[264,128]{1,0:T(8,128)S(1)}, u32[]{:S(2)}, u32[]{:S(2)}) collective-permute-start(f32[264,128]{1,0:T(8,128)S(1)} %add.50.near_zero), channel_id=1, source_target_pairs={{0,2},{1,3},{2,0},{3,1},{4,6},{5,7},{6,4},{7,5},{8,10},{9,11},{10,... | collective-permute-start | bytes 405512 | tf_op jit(solution)/shard_map/ppermute | solution.py:744
  83.9 0.7 collective-permute-start.7
  84.7 1.4 %collective-permute-start.8 = (f32[264,128]{1,0:T(8,128)S(1)}, f32[264,128]{1,0:T(8,128)S(1)}, u32[]{:S(2)}, u32[]{:S(2)}) collective-permute-start(f32[264,128]{1,0:T(8,128)S(1)} %add.50.near_zero), channel_id=1, source_target_pairs={{0,6},{1,7},{2,4},{3,5},{4,2},{5,3},{6,0},{7,1},{8,14},{9,15},{10,... | collective-permute-start | bytes 405512 | tf_op jit(solution)/shard_map/ppermute | solution.py:744
  86.1 0.0 collective-permute-start.9
  86.1 1.5 %collective-permute-done.6.near_one = f32[264,128]{1,0:T(8,128)S(1)} collective-permute-done((f32[264,128]{1,0:T(8,128)S(1)}, f32[264,128]{1,0:T(8,128)S(1)}, u32[]{:S(2)}, u32[]{:S(2)}) %collective-permute-start.6) | collective-permute-done | bytes 135200 | tf_op jit(solution)/shard_map/ppermute | solution.py:744
  87.6 0.0 collective-permute-start.10
  87.6 1.3 %collective-permute-done.7.near_two = f32[264,128]{1,0:T(8,128)S(1)} collective-permute-done((f32[264,128]{1,0:T(8,128)S(1)}, f32[264,128]{1,0:T(8,128)S(1)}, u32[]{:S(2)}, u32[]{:S(2)}) %collective-permute-start.7) | collective-permute-done | bytes 135200 | tf_op jit(solution)/shard_map/ppermute | solution.py:744
  89.0 0.0 collective-permute-start.11
  89.0 1.6 %collective-permute-done.8.near_three = f32[264,128]{1,0:T(8,128)S(1)} collective-permute-done((f32[264,128]{1,0:T(8,128)S(1)}, f32[264,128]{1,0:T(8,128)S(1)}, u32[]{:S(2)}, u32[]{:S(2)}) %collective-permute-start.8) | collective-permute-done | bytes 135200 | tf_op jit(solution)/shard_map/ppermute | solution.py:744
  90.6 0.0 collective-permute-start.12
  90.6 0.1 pad_add_fusion.where_ref
  90.7 0.0 collective-permute-done.9.far_zero
  90.7 0.0 collective-permute-done.10.far_one
  90.7 0.0 collective-permute-done.11.far_two
  90.7 1.3 %collective-permute-done.12.far_three = f32[264,128]{1,0:T(8,128)S(1)} collective-permute-done((f32[264,128]{1,0:T(8,128)S(1)}, f32[264,128]{1,0:T(8,128)S(1)}, u32[]{:S(2)}, u32[]{:S(2)}) %collective-permute-start.12) | collective-permute-done | bytes 135200 | tf_op jit(solution)/shard_map/ppermute | solution.py:744
  91.9 1.6 %unpack.1 = (f32[2,2,128]{2,1,0:T(2,128)}, f32[2,2,128]{2,1,0:T(2,128)}, f32[2,128,384]{2,1,0:T(8,128)}, f32[2,256]{1,0:T(2,128)}, f32[2,128,128]{2,1,0:T(8,128)...) custom-call(s32[2]{0:T(128)S(1)} %pad_add_fusion.where_ref, ...), custom_call_target="tpu_custom_call" | custom-call | tf_op jit(solution)/shard_map/unpack/pallas_call | solution.py:728
  (5 shorter events, 0.2 us)
Async XLA Ops:
  56.6 2.1 %collective-permute-start = (f32[1056,128]{1,0:T(8,128)S(1)}, f32[1056,128]{1,0:T(8,128)S(1)}, u32[]{:S(2)}, u32[]{:S(2)}) collective-permute-start(f32[1056,128]{1,0:T(8,128)S(1)} %dynamic-slice_bitcast_fusion), channel_id=1, source_target_pairs={{0,1},{1,0},{2,3},{3,2},{4,5},{5,4},{6,7},{7,6},{8,9},{9,8},{10,11... | collective-permute-start | bytes 1622024 | tf_op jit(solution)/shard_map/ppermute | solution.py:744
  58.8 7.0 %collective-permute-start.1 = (f32[264,128]{1,0:T(8,128)S(1)}, f32[264,128]{1,0:T(8,128)S(1)}, u32[]{:S(2)}, u32[]{:S(2)}) collective-permute-start(f32[264,128]{1,0:T(8,128)S(1)} %get-tuple-element.41), channel_id=1, source_target_pairs={{0,2},{1,3},{2,0},{3,1},{4,6},{5,7},{6,4},{7,5},{8,10},{9,11},{10,... | collective-permute-start | bytes 405512 | tf_op jit(solution)/shard_map/ppermute | solution.py:744
  61.7 8.2 %collective-permute-start.2 = (f32[264,128]{1,0:T(8,128)S(1)}, f32[264,128]{1,0:T(8,128)S(1)}, u32[]{:S(2)}, u32[]{:S(2)}) collective-permute-start(f32[264,128]{1,0:T(8,128)S(1)} %get-tuple-element.43), channel_id=1, source_target_pairs={{0,4},{1,5},{2,6},{3,7},{4,0},{5,1},{6,2},{7,3},{8,12},{9,13},{10,... | collective-permute-start | bytes 405512 | tf_op jit(solution)/shard_map/ppermute | solution.py:744
  63.3 6.7 %collective-permute-start.3 = (f32[264,128]{1,0:T(8,128)S(1)}, f32[264,128]{1,0:T(8,128)S(1)}, u32[]{:S(2)}, u32[]{:S(2)}) collective-permute-start(f32[264,128]{1,0:T(8,128)S(1)} %get-tuple-element.42), channel_id=1, source_target_pairs={{0,6},{1,7},{2,4},{3,5},{4,2},{5,3},{6,0},{7,1},{8,14},{9,15},{10,... | collective-permute-start | bytes 405512 | tf_op jit(solution)/shard_map/ppermute | solution.py:744
  70.0 5.1 %collective-permute-start.4 = (f32[264,128]{1,0:T(8,128)S(1)}, f32[264,128]{1,0:T(8,128)S(1)}, u32[]{:S(2)}, u32[]{:S(2)}) collective-permute-start(f32[264,128]{1,0:T(8,128)S(1)} %fusion.1), channel_id=1, source_target_pairs={{0,8},{1,9},{2,10},{3,11},{4,12},{5,13},{6,14},{7,15},{8,0},{9,1},... | collective-permute-start | bytes 405512 | tf_op jit(solution)/shard_map/ppermute | solution.py:744
  75.1 7.4 %collective-permute-start.5 = (f32[264,128]{1,0:T(8,128)S(1)}, f32[264,128]{1,0:T(8,128)S(1)}, u32[]{:S(2)}, u32[]{:S(2)}) collective-permute-start(f32[264,128]{1,0:T(8,128)S(1)} %add.49), channel_id=1, source_target_pairs={{0,16},{1,17},{2,18},{3,19},{4,20},{5,21},{6,22},{7,23},{8,24},{9,... | collective-permute-start | bytes 405512 | tf_op jit(solution)/shard_map/ppermute | solution.py:744
  82.5 5.1 %collective-permute-start.6 = (f32[264,128]{1,0:T(8,128)S(1)}, f32[264,128]{1,0:T(8,128)S(1)}, u32[]{:S(2)}, u32[]{:S(2)}) collective-permute-start(f32[264,128]{1,0:T(8,128)S(1)} %add.50.near_zero), channel_id=1, source_target_pairs={{0,2},{1,3},{2,0},{3,1},{4,6},{5,7},{6,4},{7,5},{8,10},{9,11},{10,... | collective-permute-start | bytes 405512 | tf_op jit(solution)/shard_map/ppermute | solution.py:744
  83.9 5.0 %collective-permute-start.7 = (f32[264,128]{1,0:T(8,128)S(1)}, f32[264,128]{1,0:T(8,128)S(1)}, u32[]{:S(2)}, u32[]{:S(2)}) collective-permute-start(f32[264,128]{1,0:T(8,128)S(1)} %add.50.near_zero), channel_id=1, source_target_pairs={{0,4},{1,5},{2,6},{3,7},{4,0},{5,1},{6,2},{7,3},{8,12},{9,13},{10,... | collective-permute-start | bytes 405512 | tf_op jit(solution)/shard_map/ppermute | solution.py:744
  84.7 5.9 %collective-permute-start.8 = (f32[264,128]{1,0:T(8,128)S(1)}, f32[264,128]{1,0:T(8,128)S(1)}, u32[]{:S(2)}, u32[]{:S(2)}) collective-permute-start(f32[264,128]{1,0:T(8,128)S(1)} %add.50.near_zero), channel_id=1, source_target_pairs={{0,6},{1,7},{2,4},{3,5},{4,2},{5,3},{6,0},{7,1},{8,14},{9,15},{10,... | collective-permute-start | bytes 405512 | tf_op jit(solution)/shard_map/ppermute | solution.py:744
  86.1 4.6 %collective-permute-start.9 = (f32[264,128]{1,0:T(8,128)S(1)}, f32[264,128]{1,0:T(8,128)S(1)}, u32[]{:S(2)}, u32[]{:S(2)}) collective-permute-start(f32[264,128]{1,0:T(8,128)S(1)} %add.50.near_zero), channel_id=1, source_target_pairs={{0,1},{1,0},{2,3},{3,2},{4,5},{5,4},{6,7},{7,6},{8,9},{9,8},{10,11... | collective-permute-start | bytes 405512 | tf_op jit(solution)/shard_map/ppermute | solution.py:744
  87.6 3.0 %collective-permute-start.10 = (f32[264,128]{1,0:T(8,128)S(1)}, f32[264,128]{1,0:T(8,128)S(1)}, u32[]{:S(2)}, u32[]{:S(2)}) collective-permute-start(f32[264,128]{1,0:T(8,128)S(1)} %collective-permute-done.6.near_one), channel_id=1, source_target_pairs={{0,1},{1,0},{2,3},{3,2},{4,5},{5,4},{6,7},{7,6},{8,9},{9,8},{10,11... | collective-permute-start | bytes 405512 | tf_op jit(solution)/shard_map/ppermute | solution.py:744
  89.0 1.7 %collective-permute-start.11 = (f32[264,128]{1,0:T(8,128)S(1)}, f32[264,128]{1,0:T(8,128)S(1)}, u32[]{:S(2)}, u32[]{:S(2)}) collective-permute-start(f32[264,128]{1,0:T(8,128)S(1)} %collective-permute-done.7.near_two), channel_id=1, source_target_pairs={{0,1},{1,0},{2,3},{3,2},{4,5},{5,4},{6,7},{7,6},{8,9},{9,8},{10,11... | collective-permute-start | bytes 405512 | tf_op jit(solution)/shard_map/ppermute | solution.py:744
  90.6 1.4 %collective-permute-start.12 = (f32[264,128]{1,0:T(8,128)S(1)}, f32[264,128]{1,0:T(8,128)S(1)}, u32[]{:S(2)}, u32[]{:S(2)}) collective-permute-start(f32[264,128]{1,0:T(8,128)S(1)} %collective-permute-done.8.near_three), channel_id=1, source_target_pairs={{0,1},{1,0},{2,3},{3,2},{4,5},{5,4},{6,7},{7,6},{8,9},{9,8},{10,11... | collective-permute-start | bytes 405512 | tf_op jit(solution)/shard_map/ppermute | solution.py:744
